TPU v7x, 32 devices: a whole 2x2x4 slice. The times are simulated.
32 devices in a mesh: row: 8 (over z, x), col: 1, seq: 4 (over y, core).
Axes of the slice: x: 2, y: 2, z: 4, core: 2. Of those that a mesh axis runs over, the one named last changes fastest.
Arguments:
- pair: bfloat16 [256, 256, 128], P(('row', 'seq'), 'col'), may hold values from -6 to 6
- alignment: bfloat16 [128, 256, 256], P(('row', 'seq'), 'col'), may hold values from -6 to 6
- opm_left: bfloat16 [256, 32], replicated, may hold values from -0.375 to 0.375
- opm_right: bfloat16 [256, 32], replicated, may hold values from -0.375 to 0.375
- opm_out: bfloat16 [1024, 128], replicated, may hold values from -2 to 2
- tri_left: bfloat16 [128, 128], replicated, may hold values from -0.5 to 0.5
- tri_left_gate: bfloat16 [128, 128], replicated, may hold values from -0.5 to 0.5
- tri_right: bfloat16 [128, 128], replicated, may hold values from -0.5 to 0.5
- tri_right_gate: bfloat16 [128, 128], replicated, may hold values from -0.5 to 0.5
- tri_gate: bfloat16 [128, 128], replicated, may hold values from -0.5 to 0.5
- tri_out: bfloat16 [128, 128], replicated, may hold values from -0.5 to 0.5
Outputs:
- pair_out: bfloat16 [256, 256, 128], P(('row', 'seq'), 'col')
All inputs are finite; a program needn't handle non-finite values.
Results may differ from a plain program's by a relative error of at most 0.0075.
Values may be sent and summed in bfloat16 or wider, within the bound.
No kernel may reach another device: no remote copies, remote signals or barrier semaphores. Data moves between devices by JAX's collectives and lax.ppermute only.
A program may use at most 64 MiB of HBM per device.

v0:
```python
import jax
import jax.numpy as jnp
from jax import lax
from jax.sharding import PartitionSpec as P

EPS = 1e-05


def spread_2(shard, axis, root):
    mine = lax.axis_index(axis) == root
    return lax.psum(jnp.where(mine, shard, jnp.zeros_like(shard)), axis)


def layer_norm(values, axis):
    values = values.astype(jnp.float32)
    center = values - jnp.mean(values, axis=axis, keepdims=True)
    spread = jnp.mean(center * center, axis=axis, keepdims=True)
    return center * lax.rsqrt(spread + EPS)


def contract(local_rows, piece):
    return jnp.einsum("cik,cjk->cij", local_rows, piece, preferred_element_type=jnp.float32)


def on_device(
    pair,
    alignment,
    opm_left,
    opm_right,
    opm_out,
    tri_left,
    tri_left_gate,
    tri_right,
    tri_right_gate,
    tri_gate,
    tri_out,
):
    rows_here, cols_here, pair_width = pair.shape
    seq_here = alignment.shape[0]
    model_width = alignment.shape[2]
    factor_width = opm_left.shape[1]
    hidden = tri_left.shape[1]
    n_row = lax.axis_size("row")
    n_col = lax.axis_size("col")
    n_seq = lax.axis_size("seq")
    seq_normed = (
        layer_norm(alignment, 2).astype(jnp.bfloat16).reshape(seq_here * cols_here, model_width)
    )
    left_proj = (
        jnp.dot(seq_normed, opm_left, preferred_element_type=jnp.float32)
        .astype(jnp.bfloat16)
        .reshape(seq_here, cols_here * factor_width)
    )
    right_proj = (
        jnp.dot(seq_normed, opm_right, preferred_element_type=jnp.float32)
        .astype(jnp.bfloat16)
        .reshape(seq_here, cols_here * factor_width)
    )
    per_col = n_row // n_col
    index_row = lax.axis_index("row")
    root_col = index_row // per_col
    right_all = lax.all_gather(right_proj, ("row", "seq"), axis=0, tiled=True)
    left_blocks = left_proj.reshape(seq_here, per_col * n_seq, rows_here * factor_width)
    left_send = jnp.tile(left_blocks, (1, n_col, 1))
    left_recv = lax.all_to_all(left_send, ("row", "seq"), split_axis=1, concat_axis=0, tiled=True)
    row_slice = left_recv.reshape(seq_here * n_row * n_seq, rows_here * factor_width)
    seqs_all = right_all.shape[0]
    row_factors = spread_2(row_slice, "col", root_col)
    right_wide = right_all.reshape(seqs_all, cols_here, factor_width)
    row_stack = jnp.swapaxes(row_factors.reshape(seqs_all, rows_here, factor_width), 0, 1)

    def outer_row(packed):
        row_vals, pair_row = packed
        outer_sum = jnp.einsum(
            "np,njq->jpq", row_vals, right_wide, preferred_element_type=jnp.float32
        )
        mean_outer = (
            (outer_sum * (1.0 / seqs_all))
            .astype(jnp.bfloat16)
            .reshape(cols_here, factor_width * factor_width)
        )
        return (
            pair_row.astype(jnp.float32)
            + jnp.dot(mean_outer, opm_out, preferred_element_type=jnp.float32)
        ).astype(jnp.bfloat16)

    pair_mid = lax.map(outer_row, (row_stack, pair))
    normed_pair = layer_norm(pair_mid, 2).astype(jnp.bfloat16)
    flat_pair = normed_pair.reshape(rows_here * cols_here, pair_width)

    def project(weight):
        return lax.dot_general(
            weight, flat_pair, (((0,), (1,)), ((), ())), preferred_element_type=jnp.float32
        )

    def gated(weight_gate, weight_value):
        gate_part = jax.nn.sigmoid(project(weight_gate))
        return (
            (gate_part * project(weight_value))
            .astype(jnp.bfloat16)
            .reshape(hidden, rows_here, cols_here)
        )

    left_first = gated(tri_left_gate, tri_left)
    right_first = gated(tri_right_gate, tri_right)
    left_local, right_local = (
        lax.all_to_all(
            lax.all_to_all(left_first, "col", split_axis=0, concat_axis=2, tiled=True),
            "seq",
            split_axis=0,
            concat_axis=1,
            tiled=True,
        ),
        lax.all_to_all(
            lax.all_to_all(right_first, "col", split_axis=0, concat_axis=2, tiled=True),
            "seq",
            split_axis=0,
            concat_axis=1,
            tiled=True,
        ),
    )
    product = contract(left_local, lax.all_gather(right_local, "row", axis=1, tiled=True))
    product = product.astype(jnp.bfloat16)
    returned = lax.all_to_all(
        lax.all_to_all(product, "col", split_axis=2, concat_axis=0, tiled=True),
        "seq",
        split_axis=1,
        concat_axis=0,
        tiled=True,
    )
    per_group = hidden // (n_col * n_seq)
    weights_order = (
        tri_out.reshape(n_col, n_seq, per_group, pair_width)
        .transpose(1, 0, 2, 3)
        .reshape(hidden, pair_width)
    )
    normed_product = layer_norm(returned, 0).astype(jnp.bfloat16)
    update = jnp.einsum(
        "cij,cd->ijd", normed_product, weights_order, preferred_element_type=jnp.float32
    )
    gate_part = jax.nn.sigmoid(
        jnp.dot(flat_pair, tri_gate, preferred_element_type=jnp.float32)
    ).reshape(rows_here, cols_here, pair_width)
    return (pair_mid.astype(jnp.float32) + gate_part * update).astype(jnp.bfloat16)


def solution(mesh):
    return jax.shard_map(
        on_device,
        mesh=mesh,
        in_specs=(
            P(("row", "seq"), "col", None),
            P(("row", "seq"), "col", None),
            P(),
            P(),
            P(),
            P(),
            P(),
            P(),
            P(),
            P(),
            P(),
        ),
        out_specs=P(("row", "seq"), "col", None),
        check_vma=False,
    )
```

profile of v0, /device:TPU:0, one launch (start us, length us, event | category | flops | bytes accessed | tf_op | source)
XLA Modules:
  0.0 219.2 jit_solution(17473537091291251252)
XLA Ops:
  6.5 1.3 convert_reduce_fusion.1
  7.8 1.4 fusion.26
  9.3 1.4 fusion.27
  10.6 1.0 convolution_convert_fusion.1
  11.8 0.9 reshape.89
  12.7 1.0 convolution_convert_fusion.2
  14.1 0.7 copy.41
  14.8 7.3 %all-to-all-start = ((bf16[4,32,256]{2,0,1:T(4,128)(2,1)}), bf16[4,32,256]{2,0,1:T(4,128)(2,1)S(1)}, u32[]{:S(2)}, u32[]{:S(2)}) async-start(bf16[4,32,256]{2,0,1:T(4,128)(2,1)} %copy.41), calls=%async_computation | async-start | bytes 131072 | tf_op jit(solution)/shard_map/all_to_all | solution.py:65
  22.2 7.3 %all-to-all-done = bf16[4,32,256]{2,0,1:T(4,128)(2,1)S(1)} async-done(((bf16[4,32,256]{2,0,1:T(4,128)(2,1)}), bf16[4,32,256]{2,0,1:T(4,128)(2,1)S(1)}, u32[]{:S(2)}, u32[]{:S(2)}) %all-to-all-start) | async-done | bytes 65568 | tf_op jit(solution)/shard_map/all_to_all | solution.py:65
  29.9 42.1 %all-gather.6.cloned.1.call-done = bf16[32,4,8192]{2,1,0:T(4,128)(2,1)} async-done(((bf16[1,4,8192]{2,1,0:T(4,128)(2,1)}), bf16[32,4,8192]{2,1,0:T(4,128)(2,1)}) %all-gather.6.cloned.1.call-update) | async-done | bytes 2097168 | tf_op jit(solution)/shard_map/all_gather | solution.py:62
  72.0 11.1 %reshape.80 = bf16[128,256,32]{2,1,0:T(8,128)(2,1)} reshape(bf16[32,4,8192]{2,1,0:T(4,128)(2,1)} %all-gather.6.cloned.1.call-done) | data formatting | bytes 4194304 | tf_op jit(solution)/shard_map/reshape | solution.py:69
  83.1 7.5 %copy.44 = bf16[128,256,32]{1,0,2:T(8,128)(2,1)S(1)} copy(bf16[128,256,32]{2,1,0:T(8,128)(2,1)} %reshape.80) | data formatting | bytes 4194304 | tf_op jit(solution)/shard_map/while | solution.py:87
  90.6 15.5 %while.10 = (s32[]{:T(128)}, bf16[8,256,128]{2,1,0:T(8,128)(2,1)S(1)}, bf16[8,256,128]{2,1,0:T(8,128)(2,1)}, bf16[8,128,32]{1,2,0:T(8,128)(2,1)S(1)}, bf16[128,2...) while((s32[]{:T(128)}, bf16[8,256,128]{2,1,0:T(8,128)(2,1)S(1)}, ...), condition=%wide.region_3.4_spmd, body=%wide.region_2.3_spmd.sunk | while | flops 134840320 | bytes 4595797 | solution.py:87
  91.3 1.2 fusion.64
  93.3 1.2 fusion.64
  95.2 1.2 fusion.64
  97.2 1.2 fusion.64
  99.1 1.2 fusion.64
  101.0 1.2 fusion.64
  103.0 1.2 fusion.64
  104.9 1.2 fusion.64
  106.4 0.6 fusion.24
  107.0 0.6 fusion.25
  108.8 11.4 %all_to_all.54 = bf16[128,8,256]{2,1,0:T(8,128)(2,1)S(1)} all-to-all(bf16[128,8,256]{2,1,0:T(8,128)(2,1)S(1)} %copy.47), channel_id=1, replica_groups=mesh['row'=8,'col'=1,'seq'=4] {'seq'}, dimensions={0} | all-to-all | bytes 1048576 | tf_op jit(solution)/shard_map/all_to_all | solution.py:114
  120.2 0.9 copy.63
  122.2 11.2 %all_to_all.55 = bf16[128,8,256]{2,1,0:T(8,128)(2,1)S(1)} all-to-all(bf16[128,8,256]{2,1,0:T(8,128)(2,1)S(1)} %copy.45), channel_id=1, replica_groups=mesh['row'=8,'col'=1,'seq'=4] {'seq'}, dimensions={0} | all-to-all | bytes 1048576 | tf_op jit(solution)/shard_map/all_to_all | solution.py:107
  133.5 59.8 %all-gather.4.cloned.1.call-done = bf16[32,256,256]{2,1,0:T(8,128)(2,1)} async-done(((bf16[32,32,256]{2,1,0:T(8,128)(2,1)}), bf16[32,256,256]{2,1,0:T(8,128)(2,1)}) %all-gather.4.cloned.1.call-update) | async-done | bytes 4194320 | tf_op jit(solution)/shard_map/all_gather | solution.py:122
  193.2 3.5 %convolution_convert_fusion = bf16[32,32,256]{2,1,0:T(8,128)(2,1)S(1)} fusion(bf16[32,256,256]{2,1,0:T(8,128)(2,1)} %all-gather.4.cloned.1.call-done, bf16[32,4,8,256]{3,2,0,1:T(8,128)(2,1)S(1)} %bitcast.104), kind=kOutput, calls=%fused_computation.32 | convolution fusion | flops 134479872 | bytes 5242880 | tf_op jit(solution)/shard_map/cik,cjk->cij/dot_general | solution.py:22
  196.7 1.1 copy.49
  197.9 3.5 %all-to-all-start.3 = ((bf16[32,32,256]{2,0,1:T(8,128)(2,1)}), bf16[32,32,256]{2,0,1:T(8,128)(2,1)S(1)}, u32[]{:S(2)}, u32[]{:S(2)}) async-start(bf16[32,32,256]{2,0,1:T(8,128)(2,1)} %copy.49), calls=%async_computation.3 | async-start | bytes 1048576 | tf_op jit(solution)/shard_map/all_to_all | solution.py:124
  201.8 8.4 %all-to-all-done.3 = bf16[32,32,256]{2,0,1:T(8,128)(2,1)S(1)} async-done(((bf16[32,32,256]{2,0,1:T(8,128)(2,1)}), bf16[32,32,256]{2,0,1:T(8,128)(2,1)S(1)}, u32[]{:S(2)}, u32[]{:S(2)}) %all-to-all-start.3) | async-done | bytes 524320 | tf_op jit(solution)/shard_map/all_to_all | solution.py:124
  211.3 1.1 fusion.19
  (60 shorter events, 10.6 us)
Async XLA Ops:
  6.5 101.1 %copy-start = (bf16[128,128]{1,0:T(8,128)(2,1)S(1)}, bf16[128,128]{1,0:T(8,128)(2,1)}, u32[]{:S(2)}) copy-start(bf16[128,128]{1,0:T(8,128)(2,1)} %param.21) | copy-start | bytes 98308
  6.5 65.5 %all-gather.6.cloned.1.call-start = ((), (), s32[]{:S(2)}) async-start(), calls=%async_computation.5 | async-start | bytes 2162688 | tf_op jit(solution)/shard_map/all_gather | solution.py:62
  14.8 14.7 %all-to-all-start = ((bf16[4,32,256]{2,0,1:T(4,128)(2,1)}), bf16[4,32,256]{2,0,1:T(4,128)(2,1)S(1)}, u32[]{:S(2)}, u32[]{:S(2)}) async-start(bf16[4,32,256]{2,0,1:T(4,128)(2,1)} %copy.41), calls=%async_computation | async-start | bytes 131072 | tf_op jit(solution)/shard_map/all_to_all | solution.py:65
  22.1 171.2 %all-gather.4.cloned.1.call-start = ((), (), s32[]{:S(2)}) async-start(), calls=%async_computation.4 | async-start | bytes 4718592 | tf_op jit(solution)/shard_map/all_gather | solution.py:122
  83.1 7.5 %copy-start.1 = (bf16[1024,128]{1,0:T(8,128)(2,1)S(1)}, bf16[1024,128]{1,0:T(8,128)(2,1)}, u32[]{:S(2)}) copy-start(bf16[1024,128]{1,0:T(8,128)(2,1)} %param.17) | copy-start | bytes 786436
  106.1 2.0 copy-start.2
  107.6 13.4 %copy-start.5 = (bf16[128,128]{1,0:T(8,128)(2,1)S(1)}, bf16[128,128]{1,0:T(8,128)(2,1)}, u32[]{:S(2)}) copy-start(bf16[128,128]{1,0:T(8,128)(2,1)} %param.19) | copy-start | bytes 98308
  108.4 13.1 %copy-start.3 = (bf16[128,128]{1,0:T(8,128)(2,1)S(1)}, bf16[128,128]{1,0:T(8,128)(2,1)}, u32[]{:S(2)}) copy-start(bf16[128,128]{1,0:T(8,128)(2,1)} %param.18) | copy-start | bytes 98308
  122.2 79.1 %copy-start.6 = (bf16[128,128]{1,0:T(8,128)(2,1)S(1)}, bf16[128,128]{1,0:T(8,128)(2,1)}, u32[]{:S(2)}) copy-start(bf16[128,128]{1,0:T(8,128)(2,1)} %param.22) | copy-start | bytes 98308
  197.9 12.3 %all-to-all-start.3 = ((bf16[32,32,256]{2,0,1:T(8,128)(2,1)}), bf16[32,32,256]{2,0,1:T(8,128)(2,1)S(1)}, u32[]{:S(2)}, u32[]{:S(2)}) async-start(bf16[32,32,256]{2,0,1:T(8,128)(2,1)} %copy.49), calls=%async_computation.3 | async-start | bytes 1048576 | tf_op jit(solution)/shard_map/all_to_all | solution.py:124
  201.8 9.5 %copy-start.4 = (bf16[128,128]{1,0:T(8,128)(2,1)S(1)}, bf16[128,128]{1,0:T(8,128)(2,1)}, u32[]{:S(2)}) copy-start(bf16[128,128]{1,0:T(8,128)(2,1)} %param.23) | copy-start | bytes 98308
Sparse Core Ops, SparseCore 0:
  12.9 59.0 all-gather.5
  121.2 72.0 all-gather.3
where the time goes:
time: 221 us; the launch traced here: 219 us
  waiting for transfers between devices  118 us (53%)
  local copies, waits for them, and re-layouts  26.3 us (12%)
  blocking collectives  22.6 us (10%)
  matrix products  21.4 us (10%)
  between operations  13.7 us (6%)
  starting transfers between devices  10.8 us (5%)
  other arithmetic  6.58 us (3%)
    all_gather x1, waiting for transfers between devices, on_device(): lax.all_gather(right_local, 'row', axis=1, tiled=True)  59.8 us
    all_gather x1, waiting for transfers between devices, on_device(): right_all = lax.all_gather(right_proj, ('row', 'seq'), axis=0, tiled=True)  42.1 us
    all_to_all x1, blocking collectives, on_device(): lax.all_to_all(lax.all_to_all(right_first, 'col', split_axis=0, concat_ax...  11.4 us
    all_to_all x1, blocking collectives, on_device(): lax.all_to_all(lax.all_to_all(left_first, 'col', split_axis=0, concat_axi...  11.2 us
    reshape x1, local copies, waits for them, and re-layouts, on_device(): right_wide = right_all.reshape(seqs_all, cols_here, factor_width)  11.1 us
    dot_general x8, matrix products, outer_row(): jnp.dot(mean_outer, opm_out, preferred_element_type=jnp.float32)  9.69 us
    all_to_all x1, waiting for transfers between devices, on_device(): lax.all_to_all(lax.all_to_all(product, 'col', split_axis=2, concat_axis=0...  8.36 us
    while x2, local copies, waits for them, and re-layouts, on_device(): pair_mid = lax.map(outer_row, (row_stack, pair))  7.64 us
  transfers between devices with their start and end apart: 4, of which 4 were waited for; matrix products, arithmetic and copies ran while one was open for 2% of the time, Pallas kernels for 0%

commit v1 on v0

--- a/solution.py
+++ b/solution.py
@@ -1,9 +1,16 @@
+import functools
+
 import jax
 import jax.numpy as jnp
 from jax import lax
+from jax.experimental import pallas as pl
+from jax.experimental.pallas import tpu as pltpu
 from jax.sharding import PartitionSpec as P
 
 EPS = 1e-05
+BOTH = ("row", "seq")
+BF16 = jnp.bfloat16
+F32 = jnp.float32
 
 
 def spread_2(shard, axis, root):
@@ -22,7 +29,7 @@
     return jnp.einsum("cik,cjk->cij", local_rows, piece, preferred_element_type=jnp.float32)
 
 
-def on_device(
+def by_groups(
     pair,
     alignment,
     opm_left,
@@ -144,6 +151,349 @@
     return (pair_mid.astype(jnp.float32) + gate_part * update).astype(jnp.bfloat16)
 
 
+def mul(a, b):
+    return jnp.dot(a, b, preferred_element_type=F32)
+
+
+def mul_t(a, b):
+    return lax.dot_general(a, b, (((1,), (1,)), ((), ())), preferred_element_type=F32)
+
+
+def ones_where(mask):
+    return jnp.where(mask, 1.0, 0.0).astype(BF16)
+
+
+def iotas(rows, cols):
+    shape = (rows, cols)
+    return lax.broadcasted_iota(jnp.int32, shape, 0), lax.broadcasted_iota(jnp.int32, shape, 1)
+
+
+def identity(size):
+    row, col = iotas(size, size)
+    return ones_where(row == col)
+
+
+def swap_rows(outer, inner):
+    row, col = iotas(outer * inner, outer * inner)
+    return ones_where(col == (row % outer) * inner + row // outer)
+
+
+def normalize(values, axis):
+    center = values - jnp.mean(values, axis=axis, keepdims=True)
+    spread = jnp.mean(center * center, axis=axis, keepdims=True)
+    return center * lax.rsqrt(spread + EPS)
+
+
+def factors_kernel(sizes, align_ref, left_ref, right_ref, *refs):
+    n_far, n_near, n_core, rows, _ = sizes
+    out_refs, parts = refs[:n_far], refs[n_far]
+    seqs, cols, width = align_ref.shape
+    factor = left_ref.shape[1]
+    chip_rows = n_core * rows
+    chips = n_far * n_near
+    row, col = iotas(factor, chip_rows * factor)
+    left_wide = mul(left_ref[...], ones_where(row == col % factor)).astype(BF16)
+    right_t = right_ref[...].astype(F32).T.astype(BF16)
+    row, col = iotas(cols, chip_rows * factor)
+    own_lane = (row % chip_rows) == (col // factor)
+    row, col = iotas(n_far * seqs * n_near, cols)
+    chip_of_row = (row // (seqs * n_near)) * n_near + row % n_near
+    seq_of_row = (row // n_near) % seqs
+    chip_match = chip_of_row == col // chip_rows
+    right_rows, left_rows = [], None
+    for n in range(seqs):
+        normed = normalize(align_ref[n].astype(F32), 1).astype(BF16)
+        right_rows.append(mul_t(right_t, normed))
+        spread = jnp.where(own_lane, mul(normed, left_wide), 0.0).astype(BF16)
+        part = mul(ones_where(chip_match & (seq_of_row == n)), spread)
+        left_rows = part if left_rows is None else left_rows + part
+    right_block = jnp.concatenate(right_rows, 0).astype(BF16)
+    part_rows = seqs * n_near
+    pieces = n_core
+    for far in range(n_far):
+        for piece in range(pieces):
+            parts[far, piece * part_rows : (piece + 1) * part_rows, :] = left_rows[
+                far * part_rows : (far + 1) * part_rows, piece * cols : (piece + 1) * cols
+            ].astype(BF16)
+    here = lax.axis_index("row") // 2
+    for k in range(n_far):
+        out_refs[k][: seqs * factor, :] = right_block
+        out_refs[k][seqs * factor :, :] = parts[here ^ k]
+
+
+def regroup_kernel(sizes, factor, seqs, *refs):
+    n_far, n_near, n_core, _, _ = sizes
+    in_refs, out_refs, parts = refs[:n_far], refs[n_far : n_far + n_near], refs[-1]
+    held = n_far * seqs
+    half = 256 // held
+    shuffle = swap_rows(held, half)
+    for h in range(factor // half):
+        block = jnp.concatenate(
+            [
+                ref[n * factor + h * half : n * factor + (h + 1) * half, :]
+                for ref in in_refs
+                for n in range(seqs)
+            ],
+            0,
+        )
+        block = mul(shuffle, block).astype(BF16)
+        for ref in out_refs:
+            ref[h * half * held : (h + 1) * half * held, :] = block
+    part_rows = seqs * n_near
+    base = seqs * factor
+    pick = swap_rows(held, n_near)
+    for piece in range(n_core):
+        block = jnp.concatenate(
+            [ref[base + piece * part_rows : base + (piece + 1) * part_rows, :] for ref in in_refs], 0
+        )
+        block = mul(pick, block).astype(BF16)
+        for near in range(n_near):
+            parts[near, piece * held : (piece + 1) * held, :] = block[
+                near * held : (near + 1) * held
+            ]
+    n_y = n_near // 2
+    here = (lax.axis_index("row") % 2) * n_y + lax.axis_index("seq") // n_core
+    for k in range(n_near):
+        out_refs[k][factor * held :, :] = parts[here ^ k]
+
+
+def pair_kernel(sizes, held, scale, *refs):
+    n_core, rows, n_dev = sizes[2], sizes[3], sizes[4]
+    groups = refs[:-8]
+    pair_ref, out_w, tri_w, send_ref, mid_ref, norm_ref, outer, both = refs[-8:]
+    _, cols, width = pair_ref.shape
+    factor_sq = out_w.shape[1]
+    factor = groups[0].shape[0] // held - n_core
+    hidden = tri_w.shape[0] // 4
+    core = lax.axis_index("seq") % n_core
+    at = pl.multiple_of((factor + core) * held, held)
+    left = jnp.concatenate([ref[pl.ds(at, held), :] for ref in groups], 0)
+    left_t = mul_t(identity(rows * factor), left).astype(BF16)
+    for q in range(factor):
+        right = jnp.concatenate([ref[q * held : (q + 1) * held, :] for ref in groups], 0)
+        block = mul(left_t, right).astype(BF16)
+        for i in range(rows):
+            outer[i, q * factor : (q + 1) * factor, :] = block[i * factor : (i + 1) * factor]
+    eye = identity(width)
+    for i in range(rows):
+        update = mul(out_w[...], outer[i])
+        mid = (mul_t(eye, pair_ref[i]) + update * scale).astype(BF16)
+        mid_ref[i] = mid
+        normed = normalize(mid.astype(F32), 0).astype(BF16)
+        norm_ref[i] = normed
+        for side in range(2):
+            at = 2 * side * hidden
+            gate = jax.nn.sigmoid(mul(tri_w[at : at + hidden, :], normed))
+            value = mul(tri_w[at + hidden : at + 2 * hidden, :], normed)
+            both[side, i] = (gate * value).astype(BF16)
+    per = hidden // n_dev
+    some = 256 // rows
+    shuffle = swap_rows(rows, some)
+    chunk = per * rows
+    for side in range(2):
+        for b in range(hidden // some):
+            block = jnp.concatenate(
+                [both[side, i, b * some : (b + 1) * some, :] for i in range(rows)], 0
+            )
+            block = mul(shuffle, block).astype(BF16)
+            for d in range(some // per):
+                to = ((b * some // per + d) * 2 + side) * chunk
+                send_ref[to : to + chunk, :] = block[d * chunk : (d + 1) * chunk]
+
+
+def product_kernel(sizes, per, recv_ref, send_ref, factors, total):
+    rows, n_dev = sizes[3], sizes[4]
+    chunk = per * rows
+    for src in range(n_dev):
+        for side in range(2):
+            at = (src * 2 + side) * chunk
+            block = recv_ref[at : at + chunk, :].astype(F32)
+            for c in range(per):
+                factors[side, c, src * rows : (src + 1) * rows, :] = block[c * rows : (c + 1) * rows]
+    for c in range(per):
+        prod = mul_t(factors[0, c].astype(BF16), factors[1, c].astype(BF16))
+        for dst in range(n_dev):
+            total[dst, c * rows : (c + 1) * rows, :] = prod[dst * rows : (dst + 1) * rows]
+    for dst in range(n_dev):
+        send_ref[dst * chunk : (dst + 1) * chunk, :] = total[dst].astype(BF16)
+
+
+def finish_kernel(sizes, recv_ref, mid_ref, norm_ref, gate_w, out_w, out_ref, apart):
+    rows = sizes[3]
+    _, width, cols = mid_ref.shape
+    hidden = out_w.shape[1]
+    some = 256 // rows
+    blocks = hidden // some
+    count = some * rows
+
+    def piece(b):
+        return recv_ref[b * count : (b + 1) * count, :].astype(F32).reshape(some, rows, cols)
+
+    mean = sum(jnp.sum(piece(b), 0) for b in range(blocks)) * (1.0 / hidden)
+    spread = sum(jnp.sum((piece(b) - mean) ** 2, 0) for b in range(blocks)) * (1.0 / hidden)
+    factor = lax.rsqrt(spread + EPS)
+    shuffle = swap_rows(some, rows)
+    for b in range(blocks):
+        normed = ((piece(b) - mean) * factor).reshape(count, cols).astype(BF16)
+        normed = mul(shuffle, normed).astype(BF16)
+        for i in range(rows):
+            apart[i, b * some : (b + 1) * some, :] = normed[i * some : (i + 1) * some]
+    eye = identity(cols)
+    for i in range(rows):
+        update = mul(out_w[...], apart[i])
+        gate = jax.nn.sigmoid(mul(gate_w[...], norm_ref[i]))
+        done = (mid_ref[i].astype(F32) + gate * update).astype(BF16)
+        out_ref[i] = mul_t(eye, done).astype(BF16)
+
+
+def call(kernel, out_shape, scratch, flops, *args):
+    out_shape = [jax.ShapeDtypeStruct(s, BF16) for s in out_shape]
+    moved = sum(a.size * 2 for a in (*args, *out_shape))
+    return pl.pallas_call(
+        kernel,
+        out_shape=out_shape,
+        in_specs=[pl.BlockSpec(memory_space=pltpu.VMEM)] * len(args),
+        out_specs=[pl.BlockSpec(memory_space=pltpu.VMEM)] * len(out_shape),
+        scratch_shapes=scratch,
+        compiler_params=pltpu.CompilerParams(vmem_limit_bytes=40 * 2**20),
+        cost_estimate=pl.CostEstimate(flops=flops, bytes_accessed=moved, transcendentals=0),
+    )(*args)
+
+
+def whole_channels(
+    pair,
+    alignment,
+    opm_left,
+    opm_right,
+    opm_out,
+    tri_left,
+    tri_left_gate,
+    tri_right,
+    tri_right_gate,
+    tri_gate,
+    tri_out,
+):
+    rows, cols, width = pair.shape
+    seqs = alignment.shape[0]
+    factor = opm_left.shape[1]
+    hidden = tri_left.shape[1]
+    n_row, n_seq = lax.axis_size("row"), lax.axis_size("seq")
+    n_dev = n_row * n_seq
+    n_core = 2
+    n_far, n_near = n_row // 2, 2 * (n_seq // n_core)
+    n_y = n_near // 2
+    sizes = (n_far, n_near, n_core, rows, n_dev)
+    held = n_far * seqs
+    per = hidden // n_dev
+
+    def exchange(value, row_bits, seq_bits):
+        pairs = [
+            (r * n_seq + s, (r ^ row_bits) * n_seq + (s ^ seq_bits))
+            for r in range(n_row)
+            for s in range(n_seq)
+        ]
+        return lax.ppermute(value, BOTH, pairs)
+
+    out_wt = jnp.transpose(opm_out.reshape(factor, factor, width), (2, 1, 0))
+    out_wt = out_wt.reshape(width, factor * factor)
+    tri_wt = jnp.concatenate([w.T for w in (tri_left_gate, tri_left, tri_right_gate, tri_right)], 0)
+
+    message = (seqs * factor + n_core * seqs * n_near, cols)
+    mine = call(
+        functools.partial(factors_kernel, sizes),
+        [message] * n_far,
+        [pltpu.VMEM((n_far, n_core * seqs * n_near, cols), BF16)],
+        4 * seqs * cols * alignment.shape[2] * factor,
+        alignment,
+        opm_left,
+        opm_right,
+    )
+    far = [mine[0]] + [exchange(mine[k], 2 * k, 0) for k in range(1, n_far)]
+    message = ((factor + n_core) * held, cols)
+    mine = call(
+        functools.partial(regroup_kernel, sizes, factor, seqs),
+        [message] * n_near,
+        [pltpu.VMEM((n_near, n_core * held, cols), BF16)],
+        2 * 256 * factor * held * cols,
+        *far,
+    )
+    near = [mine[0]] + [
+        exchange(mine[k], k // n_y, (k % n_y) * n_core) for k in range(1, n_near)
+    ]
+    groups = near + [exchange(block, 0, 1) for block in near]
+    scale = 1.0 / (held * n_near * n_core)
+    send, mid, normed = call(
+        functools.partial(pair_kernel, sizes, held, scale),
+        [(2 * hidden * rows, cols), (rows, width, cols), (rows, width, cols)],
+        [
+            pltpu.VMEM((rows, factor * factor, cols), BF16),
+            pltpu.VMEM((2, rows, hidden, cols), BF16),
+        ],
+        4 * rows * cols * width * (factor * factor + hidden * 2),
+        *groups,
+        pair,
+        out_wt,
+        tri_wt,
+    )
+    recv = lax.all_to_all(send, BOTH, split_axis=0, concat_axis=0, tiled=True)
+    (send,) = call(
+        functools.partial(product_kernel, sizes, per),
+        [(hidden * rows, cols)],
+        [
+            pltpu.VMEM((2, per, rows * n_dev, cols), F32),
+            pltpu.VMEM((n_dev, per * rows, cols), F32),
+        ],
+        2 * per * cols * cols * cols,
+        recv,
+    )
+    recv = lax.all_to_all(send, BOTH, split_axis=0, concat_axis=0, tiled=True)
+    (out,) = call(
+        functools.partial(finish_kernel, sizes),
+        [(rows, cols, width)],
+        [pltpu.VMEM((rows, hidden, cols), BF16)],
+        4 * rows * cols * width * hidden,
+        recv,
+        mid,
+        normed,
+        tri_gate.T,
+        tri_out.T,
+    )
+    return out
+
+
+def power_of_two(n):
+    return n & (n - 1) == 0
+
+
+def on_device(pair, alignment, opm_left, *rest):
+    rows, cols, _ = pair.shape
+    factor, hidden = opm_left.shape[1], rest[2].shape[1]
+    n_row, n_col, n_seq = (lax.axis_size(a) for a in ("row", "col", "seq"))
+    n_dev = n_row * n_seq
+    held = n_row // 2 * alignment.shape[0]
+    fits = (
+        n_col == 1
+        and power_of_two(n_row)
+        and power_of_two(n_seq)
+        and power_of_two(rows)
+        and n_row >= 4
+        and n_seq >= 4
+        and hidden % n_dev == 0
+        and rows % 8 == 0
+        and (hidden // n_dev * rows) % 16 == 0
+        and cols % 256 == 0
+        and rows * factor == cols
+        and rows * n_dev == cols
+        and held % 16 == 0
+        and 256 % held == 0
+        and factor % (256 // held) == 0
+        and hidden % (256 // rows) == 0
+        and power_of_two(held * n_seq * 2)
+    )
+    plan = whole_channels if fits else by_groups
+    return plan(pair, alignment, opm_left, *rest)
+
+
 def solution(mesh):
     return jax.shard_map(
         on_device,

time: 221 us -> 97.9 us (0.44)
  waiting for transfers between devices: 118 us -> 31.4 us
  matrix products: 21.4 us -> 0 us
  local copies, waits for them, and re-layouts: 26.3 us -> 11 us
  between operations: 13.7 us -> 0.18 us
  Pallas kernels: 0 us -> 10.2 us
  blocking collectives: 22.6 us -> 31.6 us
  other arithmetic: 6.58 us -> 0.02 us
    all_gather x2 -> x0, waiting for transfers between devices: 102 us -> none  [the longest x1 59.8 us: on_device(): lax.all_gather(right_local, 'row', axis=1, tiled=True)]
    dot_general x25 -> x0, matrix products: 21.4 us -> none  [the longest x8 9.69 us: outer_row(): jnp.dot(mean_outer, opm_out, preferred_element_type=jnp.float32)]
    ppermute x0 -> x10, waiting for transfers between devices: none -> 16.7 us  [exchange(): return lax.ppermute(value, BOTH, pairs)]
    reshape x3 -> x1, local copies, waits for them, and re-layouts: 11.9 us -> 0.14 us  [whole_channels(): out_wt = out_wt.reshape(width, factor * factor)]
    pallas_call x0 -> x5, Pallas kernels: none -> 10.2 us  [call(): pl.pallas_call(kernel, out_shape=out_shape, in_specs=[pl.BlockSpec(memory...]
    unnamed x15 -> x40, local copies, waits for them, and re-layouts: 0.95 us -> 10.7 us
    ppermute x0 -> x10, starting transfers between devices: none -> 9.25 us  [exchange(): return lax.ppermute(value, BOTH, pairs)]
    all_to_all x2 -> x1, blocking collectives: 22.6 us -> 31.6 us  [whole_channels(): recv = lax.all_to_all(send, BOTH, split_axis=0, concat_axis=0, tiled=True)]
  transfers between devices with their start and end apart: 4 -> 11, of which waited for: 4 -> 5; matrix products, arithmetic and copies ran while one was open for 2% -> 1% of each run, Pallas kernels for 0% -> 0%
where the time goes in v1:
time: 97.9 us; the launch traced here: 97.2 us
  blocking collectives  31.6 us (32%)
  waiting for transfers between devices  31.4 us (32%)
  starting transfers between devices  12.9 us (13%)
  local copies, waits for them, and re-layouts  11 us (11%)
  Pallas kernels  10.2 us (10%)
    all_to_all x1, blocking collectives, whole_channels(): recv = lax.all_to_all(send, BOTH, split_axis=0, concat_axis=0, tiled=True)  31.6 us
    ppermute x10, waiting for transfers between devices, exchange(): return lax.ppermute(value, BOTH, pairs)  16.7 us
    all_to_all x1, waiting for transfers between devices, whole_channels(): recv = lax.all_to_all(send, BOTH, split_axis=0, concat_axis=0, tiled=True)  14.7 us
    unnamed x40, local copies, waits for them, and re-layouts  10.7 us
    pallas_call x5, Pallas kernels, call(): pl.pallas_call(kernel, out_shape=out_shape, in_specs=[pl.BlockSpec(memory...  10.2 us
    ppermute x10, starting transfers between devices, exchange(): return lax.ppermute(value, BOTH, pairs)  9.25 us
    all_to_all x1, starting transfers between devices, whole_channels(): recv = lax.all_to_all(send, BOTH, split_axis=0, concat_axis=0, tiled=True)  3.63 us
  transfers between devices with their start and end apart: 11, of which 5 were waited for; matrix products, arithmetic and copies ran while one was open for 1% of the time, Pallas kernels for 0%

profile of v1, /device:TPU:0, one launch (start us, length us, event | category | flops | bytes accessed | tf_op | source)
XLA Modules:
  0.0 97.2 jit_solution(13376113617029741903)
XLA Ops:
  0.0 0.8 copy.30.left_ref
  0.9 0.1 copy.31.right_ref
  1.0 1.0 %copy-done = bf16[4,256,256]{2,1,0:T(8,128)(2,1)S(1)} copy-done((bf16[4,256,256]{2,1,0:T(8,128)(2,1)S(1)}, bf16[4,256,256]{2,1,0:T(8,128)(2,1)}, u32[]{:S(2)}) %copy-start) | copy-done | bytes 524312
  2.0 1.4 %shard_map.109 = (bf16[160,256]{1,0:T(8,128)(2,1)S(1)}, bf16[160,256]{1,0:T(8,128)(2,1)S(1)}, bf16[160,256]{1,0:T(8,128)(2,1)S(1)}, bf16[160,256]{1,0:T(8,128)(2,1)S(1)}) custom-call(bf16[4,256,256]{2,1,0:T(8,128)(2,1)S(1)} %copy-done, bf16[256,32]{1,0:T(8,128)(2,1)S(1)} %copy.30.left_ref, bf16[256,32]{1,0:T(8,128)(2,1)S(1)} %copy.31.right_ref), custom_call_target="tpu_custom_call" | custom-call | flops 33554432 | bytes 884736 | tf_op jit(solution)/shard_map/pallas_call | solution.py:352
  3.4 3.1 %collective-permute-start = (bf16[160,256]{1,0:T(8,128)(2,1)S(1)}, bf16[160,256]{1,0:T(8,128)(2,1)S(1)}, u32[]{:S(2)}, u32[]{:S(2)}) collective-permute-start(bf16[160,256]{1,0:T(8,128)(2,1)S(1)} %get-tuple-element.17), channel_id=1, source_target_pairs={{0,8},{1,9},{2,10},{3,11},{4,12},{5,13},{6,14},{7,15},{8,0},{9,1},... | collective-permute-start | bytes 245768 | tf_op jit(solution)/shard_map/ppermute | solution.py:395
  6.5 2.6 %collective-permute-start.1 = (bf16[160,256]{1,0:T(8,128)(2,1)S(1)}, bf16[160,256]{1,0:T(8,128)(2,1)S(1)}, u32[]{:S(2)}, u32[]{:S(2)}) collective-permute-start(bf16[160,256]{1,0:T(8,128)(2,1)S(1)} %get-tuple-element.18), channel_id=1, source_target_pairs={{0,16},{1,17},{2,18},{3,19},{4,20},{5,21},{6,22},{7,23},{8,24},{9,... | collective-permute-start | bytes 245768 | tf_op jit(solution)/shard_map/ppermute | solution.py:395
  9.1 6.6 %collective-permute-done.1.refs_2_ = bf16[160,256]{1,0:T(8,128)(2,1)S(1)} collective-permute-done((bf16[160,256]{1,0:T(8,128)(2,1)S(1)}, bf16[160,256]{1,0:T(8,128)(2,1)S(1)}, u32[]{:S(2)}, u32[]{:S(2)}) %collective-permute-start.1) | collective-permute-done | bytes 81952 | tf_op jit(solution)/shard_map/ppermute | solution.py:395
  15.7 0.3 shard_map.110
  16.0 1.6 %collective-permute-start.3 = (bf16[544,256]{1,0:T(8,128)(2,1)S(1)}, bf16[544,256]{1,0:T(8,128)(2,1)S(1)}, u32[]{:S(2)}, u32[]{:S(2)}) collective-permute-start(bf16[544,256]{1,0:T(8,128)(2,1)S(1)} %get-tuple-element.21), channel_id=1, source_target_pairs={{0,2},{1,3},{2,0},{3,1},{4,6},{5,7},{6,4},{7,5},{8,10},{9,11},{10,... | collective-permute-start | bytes 835592 | tf_op jit(solution)/shard_map/ppermute | solution.py:395
  17.6 1.5 %collective-permute-start.4 = (bf16[544,256]{1,0:T(8,128)(2,1)S(1)}, bf16[544,256]{1,0:T(8,128)(2,1)S(1)}, u32[]{:S(2)}, u32[]{:S(2)}) collective-permute-start(bf16[544,256]{1,0:T(8,128)(2,1)S(1)} %get-tuple-element.22), channel_id=1, source_target_pairs={{0,4},{1,5},{2,6},{3,7},{4,0},{5,1},{6,2},{7,3},{8,12},{9,13},{10,... | collective-permute-start | bytes 835592 | tf_op jit(solution)/shard_map/ppermute | solution.py:395
  19.1 0.5 collective-permute-start.5
  19.5 5.4 %collective-permute-done.3.refs_1_ = bf16[544,256]{1,0:T(8,128)(2,1)S(1)} collective-permute-done((bf16[544,256]{1,0:T(8,128)(2,1)S(1)}, bf16[544,256]{1,0:T(8,128)(2,1)S(1)}, u32[]{:S(2)}, u32[]{:S(2)}) %collective-permute-start.3) | collective-permute-done | bytes 278560 | tf_op jit(solution)/shard_map/ppermute | solution.py:395
  24.9 1.8 %collective-permute-done.4.refs_2_ = bf16[544,256]{1,0:T(8,128)(2,1)S(1)} collective-permute-done((bf16[544,256]{1,0:T(8,128)(2,1)S(1)}, bf16[544,256]{1,0:T(8,128)(2,1)S(1)}, u32[]{:S(2)}, u32[]{:S(2)}) %collective-permute-start.4) | collective-permute-done | bytes 278560 | tf_op jit(solution)/shard_map/ppermute | solution.py:395
  26.7 2.9 %collective-permute-done.5.refs_3_ = bf16[544,256]{1,0:T(8,128)(2,1)S(1)} collective-permute-done((bf16[544,256]{1,0:T(8,128)(2,1)S(1)}, bf16[544,256]{1,0:T(8,128)(2,1)S(1)}, u32[]{:S(2)}, u32[]{:S(2)}) %collective-permute-start.5) | collective-permute-done | bytes 278560 | tf_op jit(solution)/shard_map/ppermute | solution.py:395
  29.8 0.1 copy.37.refs_9_
  29.9 0.5 copy-done.9
  30.5 0.6 copy-done.10
  31.3 0.6 copy-done.11
  32.1 0.6 copy-done.12
  32.9 0.7 copy-done.2
  33.6 0.7 copy-done.4
  34.3 0.7 copy-done.6
  35.0 1.0 copy-done.3
  36.0 1.0 copy-done.5
  36.9 1.0 copy-done.7
  37.9 5.2 %shard_map.111 = (bf16[2048,256]{1,0:T(8,128)(2,1)S(1)}, bf16[8,128,256]{2,1,0:T(8,128)(2,1)S(1)}, bf16[8,128,256]{2,1,0:T(8,128)(2,1)S(1)}) custom-call(bf16[544,256]{1,0:T(8,128)(2,1)S(1)} %get-tuple-element.20.refs_0_, bf16[544,256]{1,0:T(8,128)(2,1)S(1)} %collective-permute-done.3.refs_1_, bf16[544,256]{1,0:T(8,128)(2,1)S(1)} %collective-permute-done.4.refs_2_, ...), custom_call_target="tpu_custom_call" | custom-call | flops 1342177280 | bytes 5242880 | tf_op jit(solution)/shard_map/pallas_call | solution.py:352
  43.1 31.6 %all_to_all.22 = bf16[32,64,256]{2,1,0:T(8,128)(2,1)S(1)} all-to-all(bf16[32,64,256]{2,1,0:T(8,128)(2,1)S(1)} %bitcast.16), channel_id=1, replica_groups=mesh['row'=8,'col'=1,'seq'=4] {'row','seq'}, dimensions={0} | all-to-all | bytes 2097152 | tf_op jit(solution)/shard_map/all_to_all | solution.py:438
  74.7 1.1 %shard_map.112 = bf16[1024,256]{1,0:T(8,128)(2,1)} custom-call(bf16[2048,256]{1,0:T(8,128)(2,1)S(1)} %bitcast.14), custom_call_target="tpu_custom_call" | custom-call | flops 134217728 | bytes 1572864 | tf_op jit(solution)/shard_map/pallas_call | solution.py:352
  75.8 3.6 %all-to-all-start.1 = ((bf16[32,32,256]{2,1,0:T(8,128)(2,1)}), bf16[32,32,256]{2,1,0:T(8,128)(2,1)S(1)}, u32[]{:S(2)}, u32[]{:S(2)}) async-start(bf16[32,32,256]{2,1,0:T(8,128)(2,1)} %bitcast.9), calls=%async_computation.1 | async-start | bytes 1048576 | tf_op jit(solution)/shard_map/all_to_all | solution.py:449
  79.6 0.6 copy-done.14
  80.3 14.7 %all-to-all-done.1 = bf16[32,32,256]{2,1,0:T(8,128)(2,1)S(1)} async-done(((bf16[32,32,256]{2,1,0:T(8,128)(2,1)}), bf16[32,32,256]{2,1,0:T(8,128)(2,1)S(1)}, u32[]{:S(2)}, u32[]{:S(2)}) %all-to-all-start.1) | async-done | bytes 524320 | tf_op jit(solution)/shard_map/all_to_all | solution.py:449
  95.0 2.2 %shard_map.113 = bf16[8,256,128]{2,1,0:T(8,128)(2,1)} custom-call(bf16[1024,256]{1,0:T(8,128)(2,1)S(1)} %bitcast.15, bf16[8,128,256]{2,1,0:T(8,128)(2,1)S(1)} %get-tuple-element.25.mid_ref, bf16[8,128,256]{2,1,0:T(8,128)(2,1)S(1)} %get-tuple-element.26.norm_ref, bf16[128,128]{1,0:T(8,128)(2,1)S(1)} %bitcast.17, bf16[128,128]{1,0:T(8,128)(2,1)S(1)} %bitcast.18), custom_call_target="tpu_custom_call" | custom-call | flops 134217728 | bytes 2162688 | tf_op jit(solution)/shard_map/pallas_call | solution.py:352
  (39 shorter events, 0.9 us)
Async XLA Ops:
  0.0 0.9 copy-start.15
  1.0 1.0 %copy-start = (bf16[4,256,256]{2,1,0:T(8,128)(2,1)S(1)}, bf16[4,256,256]{2,1,0:T(8,128)(2,1)}, u32[]{:S(2)}) copy-start(bf16[4,256,256]{2,1,0:T(8,128)(2,1)} %align_ref.1) | copy-start | bytes 1572868
  3.4 26.2 %copy-start.8 = (bf16[1024,128]{1,0:T(8,128)(2,1)S(1)}, bf16[1024,128]{1,0:T(8,128)(2,1)}, u32[]{:S(2)}) copy-start(bf16[1024,128]{1,0:T(8,128)(2,1)} %param.15) | copy-start | bytes 786436
  3.4 5.7 %collective-permute-start = (bf16[160,256]{1,0:T(8,128)(2,1)S(1)}, bf16[160,256]{1,0:T(8,128)(2,1)S(1)}, u32[]{:S(2)}, u32[]{:S(2)}) collective-permute-start(bf16[160,256]{1,0:T(8,128)(2,1)S(1)} %get-tuple-element.17), channel_id=1, source_target_pairs={{0,8},{1,9},{2,10},{3,11},{4,12},{5,13},{6,14},{7,15},{8,0},{9,1},... | collective-permute-start | bytes 245768 | tf_op jit(solution)/shard_map/ppermute | solution.py:395
  6.5 9.2 %collective-permute-start.1 = (bf16[160,256]{1,0:T(8,128)(2,1)S(1)}, bf16[160,256]{1,0:T(8,128)(2,1)S(1)}, u32[]{:S(2)}, u32[]{:S(2)}) collective-permute-start(bf16[160,256]{1,0:T(8,128)(2,1)S(1)} %get-tuple-element.18), channel_id=1, source_target_pairs={{0,16},{1,17},{2,18},{3,19},{4,20},{5,21},{6,22},{7,23},{8,24},{9,... | collective-permute-start | bytes 245768 | tf_op jit(solution)/shard_map/ppermute | solution.py:395
  9.1 6.6 %collective-permute-start.2 = (bf16[160,256]{1,0:T(8,128)(2,1)S(1)}, bf16[160,256]{1,0:T(8,128)(2,1)S(1)}, u32[]{:S(2)}, u32[]{:S(2)}) collective-permute-start(bf16[160,256]{1,0:T(8,128)(2,1)S(1)} %get-tuple-element.19), channel_id=1, source_target_pairs={{0,24},{1,25},{2,26},{3,27},{4,28},{5,29},{6,30},{7,31},{8,16},{9,... | collective-permute-start | bytes 245768 | tf_op jit(solution)/shard_map/ppermute | solution.py:395
  16.0 8.9 %collective-permute-start.3 = (bf16[544,256]{1,0:T(8,128)(2,1)S(1)}, bf16[544,256]{1,0:T(8,128)(2,1)S(1)}, u32[]{:S(2)}, u32[]{:S(2)}) collective-permute-start(bf16[544,256]{1,0:T(8,128)(2,1)S(1)} %get-tuple-element.21), channel_id=1, source_target_pairs={{0,2},{1,3},{2,0},{3,1},{4,6},{5,7},{6,4},{7,5},{8,10},{9,11},{10,... | collective-permute-start | bytes 835592 | tf_op jit(solution)/shard_map/ppermute | solution.py:395
  17.6 9.2 %collective-permute-start.4 = (bf16[544,256]{1,0:T(8,128)(2,1)S(1)}, bf16[544,256]{1,0:T(8,128)(2,1)S(1)}, u32[]{:S(2)}, u32[]{:S(2)}) collective-permute-start(bf16[544,256]{1,0:T(8,128)(2,1)S(1)} %get-tuple-element.22), channel_id=1, source_target_pairs={{0,4},{1,5},{2,6},{3,7},{4,0},{5,1},{6,2},{7,3},{8,12},{9,13},{10,... | collective-permute-start | bytes 835592 | tf_op jit(solution)/shard_map/ppermute | solution.py:395
  19.1 10.6 %collective-permute-start.5 = (bf16[544,256]{1,0:T(8,128)(2,1)S(1)}, bf16[544,256]{1,0:T(8,128)(2,1)S(1)}, u32[]{:S(2)}, u32[]{:S(2)}) collective-permute-start(bf16[544,256]{1,0:T(8,128)(2,1)S(1)} %get-tuple-element.23), channel_id=1, source_target_pairs={{0,6},{1,7},{2,4},{3,5},{4,2},{5,3},{6,0},{7,1},{8,14},{9,15},{10,... | collective-permute-start | bytes 835592 | tf_op jit(solution)/shard_map/ppermute | solution.py:395
  19.5 13.3 %collective-permute-start.6 = (bf16[544,256]{1,0:T(8,128)(2,1)S(1)}, bf16[544,256]{1,0:T(8,128)(2,1)S(1)}, u32[]{:S(2)}, u32[]{:S(2)}) collective-permute-start(bf16[544,256]{1,0:T(8,128)(2,1)S(1)} %get-tuple-element.20.refs_0_), channel_id=1, source_target_pairs={{0,1},{1,0},{2,3},{3,2},{4,5},{5,4},{6,7},{7,6},{8,9},{9,8},{10,11... | collective-permute-start | bytes 835592 | tf_op jit(solution)/shard_map/ppermute | solution.py:395
  24.9 8.0 %collective-permute-start.7 = (bf16[544,256]{1,0:T(8,128)(2,1)S(1)}, bf16[544,256]{1,0:T(8,128)(2,1)S(1)}, u32[]{:S(2)}, u32[]{:S(2)}) collective-permute-start(bf16[544,256]{1,0:T(8,128)(2,1)S(1)} %collective-permute-done.3.refs_1_), channel_id=1, source_target_pairs={{0,1},{1,0},{2,3},{3,2},{4,5},{5,4},{6,7},{7,6},{8,9},{9,8},{10,11... | collective-permute-start | bytes 835592 | tf_op jit(solution)/shard_map/ppermute | solution.py:395
  26.7 6.8 %collective-permute-start.8 = (bf16[544,256]{1,0:T(8,128)(2,1)S(1)}, bf16[544,256]{1,0:T(8,128)(2,1)S(1)}, u32[]{:S(2)}, u32[]{:S(2)}) collective-permute-start(bf16[544,256]{1,0:T(8,128)(2,1)S(1)} %collective-permute-done.4.refs_2_), channel_id=1, source_target_pairs={{0,1},{1,0},{2,3},{3,2},{4,5},{5,4},{6,7},{7,6},{8,9},{9,8},{10,11... | collective-permute-start | bytes 835592 | tf_op jit(solution)/shard_map/ppermute | solution.py:395
  29.7 4.6 %collective-permute-start.9 = (bf16[544,256]{1,0:T(8,128)(2,1)S(1)}, bf16[544,256]{1,0:T(8,128)(2,1)S(1)}, u32[]{:S(2)}, u32[]{:S(2)}) collective-permute-start(bf16[544,256]{1,0:T(8,128)(2,1)S(1)} %collective-permute-done.5.refs_3_), channel_id=1, source_target_pairs={{0,1},{1,0},{2,3},{3,2},{4,5},{5,4},{6,7},{7,6},{8,9},{9,8},{10,11... | collective-permute-start | bytes 835592 | tf_op jit(solution)/shard_map/ppermute | solution.py:395
  29.7 0.8 copy-start.9
  29.8 5.2 %copy-start.1 = (bf16[8,256,128]{2,1,0:T(8,128)(2,1)S(1)}, bf16[8,256,128]{2,1,0:T(8,128)(2,1)}, u32[]{:S(2)}) copy-start(bf16[8,256,128]{2,1,0:T(8,128)(2,1)} %refs_8_.1) | copy-start | bytes 1572868
  30.4 0.8 copy-start.10
  31.2 0.8 copy-start.11
  31.9 0.8 copy-start.12
  32.9 0.7 copy-start.2
  33.6 0.7 copy-start.4
  34.3 0.7 copy-start.6
  35.0 1.0 copy-start.3
  36.0 1.0 copy-start.5
  36.9 1.0 copy-start.7
  75.8 3.6 %copy-start.13 = (bf16[128,128]{1,0:T(8,128)(2,1)S(1)}, bf16[128,128]{1,0:T(8,128)(2,1)}, u32[]{:S(2)}) copy-start(bf16[128,128]{1,0:T(8,128)(2,1)} %param.20) | copy-start | bytes 98308
  75.8 19.2 %all-to-all-start.1 = ((bf16[32,32,256]{2,1,0:T(8,128)(2,1)}), bf16[32,32,256]{2,1,0:T(8,128)(2,1)S(1)}, u32[]{:S(2)}, u32[]{:S(2)}) async-start(bf16[32,32,256]{2,1,0:T(8,128)(2,1)} %bitcast.9), calls=%async_computation.1 | async-start | bytes 1048576 | tf_op jit(solution)/shard_map/all_to_all | solution.py:449
  79.5 0.8 copy-start.14

commit v2 on v1

--- a/solution.py
+++ b/solution.py
@@ -1,4 +1,5 @@
 import functools
+import math
 
 import jax
 import jax.numpy as jnp
@@ -184,16 +185,29 @@
     return center * lax.rsqrt(spread + EPS)
 
 
-def factors_kernel(sizes, align_ref, left_ref, right_ref, *refs):
+def fetch(sems, pairs):
+    copies = [
+        pltpu.make_async_copy(source, target, sems.at[k]) for k, (source, target) in enumerate(pairs)
+    ]
+    for copy in copies:
+        copy.start()
+    return copies
+
+
+def factors_kernel(sizes, align_in, left_in, right_in, *refs):
     n_far, n_near, n_core, rows, _ = sizes
-    out_refs, parts = refs[:n_far], refs[n_far]
+    out_refs, (parts, align_ref, left_ref, right_ref, sems) = refs[:n_far], refs[n_far:]
+    pairs = [(left_in, left_ref), (right_in, right_ref)]
+    pairs += [(align_in.at[n], align_ref.at[n]) for n in range(align_in.shape[0])]
+    copies = fetch(sems, pairs)
+    copies[0].wait()
+    copies[1].wait()
     seqs, cols, width = align_ref.shape
-    factor = left_ref.shape[1]
+    factor = left_ref.shape[0]
     chip_rows = n_core * rows
     chips = n_far * n_near
-    row, col = iotas(factor, chip_rows * factor)
-    left_wide = mul(left_ref[...], ones_where(row == col % factor)).astype(BF16)
-    right_t = right_ref[...].astype(F32).T.astype(BF16)
+    row, col = iotas(chip_rows * factor, factor)
+    left_wide = mul(ones_where(row % factor == col), left_ref[...]).astype(BF16)
     row, col = iotas(cols, chip_rows * factor)
     own_lane = (row % chip_rows) == (col // factor)
     row, col = iotas(n_far * seqs * n_near, cols)
@@ -202,9 +216,10 @@
     chip_match = chip_of_row == col // chip_rows
     right_rows, left_rows = [], None
     for n in range(seqs):
+        copies[2 + n].wait()
         normed = normalize(align_ref[n].astype(F32), 1).astype(BF16)
-        right_rows.append(mul_t(right_t, normed))
-        spread = jnp.where(own_lane, mul(normed, left_wide), 0.0).astype(BF16)
+        right_rows.append(mul_t(right_ref[...], normed))
+        spread = jnp.where(own_lane, mul_t(normed, left_wide), 0.0).astype(BF16)
         part = mul(ones_where(chip_match & (seq_of_row == n)), spread)
         left_rows = part if left_rows is None else left_rows + part
     right_block = jnp.concatenate(right_rows, 0).astype(BF16)
@@ -257,12 +272,46 @@
         out_refs[k][factor * held :, :] = parts[here ^ k]
 
 
+def prepare_kernel(factor, *refs):
+    n = (len(refs) - 6) // 2
+    sources, (pair_t, out_t, tri_t, gate_t, final_t), targets = refs[:n], refs[n : n + 5], refs[n + 5 : -1]
+    copies = fetch(refs[-1], list(zip(sources, targets, strict=True)))
+    pair_ref, out_w, *tri, gate_w, final_w = targets
+    eye = identity(pair_ref.shape[2])
+    for copy in copies:
+        copy.wait()
+    for i in range(pair_ref.shape[0]):
+        pair_t[i] = mul_t(eye, pair_ref[i]).astype(BF16)
+    shuffle = swap_rows(256 // 16, 16)
+    for q in range(0, factor, 16):
+        for p in range(0, factor, 256 // 16):
+            block = jnp.concatenate(
+                [
+                    out_w[(p + k) * factor + q : (p + k) * factor + q + 16, :]
+                    for k in range(256 // 16)
+                ],
+                0,
+            )
+            block = mul(shuffle, block).astype(BF16)
+            block = mul_t(eye, block).astype(BF16)
+            at = (q // 16 * (factor // 16) + p // 16) * 256
+            out_t[:, at : at + 256] = block
+    for k, ref in enumerate(tri):
+        width = ref.shape[1]
+        tri_t[k * width : (k + 1) * width, :] = mul_t(eye, ref[...]).astype(BF16)
+    gate_t[...] = mul_t(eye, gate_w[...]).astype(BF16)
+    final_t[...] = mul_t(eye, final_w[...]).astype(BF16)
+
+
+def gate_kernel(norm_ref, gate_w, gate_ref):
+    for i in range(norm_ref.shape[0]):
+        gate_ref[i] = jax.nn.sigmoid(mul(gate_w[...], norm_ref[i]))
+
+
 def pair_kernel(sizes, held, scale, *refs):
     n_core, rows, n_dev = sizes[2], sizes[3], sizes[4]
     groups = refs[:-8]
     pair_ref, out_w, tri_w, send_ref, mid_ref, norm_ref, outer, both = refs[-8:]
-    _, cols, width = pair_ref.shape
-    factor_sq = out_w.shape[1]
     factor = groups[0].shape[0] // held - n_core
     hidden = tri_w.shape[0] // 4
     core = lax.axis_index("seq") % n_core
@@ -273,11 +322,12 @@
         right = jnp.concatenate([ref[q * held : (q + 1) * held, :] for ref in groups], 0)
         block = mul(left_t, right).astype(BF16)
         for i in range(rows):
-            outer[i, q * factor : (q + 1) * factor, :] = block[i * factor : (i + 1) * factor]
-    eye = identity(width)
+            for p in range(0, factor, 16):
+                at = (q // 16 * (factor // 16) + p // 16) * 256 + q % 16 * 16
+                outer[i, at : at + 16, :] = block[i * factor + p : i * factor + p + 16]
     for i in range(rows):
         update = mul(out_w[...], outer[i])
-        mid = (mul_t(eye, pair_ref[i]) + update * scale).astype(BF16)
+        mid = (pair_ref[i].astype(F32) + update * scale).astype(BF16)
         mid_ref[i] = mid
         normed = normalize(mid.astype(F32), 0).astype(BF16)
         norm_ref[i] = normed
@@ -318,7 +368,7 @@
         send_ref[dst * chunk : (dst + 1) * chunk, :] = total[dst].astype(BF16)
 
 
-def finish_kernel(sizes, recv_ref, mid_ref, norm_ref, gate_w, out_w, out_ref, apart):
+def finish_kernel(sizes, recv_ref, mid_ref, gate_ref, out_w, out_ref, apart, done_ref, sems):
     rows = sizes[3]
     _, width, cols = mid_ref.shape
     hidden = out_w.shape[1]
@@ -339,23 +389,31 @@
         for i in range(rows):
             apart[i, b * some : (b + 1) * some, :] = normed[i * some : (i + 1) * some]
     eye = identity(cols)
+    copies = []
     for i in range(rows):
         update = mul(out_w[...], apart[i])
-        gate = jax.nn.sigmoid(mul(gate_w[...], norm_ref[i]))
-        done = (mid_ref[i].astype(F32) + gate * update).astype(BF16)
-        out_ref[i] = mul_t(eye, done).astype(BF16)
-
-
-def call(kernel, out_shape, scratch, flops, *args):
-    out_shape = [jax.ShapeDtypeStruct(s, BF16) for s in out_shape]
-    moved = sum(a.size * 2 for a in (*args, *out_shape))
+        done = (mid_ref[i].astype(F32) + gate_ref[i] * update).astype(BF16)
+        done_ref[i] = mul_t(eye, done).astype(BF16)
+        copies.append(pltpu.make_async_copy(done_ref.at[i], out_ref.at[i], sems.at[i]))
+        copies[i].start()
+    for copy in copies:
+        copy.wait()
+
+
+def call(kernel, out_shape, scratch, grant, flops, *args, far_in=False, far_out=False):
+    spaces = [pltpu.HBM if far else pltpu.VMEM for far in (far_in, far_out)]
+    place = jax.ShapeDtypeStruct if far_out else pltpu.VMEM
+    out_shape = [place(*s) if isinstance(s[0], tuple) else place(s, BF16) for s in out_shape]
+    if far_in:
+        args = [pltpu.with_memory_space_constraint(a, pltpu.HBM) for a in args]
+    moved = sum(math.prod(a.shape) * jnp.dtype(a.dtype).itemsize for a in (*args, *out_shape))
     return pl.pallas_call(
         kernel,
         out_shape=out_shape,
-        in_specs=[pl.BlockSpec(memory_space=pltpu.VMEM)] * len(args),
-        out_specs=[pl.BlockSpec(memory_space=pltpu.VMEM)] * len(out_shape),
+        in_specs=[pl.BlockSpec(memory_space=spaces[0])] * len(args),
+        out_specs=[pl.BlockSpec(memory_space=spaces[1])] * len(out_shape),
         scratch_shapes=scratch,
-        compiler_params=pltpu.CompilerParams(vmem_limit_bytes=40 * 2**20),
+        compiler_params=pltpu.CompilerParams(vmem_limit_bytes=grant * 2**20),
         cost_estimate=pl.CostEstimate(flops=flops, bytes_accessed=moved, transcendentals=0),
     )(*args)
 
@@ -394,26 +452,59 @@
         ]
         return lax.ppermute(value, BOTH, pairs)
 
-    out_wt = jnp.transpose(opm_out.reshape(factor, factor, width), (2, 1, 0))
-    out_wt = out_wt.reshape(width, factor * factor)
-    tri_wt = jnp.concatenate([w.T for w in (tri_left_gate, tri_left, tri_right_gate, tri_right)], 0)
-
     message = (seqs * factor + n_core * seqs * n_near, cols)
     mine = call(
         functools.partial(factors_kernel, sizes),
         [message] * n_far,
-        [pltpu.VMEM((n_far, n_core * seqs * n_near, cols), BF16)],
+        [
+            pltpu.VMEM((n_far, n_core * seqs * n_near, cols), BF16),
+            pltpu.VMEM(alignment.shape, BF16),
+            pltpu.VMEM(opm_left.shape[::-1], BF16),
+            pltpu.VMEM(opm_right.shape[::-1], BF16),
+            pltpu.SemaphoreType.DMA((2 + seqs,)),
+        ],
+        8,
         4 * seqs * cols * alignment.shape[2] * factor,
         alignment,
-        opm_left,
-        opm_right,
-    )
+        opm_left.T,
+        opm_right.T,
+        far_in=True,
+    )
+    weights = (
+        pair,
+        opm_out,
+        tri_left_gate,
+        tri_left,
+        tri_right_gate,
+        tri_right,
+        tri_gate,
+        tri_out,
+    )
+    mine, weights = lax.optimization_barrier((mine, weights))
     far = [mine[0]] + [exchange(mine[k], 2 * k, 0) for k in range(1, n_far)]
+    prepared = call(
+        functools.partial(prepare_kernel, factor),
+        [
+            (rows, width, cols),
+            (width, factor * factor),
+            (4 * hidden, width),
+            (width, width),
+            (width, hidden),
+        ],
+        [pltpu.VMEM(w.shape, BF16) for w in weights] + [pltpu.SemaphoreType.DMA((len(weights),))],
+        8,
+        4 * rows * cols * width * width,
+        *weights,
+        far_in=True,
+    )
+    far, prepared = lax.optimization_barrier((far, prepared))
+    pair_t, out_t, tri_t, gate_t, final_t = prepared
     message = ((factor + n_core) * held, cols)
     mine = call(
         functools.partial(regroup_kernel, sizes, factor, seqs),
         [message] * n_near,
         [pltpu.VMEM((n_near, n_core * held, cols), BF16)],
+        8,
         2 * 256 * factor * held * cols,
         *far,
     )
@@ -429,11 +520,21 @@
             pltpu.VMEM((rows, factor * factor, cols), BF16),
             pltpu.VMEM((2, rows, hidden, cols), BF16),
         ],
+        16,
         4 * rows * cols * width * (factor * factor + hidden * 2),
         *groups,
-        pair,
-        out_wt,
-        tri_wt,
+        pair_t,
+        out_t,
+        tri_t,
+    )
+    (gate,) = call(
+        gate_kernel,
+        [((rows, width, cols), F32)],
+        [],
+        8,
+        2 * rows * cols * width * width,
+        normed,
+        gate_t,
     )
     recv = lax.all_to_all(send, BOTH, split_axis=0, concat_axis=0, tiled=True)
     (send,) = call(
@@ -443,6 +544,7 @@
             pltpu.VMEM((2, per, rows * n_dev, cols), F32),
             pltpu.VMEM((n_dev, per * rows, cols), F32),
         ],
+        16,
         2 * per * cols * cols * cols,
         recv,
     )
@@ -450,13 +552,18 @@
     (out,) = call(
         functools.partial(finish_kernel, sizes),
         [(rows, cols, width)],
-        [pltpu.VMEM((rows, hidden, cols), BF16)],
+        [
+            pltpu.VMEM((rows, hidden, cols), BF16),
+            pltpu.VMEM((rows, cols, width), BF16),
+            pltpu.SemaphoreType.DMA((rows,)),
+        ],
+        16,
         4 * rows * cols * width * hidden,
         recv,
         mid,
-        normed,
-        tri_gate.T,
-        tri_out.T,
+        gate,
+        final_t,
+        far_out=True,
     )
     return out
 
@@ -466,7 +573,7 @@
 
 
 def on_device(pair, alignment, opm_left, *rest):
-    rows, cols, _ = pair.shape
+    rows, cols, width = pair.shape
     factor, hidden = opm_left.shape[1], rest[2].shape[1]
     n_row, n_col, n_seq = (lax.axis_size(a) for a in ("row", "col", "seq"))
     n_dev = n_row * n_seq
@@ -479,6 +586,8 @@
         and n_row >= 4
         and n_seq >= 4
         and hidden % n_dev == 0
+        and hidden == width
+        and factor % 16 == 0
         and rows % 8 == 0
         and (hidden // n_dev * rows) % 16 == 0
         and cols % 256 == 0

time: 97.9 us -> 89.3 us (0.912)
  local copies, waits for them, and re-layouts: 11 us -> 0 us
  Pallas kernels: 10.2 us -> 13.5 us
    unnamed x40 -> x0, local copies, waits for them, and re-layouts: 10.7 us -> none
    pallas_call x5 -> x7, Pallas kernels: 10.2 us -> 13.5 us  [call(): pl.pallas_call(kernel, out_shape=out_shape, in_specs=[pl.BlockSpec(memory...]
  transfers between devices with their start and end apart: 11 -> 11, of which waited for: 5 -> 6; matrix products, arithmetic and copies ran while one was open for 1% -> 0% of each run, Pallas kernels for 0% -> 3%
where the time goes in v2:
time: 89.3 us; the launch traced here: 89 us
  blocking collectives  31.5 us (35%)
  waiting for transfers between devices  31 us (35%)
  Pallas kernels  13.5 us (15%)
  starting transfers between devices  12.9 us (14%)
    all_to_all x1, blocking collectives, whole_channels(): recv = lax.all_to_all(send, BOTH, split_axis=0, concat_axis=0, tiled=True)  31.5 us
    ppermute x10, waiting for transfers between devices, exchange(): return lax.ppermute(value, BOTH, pairs)  15.8 us
    all_to_all x1, waiting for transfers between devices, whole_channels(): recv = lax.all_to_all(send, BOTH, split_axis=0, concat_axis=0, tiled=True)  15.2 us
    pallas_call x7, Pallas kernels, call(): pl.pallas_call(kernel, out_shape=out_shape, in_specs=[pl.BlockSpec(memory...  13.5 us
    ppermute x10, starting transfers between devices, exchange(): return lax.ppermute(value, BOTH, pairs)  9.25 us
    all_to_all x1, starting transfers between devices, whole_channels(): recv = lax.all_to_all(send, BOTH, split_axis=0, concat_axis=0, tiled=True)  3.62 us
  transfers between devices with their start and end apart: 11, of which 6 were waited for; matrix products, arithmetic and copies ran while one was open for 0% of the time, Pallas kernels for 3%

profile of v2, /device:TPU:0, one launch (start us, length us, event | category | flops | bytes accessed | tf_op | source)
XLA Modules:
  0.0 89.0 jit_solution(11614897646576859656)
XLA Ops:
  0.0 3.5 %shard_map.109 = (bf16[160,256]{1,0:T(8,128)(2,1)S(1)}, bf16[160,256]{1,0:T(8,128)(2,1)S(1)}, bf16[160,256]{1,0:T(8,128)(2,1)S(1)}, bf16[160,256]{1,0:T(8,128)(2,1)S(1)}) custom-call(bf16[4,256,256]{2,1,0:T(8,128)(2,1)} %align_in.1, bf16[32,256]{1,0:T(8,128)(2,1)} %bitcast.9, bf16[32,256]{1,0:T(8,128)(2,1)} %bitcast.10), custom_call_target="tpu_custom_call" | custom-call | flops 33554432 | bytes 884736 | tf_op jit(solution)/shard_map/pallas_call | solution.py:410
  3.5 3.1 %collective-permute-start = (bf16[160,256]{1,0:T(8,128)(2,1)S(1)}, bf16[160,256]{1,0:T(8,128)(2,1)S(1)}, u32[]{:S(2)}, u32[]{:S(2)}) collective-permute-start(bf16[160,256]{1,0:T(8,128)(2,1)S(1)} %get-tuple-element.47), channel_id=1, source_target_pairs={{0,8},{1,9},{2,10},{3,11},{4,12},{5,13},{6,14},{7,15},{8,0},{9,1},... | collective-permute-start | bytes 245768 | tf_op jit(solution)/shard_map/ppermute | solution.py:453
  6.6 2.6 %collective-permute-start.1 = (bf16[160,256]{1,0:T(8,128)(2,1)S(1)}, bf16[160,256]{1,0:T(8,128)(2,1)S(1)}, u32[]{:S(2)}, u32[]{:S(2)}) collective-permute-start(bf16[160,256]{1,0:T(8,128)(2,1)S(1)} %get-tuple-element.48), channel_id=1, source_target_pairs={{0,16},{1,17},{2,18},{3,19},{4,20},{5,21},{6,22},{7,23},{8,24},{9,... | collective-permute-start | bytes 245768 | tf_op jit(solution)/shard_map/ppermute | solution.py:453
  9.2 0.0 collective-permute-start.2
  9.2 2.5 %shard_map.110 = (bf16[8,128,256]{2,1,0:T(8,128)(2,1)S(1)}, bf16[128,1024]{1,0:T(8,128)(2,1)S(1)}, bf16[512,128]{1,0:T(8,128)(2,1)S(1)}, bf16[128,128]{1,0:T(8,128)(2,1)S(1)}, bf16[128,128]{1,0:T(8,128)(2,1)S(1)}) custom-call(bf16[8,256,128]{2,1,0:T(8,128)(2,1)} %refs_0_, bf16[1024,128]{1,0:T(8,128)(2,1)} %refs_1_, bf16[128,128]{1,0:T(8,128)(2,1)} %refs_2_, ...), custom_call_target="tpu_custom_call" | custom-call | flops 134217728 | bytes 1966080 | tf_op jit(solution)/shard_map/pallas_call | solution.py:410
  11.7 0.0 collective-permute-done.refs_1_
  11.7 4.1 %collective-permute-done.1.refs_2_ = bf16[160,256]{1,0:T(8,128)(2,1)S(1)} collective-permute-done((bf16[160,256]{1,0:T(8,128)(2,1)S(1)}, bf16[160,256]{1,0:T(8,128)(2,1)S(1)}, u32[]{:S(2)}, u32[]{:S(2)}) %collective-permute-start.1) | collective-permute-done | bytes 81952 | tf_op jit(solution)/shard_map/ppermute | solution.py:453
  15.8 0.0 collective-permute-done.2.refs_3_
  15.8 0.3 shard_map.111
  16.1 1.6 %collective-permute-start.3 = (bf16[544,256]{1,0:T(8,128)(2,1)S(1)}, bf16[544,256]{1,0:T(8,128)(2,1)S(1)}, u32[]{:S(2)}, u32[]{:S(2)}) collective-permute-start(bf16[544,256]{1,0:T(8,128)(2,1)S(1)} %get-tuple-element.68), channel_id=1, source_target_pairs={{0,2},{1,3},{2,0},{3,1},{4,6},{5,7},{6,4},{7,5},{8,10},{9,11},{10,... | collective-permute-start | bytes 835592 | tf_op jit(solution)/shard_map/ppermute | solution.py:453
  17.6 1.5 %collective-permute-start.4 = (bf16[544,256]{1,0:T(8,128)(2,1)S(1)}, bf16[544,256]{1,0:T(8,128)(2,1)S(1)}, u32[]{:S(2)}, u32[]{:S(2)}) collective-permute-start(bf16[544,256]{1,0:T(8,128)(2,1)S(1)} %get-tuple-element.69), channel_id=1, source_target_pairs={{0,4},{1,5},{2,6},{3,7},{4,0},{5,1},{6,2},{7,3},{8,12},{9,13},{10,... | collective-permute-start | bytes 835592 | tf_op jit(solution)/shard_map/ppermute | solution.py:453
  19.1 0.5 collective-permute-start.5
  19.6 0.0 collective-permute-start.6
  19.6 5.4 %collective-permute-done.3.refs_1_ = bf16[544,256]{1,0:T(8,128)(2,1)S(1)} collective-permute-done((bf16[544,256]{1,0:T(8,128)(2,1)S(1)}, bf16[544,256]{1,0:T(8,128)(2,1)S(1)}, u32[]{:S(2)}, u32[]{:S(2)}) %collective-permute-start.3) | collective-permute-done | bytes 278560 | tf_op jit(solution)/shard_map/ppermute | solution.py:453
  25.0 0.0 collective-permute-start.7
  25.0 1.8 %collective-permute-done.4.refs_2_ = bf16[544,256]{1,0:T(8,128)(2,1)S(1)} collective-permute-done((bf16[544,256]{1,0:T(8,128)(2,1)S(1)}, bf16[544,256]{1,0:T(8,128)(2,1)S(1)}, u32[]{:S(2)}, u32[]{:S(2)}) %collective-permute-start.4) | collective-permute-done | bytes 278560 | tf_op jit(solution)/shard_map/ppermute | solution.py:453
  26.8 0.0 collective-permute-start.8
  26.8 2.9 %collective-permute-done.5.refs_3_ = bf16[544,256]{1,0:T(8,128)(2,1)S(1)} collective-permute-done((bf16[544,256]{1,0:T(8,128)(2,1)S(1)}, bf16[544,256]{1,0:T(8,128)(2,1)S(1)}, u32[]{:S(2)}, u32[]{:S(2)}) %collective-permute-start.5) | collective-permute-done | bytes 278560 | tf_op jit(solution)/shard_map/ppermute | solution.py:453
  29.7 0.0 collective-permute-start.9
  29.7 0.0 collective-permute-done.6.refs_4_
  29.7 0.0 collective-permute-done.7.refs_5_
  29.7 0.0 collective-permute-done.8.refs_6_
  29.8 1.5 %collective-permute-done.9.refs_7_ = bf16[544,256]{1,0:T(8,128)(2,1)S(1)} collective-permute-done((bf16[544,256]{1,0:T(8,128)(2,1)S(1)}, bf16[544,256]{1,0:T(8,128)(2,1)S(1)}, u32[]{:S(2)}, u32[]{:S(2)}) %collective-permute-start.9) | collective-permute-done | bytes 278560 | tf_op jit(solution)/shard_map/ppermute | solution.py:453
  31.3 3.5 %shard_map.112 = (bf16[2048,256]{1,0:T(8,128)(2,1)S(1)}, bf16[8,128,256]{2,1,0:T(8,128)(2,1)S(1)}, bf16[8,128,256]{2,1,0:T(8,128)(2,1)S(1)}) custom-call(bf16[544,256]{1,0:T(8,128)(2,1)S(1)} %get-tuple-element.67.refs_0_, bf16[544,256]{1,0:T(8,128)(2,1)S(1)} %collective-permute-done.3.refs_1_, bf16[544,256]{1,0:T(8,128)(2,1)S(1)} %collective-permute-done.4.refs_2_, ...), custom_call_target="tpu_custom_call" | custom-call | flops 1342177280 | bytes 5242880 | tf_op jit(solution)/shard_map/pallas_call | solution.py:410
  34.8 31.5 %all_to_all.22 = bf16[32,64,256]{2,1,0:T(8,128)(2,1)S(1)} all-to-all(bf16[32,64,256]{2,1,0:T(8,128)(2,1)S(1)} %bitcast.8), channel_id=1, replica_groups=mesh['row'=8,'col'=1,'seq'=4] {'row','seq'}, dimensions={0} | all-to-all | bytes 2097152 | tf_op jit(solution)/shard_map/all_to_all | solution.py:539
  66.3 1.1 %shard_map.113 = bf16[1024,256]{1,0:T(8,128)(2,1)} custom-call(bf16[2048,256]{1,0:T(8,128)(2,1)S(1)} %bitcast.6), custom_call_target="tpu_custom_call" | custom-call | flops 134217728 | bytes 1572864 | tf_op jit(solution)/shard_map/pallas_call | solution.py:410
  67.5 3.6 %all-to-all-start.1 = ((bf16[32,32,256]{2,1,0:T(8,128)(2,1)}), bf16[32,32,256]{2,1,0:T(8,128)(2,1)S(1)}, u32[]{:S(2)}, u32[]{:S(2)}) async-start(bf16[32,32,256]{2,1,0:T(8,128)(2,1)} %bitcast.4), calls=%async_computation.1 | async-start | bytes 1048576 | tf_op jit(solution)/shard_map/all_to_all | solution.py:551
  71.1 0.3 shard_map.114.gate_ref
  71.4 15.2 %all-to-all-done.1 = bf16[32,32,256]{2,1,0:T(8,128)(2,1)S(1)} async-done(((bf16[32,32,256]{2,1,0:T(8,128)(2,1)}), bf16[32,32,256]{2,1,0:T(8,128)(2,1)S(1)}, u32[]{:S(2)}, u32[]{:S(2)}) %all-to-all-start.1) | async-done | bytes 524320 | tf_op jit(solution)/shard_map/all_to_all | solution.py:551
  86.6 2.4 %shard_map.115 = bf16[8,256,128]{2,1,0:T(8,128)(2,1)} custom-call(bf16[1024,256]{1,0:T(8,128)(2,1)S(1)} %bitcast.7, bf16[8,128,256]{2,1,0:T(8,128)(2,1)S(1)} %get-tuple-element.75.mid_ref, f32[8,128,256]{2,1,0:T(8,128)S(1)} %shard_map.114.gate_ref, bf16[128,128]{1,0:T(8,128)(2,1)S(1)} %get-tuple-element.78.out_w), custom_call_target="tpu_custom_call" | custom-call | flops 134217728 | bytes 2654208 | tf_op jit(solution)/shard_map/pallas_call | solution.py:410
Async XLA Ops:
  3.5 8.2 %collective-permute-start = (bf16[160,256]{1,0:T(8,128)(2,1)S(1)}, bf16[160,256]{1,0:T(8,128)(2,1)S(1)}, u32[]{:S(2)}, u32[]{:S(2)}) collective-permute-start(bf16[160,256]{1,0:T(8,128)(2,1)S(1)} %get-tuple-element.47), channel_id=1, source_target_pairs={{0,8},{1,9},{2,10},{3,11},{4,12},{5,13},{6,14},{7,15},{8,0},{9,1},... | collective-permute-start | bytes 245768 | tf_op jit(solution)/shard_map/ppermute | solution.py:453
  6.6 9.2 %collective-permute-start.1 = (bf16[160,256]{1,0:T(8,128)(2,1)S(1)}, bf16[160,256]{1,0:T(8,128)(2,1)S(1)}, u32[]{:S(2)}, u32[]{:S(2)}) collective-permute-start(bf16[160,256]{1,0:T(8,128)(2,1)S(1)} %get-tuple-element.48), channel_id=1, source_target_pairs={{0,16},{1,17},{2,18},{3,19},{4,20},{5,21},{6,22},{7,23},{8,24},{9,... | collective-permute-start | bytes 245768 | tf_op jit(solution)/shard_map/ppermute | solution.py:453
  9.2 6.6 %collective-permute-start.2 = (bf16[160,256]{1,0:T(8,128)(2,1)S(1)}, bf16[160,256]{1,0:T(8,128)(2,1)S(1)}, u32[]{:S(2)}, u32[]{:S(2)}) collective-permute-start(bf16[160,256]{1,0:T(8,128)(2,1)S(1)} %get-tuple-element.49), channel_id=1, source_target_pairs={{0,24},{1,25},{2,26},{3,27},{4,28},{5,29},{6,30},{7,31},{8,16},{9,... | collective-permute-start | bytes 245768 | tf_op jit(solution)/shard_map/ppermute | solution.py:453
  16.1 8.9 %collective-permute-start.3 = (bf16[544,256]{1,0:T(8,128)(2,1)S(1)}, bf16[544,256]{1,0:T(8,128)(2,1)S(1)}, u32[]{:S(2)}, u32[]{:S(2)}) collective-permute-start(bf16[544,256]{1,0:T(8,128)(2,1)S(1)} %get-tuple-element.68), channel_id=1, source_target_pairs={{0,2},{1,3},{2,0},{3,1},{4,6},{5,7},{6,4},{7,5},{8,10},{9,11},{10,... | collective-permute-start | bytes 835592 | tf_op jit(solution)/shard_map/ppermute | solution.py:453
  17.6 9.2 %collective-permute-start.4 = (bf16[544,256]{1,0:T(8,128)(2,1)S(1)}, bf16[544,256]{1,0:T(8,128)(2,1)S(1)}, u32[]{:S(2)}, u32[]{:S(2)}) collective-permute-start(bf16[544,256]{1,0:T(8,128)(2,1)S(1)} %get-tuple-element.69), channel_id=1, source_target_pairs={{0,4},{1,5},{2,6},{3,7},{4,0},{5,1},{6,2},{7,3},{8,12},{9,13},{10,... | collective-permute-start | bytes 835592 | tf_op jit(solution)/shard_map/ppermute | solution.py:453
  19.1 10.6 %collective-permute-start.5 = (bf16[544,256]{1,0:T(8,128)(2,1)S(1)}, bf16[544,256]{1,0:T(8,128)(2,1)S(1)}, u32[]{:S(2)}, u32[]{:S(2)}) collective-permute-start(bf16[544,256]{1,0:T(8,128)(2,1)S(1)} %get-tuple-element.70), channel_id=1, source_target_pairs={{0,6},{1,7},{2,4},{3,5},{4,2},{5,3},{6,0},{7,1},{8,14},{9,15},{10,... | collective-permute-start | bytes 835592 | tf_op jit(solution)/shard_map/ppermute | solution.py:453
  19.6 10.1 %collective-permute-start.6 = (bf16[544,256]{1,0:T(8,128)(2,1)S(1)}, bf16[544,256]{1,0:T(8,128)(2,1)S(1)}, u32[]{:S(2)}, u32[]{:S(2)}) collective-permute-start(bf16[544,256]{1,0:T(8,128)(2,1)S(1)} %get-tuple-element.67.refs_0_), channel_id=1, source_target_pairs={{0,1},{1,0},{2,3},{3,2},{4,5},{5,4},{6,7},{7,6},{8,9},{9,8},{10,11... | collective-permute-start | bytes 835592 | tf_op jit(solution)/shard_map/ppermute | solution.py:453
  25.0 4.8 %collective-permute-start.7 = (bf16[544,256]{1,0:T(8,128)(2,1)S(1)}, bf16[544,256]{1,0:T(8,128)(2,1)S(1)}, u32[]{:S(2)}, u32[]{:S(2)}) collective-permute-start(bf16[544,256]{1,0:T(8,128)(2,1)S(1)} %collective-permute-done.3.refs_1_), channel_id=1, source_target_pairs={{0,1},{1,0},{2,3},{3,2},{4,5},{5,4},{6,7},{7,6},{8,9},{9,8},{10,11... | collective-permute-start | bytes 835592 | tf_op jit(solution)/shard_map/ppermute | solution.py:453
  26.8 2.9 %collective-permute-start.8 = (bf16[544,256]{1,0:T(8,128)(2,1)S(1)}, bf16[544,256]{1,0:T(8,128)(2,1)S(1)}, u32[]{:S(2)}, u32[]{:S(2)}) collective-permute-start(bf16[544,256]{1,0:T(8,128)(2,1)S(1)} %collective-permute-done.4.refs_2_), channel_id=1, source_target_pairs={{0,1},{1,0},{2,3},{3,2},{4,5},{5,4},{6,7},{7,6},{8,9},{9,8},{10,11... | collective-permute-start | bytes 835592 | tf_op jit(solution)/shard_map/ppermute | solution.py:453
  29.7 1.6 %collective-permute-start.9 = (bf16[544,256]{1,0:T(8,128)(2,1)S(1)}, bf16[544,256]{1,0:T(8,128)(2,1)S(1)}, u32[]{:S(2)}, u32[]{:S(2)}) collective-permute-start(bf16[544,256]{1,0:T(8,128)(2,1)S(1)} %collective-permute-done.5.refs_3_), channel_id=1, source_target_pairs={{0,1},{1,0},{2,3},{3,2},{4,5},{5,4},{6,7},{7,6},{8,9},{9,8},{10,11... | collective-permute-start | bytes 835592 | tf_op jit(solution)/shard_map/ppermute | solution.py:453
  67.5 19.2 %all-to-all-start.1 = ((bf16[32,32,256]{2,1,0:T(8,128)(2,1)}), bf16[32,32,256]{2,1,0:T(8,128)(2,1)S(1)}, u32[]{:S(2)}, u32[]{:S(2)}) async-start(bf16[32,32,256]{2,1,0:T(8,128)(2,1)} %bitcast.4), calls=%async_computation.1 | async-start | bytes 1048576 | tf_op jit(solution)/shard_map/all_to_all | solution.py:551

commit v3 on v2

--- a/solution.py
+++ b/solution.py
@@ -196,31 +196,34 @@
 
 def factors_kernel(sizes, align_in, left_in, right_in, *refs):
     n_far, n_near, n_core, rows, _ = sizes
-    out_refs, (parts, align_ref, left_ref, right_ref, sems) = refs[:n_far], refs[n_far:]
+    out_refs, (parts, align_ref, left_ref, right_ref, own_lane, picks, sems) = refs[:n_far], refs[n_far:]
     pairs = [(left_in, left_ref), (right_in, right_ref)]
-    pairs += [(align_in.at[n], align_ref.at[n]) for n in range(align_in.shape[0])]
+    pairs += [(align_in, align_ref)]
     copies = fetch(sems, pairs)
-    copies[0].wait()
-    copies[1].wait()
     seqs, cols, width = align_ref.shape
     factor = left_ref.shape[0]
     chip_rows = n_core * rows
-    chips = n_far * n_near
     row, col = iotas(chip_rows * factor, factor)
-    left_wide = mul(ones_where(row % factor == col), left_ref[...]).astype(BF16)
+    widen = ones_where(row % factor == col)
     row, col = iotas(cols, chip_rows * factor)
-    own_lane = (row % chip_rows) == (col // factor)
+    own_lane[...] = ones_where((row % chip_rows) == (col // factor))
     row, col = iotas(n_far * seqs * n_near, cols)
     chip_of_row = (row // (seqs * n_near)) * n_near + row % n_near
+    chip_match = chip_of_row == col // chip_rows
     seq_of_row = (row // n_near) % seqs
-    chip_match = chip_of_row == col // chip_rows
+    for n in range(seqs):
+        picks[n] = ones_where(chip_match & (seq_of_row == n))
+    copies[0].wait()
+    copies[1].wait()
+    left_wide = mul(widen, left_ref[...]).astype(BF16)
     right_rows, left_rows = [], None
     for n in range(seqs):
-        copies[2 + n].wait()
+        if n == 0:
+            copies[2].wait()
         normed = normalize(align_ref[n].astype(F32), 1).astype(BF16)
         right_rows.append(mul_t(right_ref[...], normed))
-        spread = jnp.where(own_lane, mul_t(normed, left_wide), 0.0).astype(BF16)
-        part = mul(ones_where(chip_match & (seq_of_row == n)), spread)
+        spread = mul_t(normed, left_wide).astype(BF16) * own_lane[...]
+        part = mul(picks[n], spread)
         left_rows = part if left_rows is None else left_rows + part
     right_block = jnp.concatenate(right_rows, 0).astype(BF16)
     part_rows = seqs * n_near
@@ -418,6 +421,31 @@
     )(*args)
 
 
+def factors_call(sizes, alignment, opm_left, opm_right):
+    n_far, n_near, n_core, rows, _ = sizes
+    seqs, cols, width = alignment.shape
+    factor = opm_left.shape[1]
+    return call(
+        functools.partial(factors_kernel, sizes),
+        [(seqs * factor + n_core * seqs * n_near, cols)] * n_far,
+        [
+            pltpu.VMEM((n_far, n_core * seqs * n_near, cols), BF16),
+            pltpu.VMEM(alignment.shape, BF16),
+            pltpu.VMEM(opm_left.shape[::-1], BF16),
+            pltpu.VMEM(opm_right.shape[::-1], BF16),
+            pltpu.VMEM((cols, n_core * rows * factor), BF16),
+            pltpu.VMEM((seqs, n_far * seqs * n_near, cols), BF16),
+            pltpu.SemaphoreType.DMA((2 + seqs,)),
+        ],
+        8,
+        4 * seqs * cols * width * factor,
+        alignment,
+        opm_left.T,
+        opm_right.T,
+        far_in=True,
+    )
+
+
 def whole_channels(
     pair,
     alignment,
@@ -452,24 +480,7 @@
         ]
         return lax.ppermute(value, BOTH, pairs)
 
-    message = (seqs * factor + n_core * seqs * n_near, cols)
-    mine = call(
-        functools.partial(factors_kernel, sizes),
-        [message] * n_far,
-        [
-            pltpu.VMEM((n_far, n_core * seqs * n_near, cols), BF16),
-            pltpu.VMEM(alignment.shape, BF16),
-            pltpu.VMEM(opm_left.shape[::-1], BF16),
-            pltpu.VMEM(opm_right.shape[::-1], BF16),
-            pltpu.SemaphoreType.DMA((2 + seqs,)),
-        ],
-        8,
-        4 * seqs * cols * alignment.shape[2] * factor,
-        alignment,
-        opm_left.T,
-        opm_right.T,
-        far_in=True,
-    )
+    mine = factors_call(sizes, alignment, opm_left, opm_right)
     weights = (
         pair,
         opm_out,
@@ -481,7 +492,8 @@
         tri_out,
     )
     mine, weights = lax.optimization_barrier((mine, weights))
-    far = [mine[0]] + [exchange(mine[k], 2 * k, 0) for k in range(1, n_far)]
+    far = [exchange(mine[k], 2 * k, 0) for k in range(n_far - 1, 0, -1)]
+    far = [mine[0]] + far
     prepared = call(
         functools.partial(prepare_kernel, factor),
         [
@@ -508,9 +520,10 @@
         2 * 256 * factor * held * cols,
         *far,
     )
-    near = [mine[0]] + [
-        exchange(mine[k], k // n_y, (k % n_y) * n_core) for k in range(1, n_near)
+    near = [
+        exchange(mine[k], k // n_y, (k % n_y) * n_core) for k in range(n_near - 1, 0, -1)
     ]
+    near = [mine[0]] + near
     groups = near + [exchange(block, 0, 1) for block in near]
     scale = 1.0 / (held * n_near * n_core)
     send, mid, normed = call(

time: 89.3 us -> 87.9 us (0.984)
  blocking collectives: 31.5 us -> 29.7 us
  Pallas kernels: 13.5 us -> 12.5 us
  waiting for transfers between devices: 31 us -> 31.9 us
    all_to_all x1, blocking collectives: 31.5 us -> 29.7 us  [whole_channels(): recv = lax.all_to_all(send, BOTH, split_axis=0, concat_axis=0, tiled=True)]
    pallas_call x7, Pallas kernels: 13.5 us -> 12.5 us  [call(): pl.pallas_call(kernel, out_shape=out_shape, in_specs=[pl.BlockSpec(memory...]
where the time goes in v3:
time: 87.9 us; the launch traced here: 87.6 us
  waiting for transfers between devices  31.9 us (36%)
  blocking collectives  29.7 us (34%)
  starting transfers between devices  13.4 us (15%)
  Pallas kernels  12.5 us (14%)
    all_to_all x1, blocking collectives, whole_channels(): recv = lax.all_to_all(send, BOTH, split_axis=0, concat_axis=0, tiled=True)  29.7 us
    ppermute x10, waiting for transfers between devices, exchange(): return lax.ppermute(value, BOTH, pairs)  16.7 us
    all_to_all x1, waiting for transfers between devices, whole_channels(): recv = lax.all_to_all(send, BOTH, split_axis=0, concat_axis=0, tiled=True)  15.2 us
    pallas_call x7, Pallas kernels, call(): pl.pallas_call(kernel, out_shape=out_shape, in_specs=[pl.BlockSpec(memory...  12.5 us
    ppermute x10, starting transfers between devices, exchange(): return lax.ppermute(value, BOTH, pairs)  9.83 us
    all_to_all x1, starting transfers between devices, whole_channels(): recv = lax.all_to_all(send, BOTH, split_axis=0, concat_axis=0, tiled=True)  3.62 us
  transfers between devices with their start and end apart: 11, of which 6 were waited for; matrix products, arithmetic and copies ran while one was open for 0% of the time, Pallas kernels for 3%

profile of v3, /device:TPU:0, one launch (start us, length us, event | category | flops | bytes accessed | tf_op | source)
XLA Modules:
  0.0 87.6 jit_solution(952082566323015186)
XLA Ops:
  0.0 2.5 %shard_map.109 = (bf16[160,256]{1,0:T(8,128)(2,1)S(1)}, bf16[160,256]{1,0:T(8,128)(2,1)S(1)}, bf16[160,256]{1,0:T(8,128)(2,1)S(1)}, bf16[160,256]{1,0:T(8,128)(2,1)S(1)}) custom-call(bf16[4,256,256]{2,1,0:T(8,128)(2,1)} %align_in.1, bf16[32,256]{1,0:T(8,128)(2,1)} %bitcast.9, bf16[32,256]{1,0:T(8,128)(2,1)} %bitcast.10), custom_call_target="tpu_custom_call" | custom-call | flops 33554432 | bytes 884736 | tf_op jit(solution)/shard_map/pallas_call | solution.py:413
  2.5 5.1 %collective-permute-start = (bf16[160,256]{1,0:T(8,128)(2,1)S(1)}, bf16[160,256]{1,0:T(8,128)(2,1)S(1)}, u32[]{:S(2)}, u32[]{:S(2)}) collective-permute-start(bf16[160,256]{1,0:T(8,128)(2,1)S(1)} %get-tuple-element.47), channel_id=1, source_target_pairs={{0,24},{1,25},{2,26},{3,27},{4,28},{5,29},{6,30},{7,31},{8,16},{9,... | collective-permute-start | bytes 245768 | tf_op jit(solution)/shard_map/ppermute | solution.py:481
  7.6 0.0 collective-permute-start.1
  7.6 0.6 collective-permute-start.2
  8.2 2.5 %shard_map.110 = (bf16[8,128,256]{2,1,0:T(8,128)(2,1)S(1)}, bf16[128,1024]{1,0:T(8,128)(2,1)S(1)}, bf16[512,128]{1,0:T(8,128)(2,1)S(1)}, bf16[128,128]{1,0:T(8,128)(2,1)S(1)}, bf16[128,128]{1,0:T(8,128)(2,1)S(1)}) custom-call(bf16[8,256,128]{2,1,0:T(8,128)(2,1)} %refs_0_, bf16[1024,128]{1,0:T(8,128)(2,1)} %refs_1_, bf16[128,128]{1,0:T(8,128)(2,1)} %refs_2_, ...), custom_call_target="tpu_custom_call" | custom-call | flops 134217728 | bytes 1966080 | tf_op jit(solution)/shard_map/pallas_call | solution.py:413
  10.7 0.0 collective-permute-done.refs_1_
  10.7 3.7 %collective-permute-done.1.refs_2_ = bf16[160,256]{1,0:T(8,128)(2,1)S(1)} collective-permute-done((bf16[160,256]{1,0:T(8,128)(2,1)S(1)}, bf16[160,256]{1,0:T(8,128)(2,1)S(1)}, u32[]{:S(2)}, u32[]{:S(2)}) %collective-permute-start.1) | collective-permute-done | bytes 81952 | tf_op jit(solution)/shard_map/ppermute | solution.py:481
  14.4 0.0 collective-permute-done.2.refs_3_
  14.4 0.3 shard_map.111
  14.7 2.5 %collective-permute-start.3 = (bf16[544,256]{1,0:T(8,128)(2,1)S(1)}, bf16[544,256]{1,0:T(8,128)(2,1)S(1)}, u32[]{:S(2)}, u32[]{:S(2)}) collective-permute-start(bf16[544,256]{1,0:T(8,128)(2,1)S(1)} %get-tuple-element.68), channel_id=1, source_target_pairs={{0,6},{1,7},{2,4},{3,5},{4,2},{5,3},{6,0},{7,1},{8,14},{9,15},{10,... | collective-permute-start | bytes 835592 | tf_op jit(solution)/shard_map/ppermute | solution.py:481
  17.2 0.5 collective-permute-start.4
  17.8 0.5 collective-permute-start.5
  18.3 0.0 collective-permute-start.6
  18.3 7.0 %collective-permute-done.3.refs_1_ = bf16[544,256]{1,0:T(8,128)(2,1)S(1)} collective-permute-done((bf16[544,256]{1,0:T(8,128)(2,1)S(1)}, bf16[544,256]{1,0:T(8,128)(2,1)S(1)}, u32[]{:S(2)}, u32[]{:S(2)}) %collective-permute-start.3) | collective-permute-done | bytes 278560 | tf_op jit(solution)/shard_map/ppermute | solution.py:481
  25.3 0.0 collective-permute-start.7
  25.3 4.4 %collective-permute-done.4.refs_2_ = bf16[544,256]{1,0:T(8,128)(2,1)S(1)} collective-permute-done((bf16[544,256]{1,0:T(8,128)(2,1)S(1)}, bf16[544,256]{1,0:T(8,128)(2,1)S(1)}, u32[]{:S(2)}, u32[]{:S(2)}) %collective-permute-start.4) | collective-permute-done | bytes 278560 | tf_op jit(solution)/shard_map/ppermute | solution.py:481
  29.7 0.0 collective-permute-start.8
  29.7 0.0 collective-permute-done.5.refs_3_
  29.7 0.5 collective-permute-start.9
  30.3 0.0 collective-permute-done.6.refs_4_
  30.3 0.0 collective-permute-done.7.refs_5_
  30.3 1.0 %collective-permute-done.8.refs_6_ = bf16[544,256]{1,0:T(8,128)(2,1)S(1)} collective-permute-done((bf16[544,256]{1,0:T(8,128)(2,1)S(1)}, bf16[544,256]{1,0:T(8,128)(2,1)S(1)}, u32[]{:S(2)}, u32[]{:S(2)}) %collective-permute-start.8) | collective-permute-done | bytes 278560 | tf_op jit(solution)/shard_map/ppermute | solution.py:481
  31.3 0.4 collective-permute-done.9.refs_7_
  31.7 3.5 %shard_map.112 = (bf16[2048,256]{1,0:T(8,128)(2,1)S(1)}, bf16[8,128,256]{2,1,0:T(8,128)(2,1)S(1)}, bf16[8,128,256]{2,1,0:T(8,128)(2,1)S(1)}) custom-call(bf16[544,256]{1,0:T(8,128)(2,1)S(1)} %get-tuple-element.67.refs_0_, bf16[544,256]{1,0:T(8,128)(2,1)S(1)} %collective-permute-done.3.refs_1_, bf16[544,256]{1,0:T(8,128)(2,1)S(1)} %collective-permute-done.4.refs_2_, ...), custom_call_target="tpu_custom_call" | custom-call | flops 1342177280 | bytes 5242880 | tf_op jit(solution)/shard_map/pallas_call | solution.py:413
  35.3 29.7 %all_to_all.22 = bf16[32,64,256]{2,1,0:T(8,128)(2,1)S(1)} all-to-all(bf16[32,64,256]{2,1,0:T(8,128)(2,1)S(1)} %bitcast.8), channel_id=1, replica_groups=mesh['row'=8,'col'=1,'seq'=4] {'row','seq'}, dimensions={0} | all-to-all | bytes 2097152 | tf_op jit(solution)/shard_map/all_to_all | solution.py:552
  64.9 1.1 %shard_map.113 = bf16[1024,256]{1,0:T(8,128)(2,1)} custom-call(bf16[2048,256]{1,0:T(8,128)(2,1)S(1)} %bitcast.6), custom_call_target="tpu_custom_call" | custom-call | flops 134217728 | bytes 1572864 | tf_op jit(solution)/shard_map/pallas_call | solution.py:413
  66.1 3.6 %all-to-all-start.1 = ((bf16[32,32,256]{2,1,0:T(8,128)(2,1)}), bf16[32,32,256]{2,1,0:T(8,128)(2,1)S(1)}, u32[]{:S(2)}, u32[]{:S(2)}) async-start(bf16[32,32,256]{2,1,0:T(8,128)(2,1)} %bitcast.4), calls=%async_computation.1 | async-start | bytes 1048576 | tf_op jit(solution)/shard_map/all_to_all | solution.py:564
  69.7 0.3 shard_map.114.gate_ref
  70.0 15.2 %all-to-all-done.1 = bf16[32,32,256]{2,1,0:T(8,128)(2,1)S(1)} async-done(((bf16[32,32,256]{2,1,0:T(8,128)(2,1)}), bf16[32,32,256]{2,1,0:T(8,128)(2,1)S(1)}, u32[]{:S(2)}, u32[]{:S(2)}) %all-to-all-start.1) | async-done | bytes 524320 | tf_op jit(solution)/shard_map/all_to_all | solution.py:564
  85.2 2.4 %shard_map.115 = bf16[8,256,128]{2,1,0:T(8,128)(2,1)} custom-call(bf16[1024,256]{1,0:T(8,128)(2,1)S(1)} %bitcast.7, bf16[8,128,256]{2,1,0:T(8,128)(2,1)S(1)} %get-tuple-element.75.mid_ref, f32[8,128,256]{2,1,0:T(8,128)S(1)} %shard_map.114.gate_ref, bf16[128,128]{1,0:T(8,128)(2,1)S(1)} %get-tuple-element.78.out_w), custom_call_target="tpu_custom_call" | custom-call | flops 134217728 | bytes 2654208 | tf_op jit(solution)/shard_map/pallas_call | solution.py:413
Async XLA Ops:
  2.5 8.2 %collective-permute-start = (bf16[160,256]{1,0:T(8,128)(2,1)S(1)}, bf16[160,256]{1,0:T(8,128)(2,1)S(1)}, u32[]{:S(2)}, u32[]{:S(2)}) collective-permute-start(bf16[160,256]{1,0:T(8,128)(2,1)S(1)} %get-tuple-element.47), channel_id=1, source_target_pairs={{0,24},{1,25},{2,26},{3,27},{4,28},{5,29},{6,30},{7,31},{8,16},{9,... | collective-permute-start | bytes 245768 | tf_op jit(solution)/shard_map/ppermute | solution.py:481
  7.6 6.9 %collective-permute-start.1 = (bf16[160,256]{1,0:T(8,128)(2,1)S(1)}, bf16[160,256]{1,0:T(8,128)(2,1)S(1)}, u32[]{:S(2)}, u32[]{:S(2)}) collective-permute-start(bf16[160,256]{1,0:T(8,128)(2,1)S(1)} %get-tuple-element.48), channel_id=1, source_target_pairs={{0,16},{1,17},{2,18},{3,19},{4,20},{5,21},{6,22},{7,23},{8,24},{9,... | collective-permute-start | bytes 245768 | tf_op jit(solution)/shard_map/ppermute | solution.py:481
  7.6 6.9 %collective-permute-start.2 = (bf16[160,256]{1,0:T(8,128)(2,1)S(1)}, bf16[160,256]{1,0:T(8,128)(2,1)S(1)}, u32[]{:S(2)}, u32[]{:S(2)}) collective-permute-start(bf16[160,256]{1,0:T(8,128)(2,1)S(1)} %get-tuple-element.49), channel_id=1, source_target_pairs={{0,8},{1,9},{2,10},{3,11},{4,12},{5,13},{6,14},{7,15},{8,0},{9,1},... | collective-permute-start | bytes 245768 | tf_op jit(solution)/shard_map/ppermute | solution.py:481
  14.7 10.6 %collective-permute-start.3 = (bf16[544,256]{1,0:T(8,128)(2,1)S(1)}, bf16[544,256]{1,0:T(8,128)(2,1)S(1)}, u32[]{:S(2)}, u32[]{:S(2)}) collective-permute-start(bf16[544,256]{1,0:T(8,128)(2,1)S(1)} %get-tuple-element.68), channel_id=1, source_target_pairs={{0,6},{1,7},{2,4},{3,5},{4,2},{5,3},{6,0},{7,1},{8,14},{9,15},{10,... | collective-permute-start | bytes 835592 | tf_op jit(solution)/shard_map/ppermute | solution.py:481
  17.2 12.5 %collective-permute-start.4 = (bf16[544,256]{1,0:T(8,128)(2,1)S(1)}, bf16[544,256]{1,0:T(8,128)(2,1)S(1)}, u32[]{:S(2)}, u32[]{:S(2)}) collective-permute-start(bf16[544,256]{1,0:T(8,128)(2,1)S(1)} %get-tuple-element.69), channel_id=1, source_target_pairs={{0,4},{1,5},{2,6},{3,7},{4,0},{5,1},{6,2},{7,3},{8,12},{9,13},{10,... | collective-permute-start | bytes 835592 | tf_op jit(solution)/shard_map/ppermute | solution.py:481
  17.8 12.0 %collective-permute-start.5 = (bf16[544,256]{1,0:T(8,128)(2,1)S(1)}, bf16[544,256]{1,0:T(8,128)(2,1)S(1)}, u32[]{:S(2)}, u32[]{:S(2)}) collective-permute-start(bf16[544,256]{1,0:T(8,128)(2,1)S(1)} %get-tuple-element.70), channel_id=1, source_target_pairs={{0,2},{1,3},{2,0},{3,1},{4,6},{5,7},{6,4},{7,5},{8,10},{9,11},{10,... | collective-permute-start | bytes 835592 | tf_op jit(solution)/shard_map/ppermute | solution.py:481
  18.3 12.0 %collective-permute-start.6 = (bf16[544,256]{1,0:T(8,128)(2,1)S(1)}, bf16[544,256]{1,0:T(8,128)(2,1)S(1)}, u32[]{:S(2)}, u32[]{:S(2)}) collective-permute-start(bf16[544,256]{1,0:T(8,128)(2,1)S(1)} %get-tuple-element.67.refs_0_), channel_id=1, source_target_pairs={{0,1},{1,0},{2,3},{3,2},{4,5},{5,4},{6,7},{7,6},{8,9},{9,8},{10,11... | collective-permute-start | bytes 835592 | tf_op jit(solution)/shard_map/ppermute | solution.py:481
  25.3 5.0 %collective-permute-start.7 = (bf16[544,256]{1,0:T(8,128)(2,1)S(1)}, bf16[544,256]{1,0:T(8,128)(2,1)S(1)}, u32[]{:S(2)}, u32[]{:S(2)}) collective-permute-start(bf16[544,256]{1,0:T(8,128)(2,1)S(1)} %collective-permute-done.3.refs_1_), channel_id=1, source_target_pairs={{0,1},{1,0},{2,3},{3,2},{4,5},{5,4},{6,7},{7,6},{8,9},{9,8},{10,11... | collective-permute-start | bytes 835592 | tf_op jit(solution)/shard_map/ppermute | solution.py:481
  29.7 1.6 %collective-permute-start.8 = (bf16[544,256]{1,0:T(8,128)(2,1)S(1)}, bf16[544,256]{1,0:T(8,128)(2,1)S(1)}, u32[]{:S(2)}, u32[]{:S(2)}) collective-permute-start(bf16[544,256]{1,0:T(8,128)(2,1)S(1)} %collective-permute-done.4.refs_2_), channel_id=1, source_target_pairs={{0,1},{1,0},{2,3},{3,2},{4,5},{5,4},{6,7},{7,6},{8,9},{9,8},{10,11... | collective-permute-start | bytes 835592 | tf_op jit(solution)/shard_map/ppermute | solution.py:481
  29.7 2.0 %collective-permute-start.9 = (bf16[544,256]{1,0:T(8,128)(2,1)S(1)}, bf16[544,256]{1,0:T(8,128)(2,1)S(1)}, u32[]{:S(2)}, u32[]{:S(2)}) collective-permute-start(bf16[544,256]{1,0:T(8,128)(2,1)S(1)} %collective-permute-done.5.refs_3_), channel_id=1, source_target_pairs={{0,1},{1,0},{2,3},{3,2},{4,5},{5,4},{6,7},{7,6},{8,9},{9,8},{10,11... | collective-permute-start | bytes 835592 | tf_op jit(solution)/shard_map/ppermute | solution.py:481
  66.1 19.2 %all-to-all-start.1 = ((bf16[32,32,256]{2,1,0:T(8,128)(2,1)}), bf16[32,32,256]{2,1,0:T(8,128)(2,1)S(1)}, u32[]{:S(2)}, u32[]{:S(2)}) async-start(bf16[32,32,256]{2,1,0:T(8,128)(2,1)} %bitcast.4), calls=%async_computation.1 | async-start | bytes 1048576 | tf_op jit(solution)/shard_map/all_to_all | solution.py:564

commit v4 on v3

--- a/solution.py
+++ b/solution.py
@@ -328,17 +328,19 @@
             for p in range(0, factor, 16):
                 at = (q // 16 * (factor // 16) + p // 16) * 256 + q % 16 * 16
                 outer[i, at : at + 16, :] = block[i * factor + p : i * factor + p + 16]
+    updates = [mul(out_w[...], outer[i]) for i in range(rows)]
     for i in range(rows):
-        update = mul(out_w[...], outer[i])
+        update = updates[i]
         mid = (pair_ref[i].astype(F32) + update * scale).astype(BF16)
         mid_ref[i] = mid
         normed = normalize(mid.astype(F32), 0).astype(BF16)
         norm_ref[i] = normed
+    for i in range(rows):
+        parts = mul(tri_w[...], norm_ref[i])
         for side in range(2):
             at = 2 * side * hidden
-            gate = jax.nn.sigmoid(mul(tri_w[at : at + hidden, :], normed))
-            value = mul(tri_w[at + hidden : at + 2 * hidden, :], normed)
-            both[side, i] = (gate * value).astype(BF16)
+            gate = jax.nn.sigmoid(parts[at : at + hidden])
+            both[side, i] = (gate * parts[at + hidden : at + 2 * hidden]).astype(BF16)
     per = hidden // n_dev
     some = 256 // rows
     shuffle = swap_rows(rows, some)
@@ -393,10 +395,10 @@
             apart[i, b * some : (b + 1) * some, :] = normed[i * some : (i + 1) * some]
     eye = identity(cols)
     copies = []
+    updates = [mul(out_w[...], apart[i]) for i in range(rows)]
+    dones = [(mid_ref[i].astype(F32) + gate_ref[i] * updates[i]).astype(BF16) for i in range(rows)]
     for i in range(rows):
-        update = mul(out_w[...], apart[i])
-        done = (mid_ref[i].astype(F32) + gate_ref[i] * update).astype(BF16)
-        done_ref[i] = mul_t(eye, done).astype(BF16)
+        done_ref[i] = mul_t(eye, dones[i]).astype(BF16)
         copies.append(pltpu.make_async_copy(done_ref.at[i], out_ref.at[i], sems.at[i]))
         copies[i].start()
     for copy in copies:

time: 87.9 us -> 86.9 us (0.989)
  Pallas kernels: 12.5 us -> 11.5 us
    pallas_call x7, Pallas kernels: 12.5 us -> 11.5 us  [call(): pl.pallas_call(kernel, out_shape=out_shape, in_specs=[pl.BlockSpec(memory...]
where the time goes in v4:
time: 86.9 us; the launch traced here: 86.6 us
  waiting for transfers between devices  31.9 us (37%)
  blocking collectives  29.7 us (34%)
  starting transfers between devices  13.4 us (15%)
  Pallas kernels  11.5 us (13%)
    all_to_all x1, blocking collectives, whole_channels(): recv = lax.all_to_all(send, BOTH, split_axis=0, concat_axis=0, tiled=True)  29.7 us
    ppermute x10, waiting for transfers between devices, exchange(): return lax.ppermute(value, BOTH, pairs)  16.7 us
    all_to_all x1, waiting for transfers between devices, whole_channels(): recv = lax.all_to_all(send, BOTH, split_axis=0, concat_axis=0, tiled=True)  15.2 us
    pallas_call x7, Pallas kernels, call(): pl.pallas_call(kernel, out_shape=out_shape, in_specs=[pl.BlockSpec(memory...  11.5 us
    ppermute x10, starting transfers between devices, exchange(): return lax.ppermute(value, BOTH, pairs)  9.83 us
    all_to_all x1, starting transfers between devices, whole_channels(): recv = lax.all_to_all(send, BOTH, split_axis=0, concat_axis=0, tiled=True)  3.62 us
  transfers between devices with their start and end apart: 11, of which 6 were waited for; matrix products, arithmetic and copies ran while one was open for 0% of the time, Pallas kernels for 3%

profile of v4, /device:TPU:0, one launch (start us, length us, event | category | flops | bytes accessed | tf_op | source)
XLA Modules:
  0.0 86.6 jit_solution(1938731538180968294)
XLA Ops:
  0.0 2.5 %shard_map.109 = (bf16[160,256]{1,0:T(8,128)(2,1)S(1)}, bf16[160,256]{1,0:T(8,128)(2,1)S(1)}, bf16[160,256]{1,0:T(8,128)(2,1)S(1)}, bf16[160,256]{1,0:T(8,128)(2,1)S(1)}) custom-call(bf16[4,256,256]{2,1,0:T(8,128)(2,1)} %align_in.1, bf16[32,256]{1,0:T(8,128)(2,1)} %bitcast.9, bf16[32,256]{1,0:T(8,128)(2,1)} %bitcast.10), custom_call_target="tpu_custom_call" | custom-call | flops 33554432 | bytes 884736 | tf_op jit(solution)/shard_map/pallas_call | solution.py:415
  2.5 5.1 %collective-permute-start = (bf16[160,256]{1,0:T(8,128)(2,1)S(1)}, bf16[160,256]{1,0:T(8,128)(2,1)S(1)}, u32[]{:S(2)}, u32[]{:S(2)}) collective-permute-start(bf16[160,256]{1,0:T(8,128)(2,1)S(1)} %get-tuple-element.47), channel_id=1, source_target_pairs={{0,24},{1,25},{2,26},{3,27},{4,28},{5,29},{6,30},{7,31},{8,16},{9,... | collective-permute-start | bytes 245768 | tf_op jit(solution)/shard_map/ppermute | solution.py:483
  7.6 0.0 collective-permute-start.1
  7.6 0.6 collective-permute-start.2
  8.2 2.5 %shard_map.110 = (bf16[8,128,256]{2,1,0:T(8,128)(2,1)S(1)}, bf16[128,1024]{1,0:T(8,128)(2,1)S(1)}, bf16[512,128]{1,0:T(8,128)(2,1)S(1)}, bf16[128,128]{1,0:T(8,128)(2,1)S(1)}, bf16[128,128]{1,0:T(8,128)(2,1)S(1)}) custom-call(bf16[8,256,128]{2,1,0:T(8,128)(2,1)} %refs_0_, bf16[1024,128]{1,0:T(8,128)(2,1)} %refs_1_, bf16[128,128]{1,0:T(8,128)(2,1)} %refs_2_, ...), custom_call_target="tpu_custom_call" | custom-call | flops 134217728 | bytes 1966080 | tf_op jit(solution)/shard_map/pallas_call | solution.py:415
  10.7 0.0 collective-permute-done.refs_1_
  10.7 3.7 %collective-permute-done.1.refs_2_ = bf16[160,256]{1,0:T(8,128)(2,1)S(1)} collective-permute-done((bf16[160,256]{1,0:T(8,128)(2,1)S(1)}, bf16[160,256]{1,0:T(8,128)(2,1)S(1)}, u32[]{:S(2)}, u32[]{:S(2)}) %collective-permute-start.1) | collective-permute-done | bytes 81952 | tf_op jit(solution)/shard_map/ppermute | solution.py:483
  14.4 0.0 collective-permute-done.2.refs_3_
  14.4 0.3 shard_map.111
  14.7 2.5 %collective-permute-start.3 = (bf16[544,256]{1,0:T(8,128)(2,1)S(1)}, bf16[544,256]{1,0:T(8,128)(2,1)S(1)}, u32[]{:S(2)}, u32[]{:S(2)}) collective-permute-start(bf16[544,256]{1,0:T(8,128)(2,1)S(1)} %get-tuple-element.68), channel_id=1, source_target_pairs={{0,6},{1,7},{2,4},{3,5},{4,2},{5,3},{6,0},{7,1},{8,14},{9,15},{10,... | collective-permute-start | bytes 835592 | tf_op jit(solution)/shard_map/ppermute | solution.py:483
  17.2 0.5 collective-permute-start.4
  17.8 0.5 collective-permute-start.5
  18.3 0.0 collective-permute-start.6
  18.3 7.0 %collective-permute-done.3.refs_1_ = bf16[544,256]{1,0:T(8,128)(2,1)S(1)} collective-permute-done((bf16[544,256]{1,0:T(8,128)(2,1)S(1)}, bf16[544,256]{1,0:T(8,128)(2,1)S(1)}, u32[]{:S(2)}, u32[]{:S(2)}) %collective-permute-start.3) | collective-permute-done | bytes 278560 | tf_op jit(solution)/shard_map/ppermute | solution.py:483
  25.3 0.0 collective-permute-start.7
  25.3 4.4 %collective-permute-done.4.refs_2_ = bf16[544,256]{1,0:T(8,128)(2,1)S(1)} collective-permute-done((bf16[544,256]{1,0:T(8,128)(2,1)S(1)}, bf16[544,256]{1,0:T(8,128)(2,1)S(1)}, u32[]{:S(2)}, u32[]{:S(2)}) %collective-permute-start.4) | collective-permute-done | bytes 278560 | tf_op jit(solution)/shard_map/ppermute | solution.py:483
  29.7 0.0 collective-permute-start.8
  29.7 0.0 collective-permute-done.5.refs_3_
  29.7 0.5 collective-permute-start.9
  30.3 0.0 collective-permute-done.6.refs_4_
  30.3 0.0 collective-permute-done.7.refs_5_
  30.3 1.0 %collective-permute-done.8.refs_6_ = bf16[544,256]{1,0:T(8,128)(2,1)S(1)} collective-permute-done((bf16[544,256]{1,0:T(8,128)(2,1)S(1)}, bf16[544,256]{1,0:T(8,128)(2,1)S(1)}, u32[]{:S(2)}, u32[]{:S(2)}) %collective-permute-start.8) | collective-permute-done | bytes 278560 | tf_op jit(solution)/shard_map/ppermute | solution.py:483
  31.3 0.4 collective-permute-done.9.refs_7_
  31.7 3.0 %shard_map.112 = (bf16[2048,256]{1,0:T(8,128)(2,1)S(1)}, bf16[8,128,256]{2,1,0:T(8,128)(2,1)S(1)}, bf16[8,128,256]{2,1,0:T(8,128)(2,1)S(1)}) custom-call(bf16[544,256]{1,0:T(8,128)(2,1)S(1)} %get-tuple-element.67.refs_0_, bf16[544,256]{1,0:T(8,128)(2,1)S(1)} %collective-permute-done.3.refs_1_, bf16[544,256]{1,0:T(8,128)(2,1)S(1)} %collective-permute-done.4.refs_2_, ...), custom_call_target="tpu_custom_call" | custom-call | flops 1342177280 | bytes 5242880 | tf_op jit(solution)/shard_map/pallas_call | solution.py:415
  34.7 29.7 %all_to_all.22 = bf16[32,64,256]{2,1,0:T(8,128)(2,1)S(1)} all-to-all(bf16[32,64,256]{2,1,0:T(8,128)(2,1)S(1)} %bitcast.8), channel_id=1, replica_groups=mesh['row'=8,'col'=1,'seq'=4] {'row','seq'}, dimensions={0} | all-to-all | bytes 2097152 | tf_op jit(solution)/shard_map/all_to_all | solution.py:554
  64.4 1.1 %shard_map.113 = bf16[1024,256]{1,0:T(8,128)(2,1)} custom-call(bf16[2048,256]{1,0:T(8,128)(2,1)S(1)} %bitcast.6), custom_call_target="tpu_custom_call" | custom-call | flops 134217728 | bytes 1572864 | tf_op jit(solution)/shard_map/pallas_call | solution.py:415
  65.5 3.6 %all-to-all-start.1 = ((bf16[32,32,256]{2,1,0:T(8,128)(2,1)}), bf16[32,32,256]{2,1,0:T(8,128)(2,1)S(1)}, u32[]{:S(2)}, u32[]{:S(2)}) async-start(bf16[32,32,256]{2,1,0:T(8,128)(2,1)} %bitcast.4), calls=%async_computation.1 | async-start | bytes 1048576 | tf_op jit(solution)/shard_map/all_to_all | solution.py:566
  69.2 0.3 shard_map.114.gate_ref
  69.5 15.2 %all-to-all-done.1 = bf16[32,32,256]{2,1,0:T(8,128)(2,1)S(1)} async-done(((bf16[32,32,256]{2,1,0:T(8,128)(2,1)}), bf16[32,32,256]{2,1,0:T(8,128)(2,1)S(1)}, u32[]{:S(2)}, u32[]{:S(2)}) %all-to-all-start.1) | async-done | bytes 524320 | tf_op jit(solution)/shard_map/all_to_all | solution.py:566
  84.7 1.9 %shard_map.115 = bf16[8,256,128]{2,1,0:T(8,128)(2,1)} custom-call(bf16[1024,256]{1,0:T(8,128)(2,1)S(1)} %bitcast.7, bf16[8,128,256]{2,1,0:T(8,128)(2,1)S(1)} %get-tuple-element.75.mid_ref, f32[8,128,256]{2,1,0:T(8,128)S(1)} %shard_map.114.gate_ref, bf16[128,128]{1,0:T(8,128)(2,1)S(1)} %get-tuple-element.78.out_w), custom_call_target="tpu_custom_call" | custom-call | flops 134217728 | bytes 2654208 | tf_op jit(solution)/shard_map/pallas_call | solution.py:415
Async XLA Ops:
  2.5 8.2 %collective-permute-start = (bf16[160,256]{1,0:T(8,128)(2,1)S(1)}, bf16[160,256]{1,0:T(8,128)(2,1)S(1)}, u32[]{:S(2)}, u32[]{:S(2)}) collective-permute-start(bf16[160,256]{1,0:T(8,128)(2,1)S(1)} %get-tuple-element.47), channel_id=1, source_target_pairs={{0,24},{1,25},{2,26},{3,27},{4,28},{5,29},{6,30},{7,31},{8,16},{9,... | collective-permute-start | bytes 245768 | tf_op jit(solution)/shard_map/ppermute | solution.py:483
  7.6 6.9 %collective-permute-start.1 = (bf16[160,256]{1,0:T(8,128)(2,1)S(1)}, bf16[160,256]{1,0:T(8,128)(2,1)S(1)}, u32[]{:S(2)}, u32[]{:S(2)}) collective-permute-start(bf16[160,256]{1,0:T(8,128)(2,1)S(1)} %get-tuple-element.48), channel_id=1, source_target_pairs={{0,16},{1,17},{2,18},{3,19},{4,20},{5,21},{6,22},{7,23},{8,24},{9,... | collective-permute-start | bytes 245768 | tf_op jit(solution)/shard_map/ppermute | solution.py:483
  7.6 6.9 %collective-permute-start.2 = (bf16[160,256]{1,0:T(8,128)(2,1)S(1)}, bf16[160,256]{1,0:T(8,128)(2,1)S(1)}, u32[]{:S(2)}, u32[]{:S(2)}) collective-permute-start(bf16[160,256]{1,0:T(8,128)(2,1)S(1)} %get-tuple-element.49), channel_id=1, source_target_pairs={{0,8},{1,9},{2,10},{3,11},{4,12},{5,13},{6,14},{7,15},{8,0},{9,1},... | collective-permute-start | bytes 245768 | tf_op jit(solution)/shard_map/ppermute | solution.py:483
  14.7 10.6 %collective-permute-start.3 = (bf16[544,256]{1,0:T(8,128)(2,1)S(1)}, bf16[544,256]{1,0:T(8,128)(2,1)S(1)}, u32[]{:S(2)}, u32[]{:S(2)}) collective-permute-start(bf16[544,256]{1,0:T(8,128)(2,1)S(1)} %get-tuple-element.68), channel_id=1, source_target_pairs={{0,6},{1,7},{2,4},{3,5},{4,2},{5,3},{6,0},{7,1},{8,14},{9,15},{10,... | collective-permute-start | bytes 835592 | tf_op jit(solution)/shard_map/ppermute | solution.py:483
  17.2 12.5 %collective-permute-start.4 = (bf16[544,256]{1,0:T(8,128)(2,1)S(1)}, bf16[544,256]{1,0:T(8,128)(2,1)S(1)}, u32[]{:S(2)}, u32[]{:S(2)}) collective-permute-start(bf16[544,256]{1,0:T(8,128)(2,1)S(1)} %get-tuple-element.69), channel_id=1, source_target_pairs={{0,4},{1,5},{2,6},{3,7},{4,0},{5,1},{6,2},{7,3},{8,12},{9,13},{10,... | collective-permute-start | bytes 835592 | tf_op jit(solution)/shard_map/ppermute | solution.py:483
  17.8 12.0 %collective-permute-start.5 = (bf16[544,256]{1,0:T(8,128)(2,1)S(1)}, bf16[544,256]{1,0:T(8,128)(2,1)S(1)}, u32[]{:S(2)}, u32[]{:S(2)}) collective-permute-start(bf16[544,256]{1,0:T(8,128)(2,1)S(1)} %get-tuple-element.70), channel_id=1, source_target_pairs={{0,2},{1,3},{2,0},{3,1},{4,6},{5,7},{6,4},{7,5},{8,10},{9,11},{10,... | collective-permute-start | bytes 835592 | tf_op jit(solution)/shard_map/ppermute | solution.py:483
  18.3 12.0 %collective-permute-start.6 = (bf16[544,256]{1,0:T(8,128)(2,1)S(1)}, bf16[544,256]{1,0:T(8,128)(2,1)S(1)}, u32[]{:S(2)}, u32[]{:S(2)}) collective-permute-start(bf16[544,256]{1,0:T(8,128)(2,1)S(1)} %get-tuple-element.67.refs_0_), channel_id=1, source_target_pairs={{0,1},{1,0},{2,3},{3,2},{4,5},{5,4},{6,7},{7,6},{8,9},{9,8},{10,11... | collective-permute-start | bytes 835592 | tf_op jit(solution)/shard_map/ppermute | solution.py:483
  25.3 5.0 %collective-permute-start.7 = (bf16[544,256]{1,0:T(8,128)(2,1)S(1)}, bf16[544,256]{1,0:T(8,128)(2,1)S(1)}, u32[]{:S(2)}, u32[]{:S(2)}) collective-permute-start(bf16[544,256]{1,0:T(8,128)(2,1)S(1)} %collective-permute-done.3.refs_1_), channel_id=1, source_target_pairs={{0,1},{1,0},{2,3},{3,2},{4,5},{5,4},{6,7},{7,6},{8,9},{9,8},{10,11... | collective-permute-start | bytes 835592 | tf_op jit(solution)/shard_map/ppermute | solution.py:483
  29.7 1.6 %collective-permute-start.8 = (bf16[544,256]{1,0:T(8,128)(2,1)S(1)}, bf16[544,256]{1,0:T(8,128)(2,1)S(1)}, u32[]{:S(2)}, u32[]{:S(2)}) collective-permute-start(bf16[544,256]{1,0:T(8,128)(2,1)S(1)} %collective-permute-done.4.refs_2_), channel_id=1, source_target_pairs={{0,1},{1,0},{2,3},{3,2},{4,5},{5,4},{6,7},{7,6},{8,9},{9,8},{10,11... | collective-permute-start | bytes 835592 | tf_op jit(solution)/shard_map/ppermute | solution.py:483
  29.7 2.0 %collective-permute-start.9 = (bf16[544,256]{1,0:T(8,128)(2,1)S(1)}, bf16[544,256]{1,0:T(8,128)(2,1)S(1)}, u32[]{:S(2)}, u32[]{:S(2)}) collective-permute-start(bf16[544,256]{1,0:T(8,128)(2,1)S(1)} %collective-permute-done.5.refs_3_), channel_id=1, source_target_pairs={{0,1},{1,0},{2,3},{3,2},{4,5},{5,4},{6,7},{7,6},{8,9},{9,8},{10,11... | collective-permute-start | bytes 835592 | tf_op jit(solution)/shard_map/ppermute | solution.py:483
  65.5 19.2 %all-to-all-start.1 = ((bf16[32,32,256]{2,1,0:T(8,128)(2,1)}), bf16[32,32,256]{2,1,0:T(8,128)(2,1)S(1)}, u32[]{:S(2)}, u32[]{:S(2)}) async-start(bf16[32,32,256]{2,1,0:T(8,128)(2,1)} %bitcast.4), calls=%async_computation.1 | async-start | bytes 1048576 | tf_op jit(solution)/shard_map/all_to_all | solution.py:566

commit v5 on v4

--- a/solution.py
+++ b/solution.py
@@ -239,17 +239,19 @@
         out_refs[k][seqs * factor :, :] = parts[here ^ k]
 
 
-def regroup_kernel(sizes, factor, seqs, *refs):
-    n_far, n_near, n_core, _, _ = sizes
-    in_refs, out_refs, parts = refs[:n_far], refs[n_far : n_far + n_near], refs[-1]
-    held = n_far * seqs
+def near_index(n_near, n_core):
+    return (lax.axis_index("row") % 2) * (n_near // 2) + lax.axis_index("seq") // n_core
+
+
+def regroup(sizes, factor, seqs, blocks, out_refs):
+    held = sizes[0] * seqs
     half = 256 // held
     shuffle = swap_rows(held, half)
     for h in range(factor // half):
         block = jnp.concatenate(
             [
-                ref[n * factor + h * half : n * factor + (h + 1) * half, :]
-                for ref in in_refs
+                ref[at + n * factor + h * half : at + n * factor + (h + 1) * half, :]
+                for ref, at in blocks
                 for n in range(seqs)
             ],
             0,
@@ -257,22 +259,44 @@
         block = mul(shuffle, block).astype(BF16)
         for ref in out_refs:
             ref[h * half * held : (h + 1) * half * held, :] = block
-    part_rows = seqs * n_near
-    base = seqs * factor
+
+
+def regroup_kernel(sizes, factor, seqs, *refs):
+    n_far, n_near, n_core, _, _ = sizes
+    in_refs, out_refs, parts = refs[:n_far], refs[n_far : n_far + n_near], refs[-1]
+    held, part_rows, base = n_far * seqs, seqs * n_near, seqs * factor
+    regroup(sizes, factor, seqs, [(ref, 0) for ref in in_refs], out_refs[:-1])
+    for far in range(1, n_far):
+        out_refs[-1][(far - 1) * base : far * base, :] = in_refs[far][:base, :]
     pick = swap_rows(held, n_near)
+    row, _ = iotas(held * n_near, held * n_near)
+    pick_late = jnp.where(row % held < seqs, 0.0, pick.astype(F32)).astype(BF16)
     for piece in range(n_core):
         block = jnp.concatenate(
             [ref[base + piece * part_rows : base + (piece + 1) * part_rows, :] for ref in in_refs], 0
         )
-        block = mul(pick, block).astype(BF16)
-        for near in range(n_near):
-            parts[near, piece * held : (piece + 1) * held, :] = block[
-                near * held : (near + 1) * held
-            ]
-    n_y = n_near // 2
-    here = (lax.axis_index("row") % 2) * n_y + lax.axis_index("seq") // n_core
-    for k in range(n_near):
-        out_refs[k][factor * held :, :] = parts[here ^ k]
+        for late, matrix in enumerate((pick, pick_late)):
+            rows = mul(matrix, block).astype(BF16)
+            for near in range(n_near):
+                parts[late, near, piece * held : (piece + 1) * held, :] = rows[
+                    near * held : (near + 1) * held
+                ]
+    here = near_index(n_near, n_core)
+    for k in range(n_near - 1):
+        out_refs[k][factor * held :, :] = parts[0, here ^ k]
+    out_refs[-1][(n_far - 1) * base :, :] = parts[1, here ^ (n_near - 1)]
+
+
+def merge_kernel(sizes, factor, seqs, early_ref, late_ref, out_ref):
+    n_far, n_near, n_core, _, _ = sizes
+    held, part_rows, base = n_far * seqs, seqs * n_near, seqs * factor
+    blocks = [(early_ref, 0)] + [(late_ref, far * base) for far in range(n_far - 1)]
+    regroup(sizes, factor, seqs, blocks, [out_ref])
+    row, col = iotas(n_core * held, n_core * part_rows)
+    slot = row // held * part_rows + row % held * n_near + near_index(n_near, n_core)
+    pick = ones_where((row % held < seqs) & (col == slot))
+    own = mul(pick, early_ref[base:, :])
+    out_ref[factor * held :, :] = (own + late_ref[(n_far - 1) * base :, :].astype(F32)).astype(BF16)
 
 
 def prepare_kernel(factor, *refs):
@@ -494,7 +518,11 @@
         tri_out,
     )
     mine, weights = lax.optimization_barrier((mine, weights))
+    def to_near(value, k):
+        return exchange(value, k // n_y, (k % n_y) * n_core)
+
     far = [exchange(mine[k], 2 * k, 0) for k in range(n_far - 1, 0, -1)]
+    early = to_near(mine[0], n_near - 1)
     far = [mine[0]] + far
     prepared = call(
         functools.partial(prepare_kernel, factor),
@@ -511,20 +539,28 @@
         *weights,
         far_in=True,
     )
-    far, prepared = lax.optimization_barrier((far, prepared))
+    far, early, prepared = lax.optimization_barrier((far, early, prepared))
     pair_t, out_t, tri_t, gate_t, final_t = prepared
     message = ((factor + n_core) * held, cols)
+    late = ((n_far - 1) * seqs * factor + n_core * held, cols)
     mine = call(
         functools.partial(regroup_kernel, sizes, factor, seqs),
-        [message] * n_near,
-        [pltpu.VMEM((n_near, n_core * held, cols), BF16)],
+        [message] * (n_near - 1) + [late],
+        [pltpu.VMEM((2, n_near, n_core * held, cols), BF16)],
         8,
         2 * 256 * factor * held * cols,
         *far,
     )
-    near = [
-        exchange(mine[k], k // n_y, (k % n_y) * n_core) for k in range(n_near - 1, 0, -1)
-    ]
+    near = [to_near(mine[k], k) for k in range(n_near - 1, 0, -1)]
+    (near[0],) = call(
+        functools.partial(merge_kernel, sizes, factor, seqs),
+        [message],
+        [],
+        8,
+        2 * 256 * factor * held * cols,
+        early,
+        near[0],
+    )
     near = [mine[0]] + near
     groups = near + [exchange(block, 0, 1) for block in near]
     scale = 1.0 / (held * n_near * n_core)

time: 86.9 us -> 85.8 us (0.987)
  waiting for transfers between devices: 31.9 us -> 28.3 us
  starting transfers between devices: 13.4 us -> 16.2 us
    ppermute x10 -> x11, waiting for transfers between devices: 16.7 us -> 13.1 us  [exchange(): return lax.ppermute(value, BOTH, pairs)]
    ppermute x10 -> x11, starting transfers between devices: 9.83 us -> 12.6 us  [exchange(): return lax.ppermute(value, BOTH, pairs)]
    pallas_call x7 -> x8, Pallas kernels: 11.5 us -> 11.7 us  [call(): pl.pallas_call(kernel, out_shape=out_shape, in_specs=[pl.BlockSpec(memory...]
  transfers between devices with their start and end apart: 11 -> 12, of which waited for: 6 -> 6; matrix products, arithmetic and copies ran while one was open for 0% -> 0% of each run, Pallas kernels for 3% -> 3%
where the time goes in v5:
time: 85.8 us; the launch traced here: 85.5 us
  blocking collectives  29.2 us (34%)
  waiting for transfers between devices  28.3 us (33%)
  starting transfers between devices  16.2 us (19%)
  Pallas kernels  11.7 us (14%)
    all_to_all x1, blocking collectives, whole_channels(): recv = lax.all_to_all(send, BOTH, split_axis=0, concat_axis=0, tiled=True)  29.2 us
    all_to_all x1, waiting for transfers between devices, whole_channels(): recv = lax.all_to_all(send, BOTH, split_axis=0, concat_axis=0, tiled=True)  15.2 us
    ppermute x11, waiting for transfers between devices, exchange(): return lax.ppermute(value, BOTH, pairs)  13.1 us
    ppermute x11, starting transfers between devices, exchange(): return lax.ppermute(value, BOTH, pairs)  12.6 us
    pallas_call x8, Pallas kernels, call(): pl.pallas_call(kernel, out_shape=out_shape, in_specs=[pl.BlockSpec(memory...  11.7 us
    all_to_all x1, starting transfers between devices, whole_channels(): recv = lax.all_to_all(send, BOTH, split_axis=0, concat_axis=0, tiled=True)  3.62 us
  transfers between devices with their start and end apart: 12, of which 6 were waited for; matrix products, arithmetic and copies ran while one was open for 0% of the time, Pallas kernels for 3%

profile of v5, /device:TPU:0, one launch (start us, length us, event | category | flops | bytes accessed | tf_op | source)
XLA Modules:
  0.0 85.5 jit_solution(4781127868712924160)
XLA Ops:
  0.0 2.5 %shard_map.109 = (bf16[160,256]{1,0:T(8,128)(2,1)S(1)}, bf16[160,256]{1,0:T(8,128)(2,1)S(1)}, bf16[160,256]{1,0:T(8,128)(2,1)S(1)}, bf16[160,256]{1,0:T(8,128)(2,1)S(1)}) custom-call(bf16[4,256,256]{2,1,0:T(8,128)(2,1)} %align_in.1, bf16[32,256]{1,0:T(8,128)(2,1)} %bitcast.9, bf16[32,256]{1,0:T(8,128)(2,1)} %bitcast.10), custom_call_target="tpu_custom_call" | custom-call | flops 33554432 | bytes 884736 | tf_op jit(solution)/shard_map/pallas_call | solution.py:439
  2.5 5.1 %collective-permute-start = (bf16[160,256]{1,0:T(8,128)(2,1)S(1)}, bf16[160,256]{1,0:T(8,128)(2,1)S(1)}, u32[]{:S(2)}, u32[]{:S(2)}) collective-permute-start(bf16[160,256]{1,0:T(8,128)(2,1)S(1)} %get-tuple-element.48), channel_id=1, source_target_pairs={{0,24},{1,25},{2,26},{3,27},{4,28},{5,29},{6,30},{7,31},{8,16},{9,... | collective-permute-start | bytes 245768 | tf_op jit(solution)/shard_map/ppermute | solution.py:507
  7.6 0.0 collective-permute-start.1
  7.6 0.6 collective-permute-start.2
  8.2 2.6 %collective-permute-start.3 = (bf16[160,256]{1,0:T(8,128)(2,1)S(1)}, bf16[160,256]{1,0:T(8,128)(2,1)S(1)}, u32[]{:S(2)}, u32[]{:S(2)}) collective-permute-start(bf16[160,256]{1,0:T(8,128)(2,1)S(1)} %get-tuple-element.64.refs_0_), channel_id=1, source_target_pairs={{0,6},{1,7},{2,4},{3,5},{4,2},{5,3},{6,0},{7,1},{8,14},{9,15},{10,... | collective-permute-start | bytes 245768 | tf_op jit(solution)/shard_map/ppermute | solution.py:507
  10.8 2.5 %shard_map.110 = (bf16[8,128,256]{2,1,0:T(8,128)(2,1)S(1)}, bf16[128,1024]{1,0:T(8,128)(2,1)S(1)}, bf16[512,128]{1,0:T(8,128)(2,1)S(1)}, bf16[128,128]{1,0:T(8,128)(2,1)S(1)}, bf16[128,128]{1,0:T(8,128)(2,1)S(1)}) custom-call(bf16[8,256,128]{2,1,0:T(8,128)(2,1)} %refs_0_, bf16[1024,128]{1,0:T(8,128)(2,1)} %refs_1_, bf16[128,128]{1,0:T(8,128)(2,1)} %refs_2_, ...), custom_call_target="tpu_custom_call" | custom-call | flops 134217728 | bytes 1966080 | tf_op jit(solution)/shard_map/pallas_call | solution.py:439
  13.3 0.0 collective-permute-done.refs_1_
  13.3 1.2 %collective-permute-done.1.refs_2_ = bf16[160,256]{1,0:T(8,128)(2,1)S(1)} collective-permute-done((bf16[160,256]{1,0:T(8,128)(2,1)S(1)}, bf16[160,256]{1,0:T(8,128)(2,1)S(1)}, u32[]{:S(2)}, u32[]{:S(2)}) %collective-permute-start.1) | collective-permute-done | bytes 81952 | tf_op jit(solution)/shard_map/ppermute | solution.py:507
  14.4 0.0 collective-permute-done.2.refs_3_
  14.4 0.0 collective-permute-done.3.early_ref
  14.4 0.3 shard_map.111
  14.7 1.6 %collective-permute-start.5 = (bf16[544,256]{1,0:T(8,128)(2,1)S(1)}, bf16[544,256]{1,0:T(8,128)(2,1)S(1)}, u32[]{:S(2)}, u32[]{:S(2)}) collective-permute-start(bf16[544,256]{1,0:T(8,128)(2,1)S(1)} %get-tuple-element.71), channel_id=1, source_target_pairs={{0,4},{1,5},{2,6},{3,7},{4,0},{5,1},{6,2},{7,3},{8,12},{9,13},{10,... | collective-permute-start | bytes 835592 | tf_op jit(solution)/shard_map/ppermute | solution.py:507
  16.3 1.5 %collective-permute-start.6 = (bf16[544,256]{1,0:T(8,128)(2,1)S(1)}, bf16[544,256]{1,0:T(8,128)(2,1)S(1)}, u32[]{:S(2)}, u32[]{:S(2)}) collective-permute-start(bf16[544,256]{1,0:T(8,128)(2,1)S(1)} %get-tuple-element.72), channel_id=1, source_target_pairs={{0,2},{1,3},{2,0},{3,1},{4,6},{5,7},{6,4},{7,5},{8,10},{9,11},{10,... | collective-permute-start | bytes 835592 | tf_op jit(solution)/shard_map/ppermute | solution.py:507
  17.8 0.5 collective-permute-start.4
  18.3 0.0 collective-permute-start.7
  18.3 10.1 %collective-permute-done.4.late_ref = bf16[416,256]{1,0:T(8,128)(2,1)S(1)} collective-permute-done((bf16[416,256]{1,0:T(8,128)(2,1)S(1)}, bf16[416,256]{1,0:T(8,128)(2,1)S(1)}, u32[]{:S(2)}, u32[]{:S(2)}) %collective-permute-start.4) | collective-permute-done | bytes 213024 | tf_op jit(solution)/shard_map/ppermute | solution.py:507
  28.4 0.2 shard_map.112.refs_1_
  28.7 0.1 collective-permute-start.8
  28.7 0.0 collective-permute-done.5.refs_2_
  28.8 0.5 collective-permute-start.9
  29.2 0.1 collective-permute-start.10
  29.3 0.0 collective-permute-done.7.refs_4_
  29.3 1.0 %collective-permute-done.8.refs_5_ = bf16[544,256]{1,0:T(8,128)(2,1)S(1)} collective-permute-done((bf16[544,256]{1,0:T(8,128)(2,1)S(1)}, bf16[544,256]{1,0:T(8,128)(2,1)S(1)}, u32[]{:S(2)}, u32[]{:S(2)}) %collective-permute-start.8) | collective-permute-done | bytes 278560 | tf_op jit(solution)/shard_map/ppermute | solution.py:507
  30.3 0.4 collective-permute-done.9.refs_6_
  30.7 0.4 collective-permute-done.10.refs_7_
  31.1 3.0 %shard_map.113 = (bf16[2048,256]{1,0:T(8,128)(2,1)S(1)}, bf16[8,128,256]{2,1,0:T(8,128)(2,1)S(1)}, bf16[8,128,256]{2,1,0:T(8,128)(2,1)S(1)}) custom-call(bf16[544,256]{1,0:T(8,128)(2,1)S(1)} %get-tuple-element.68.refs_0_, bf16[544,256]{1,0:T(8,128)(2,1)S(1)} %shard_map.112.refs_1_, bf16[544,256]{1,0:T(8,128)(2,1)S(1)} %collective-permute-done.5.refs_2_, ...), custom_call_target="tpu_custom_call" | custom-call | flops 1342177280 | bytes 5242880 | tf_op jit(solution)/shard_map/pallas_call | solution.py:439
  34.1 29.2 %all_to_all.22 = bf16[32,64,256]{2,1,0:T(8,128)(2,1)S(1)} all-to-all(bf16[32,64,256]{2,1,0:T(8,128)(2,1)S(1)} %bitcast.8), channel_id=1, replica_groups=mesh['row'=8,'col'=1,'seq'=4] {'row','seq'}, dimensions={0} | all-to-all | bytes 2097152 | tf_op jit(solution)/shard_map/all_to_all | solution.py:590
  63.3 1.1 %shard_map.114 = bf16[1024,256]{1,0:T(8,128)(2,1)} custom-call(bf16[2048,256]{1,0:T(8,128)(2,1)S(1)} %bitcast.6), custom_call_target="tpu_custom_call" | custom-call | flops 134217728 | bytes 1572864 | tf_op jit(solution)/shard_map/pallas_call | solution.py:439
  64.4 3.6 %all-to-all-start.1 = ((bf16[32,32,256]{2,1,0:T(8,128)(2,1)}), bf16[32,32,256]{2,1,0:T(8,128)(2,1)S(1)}, u32[]{:S(2)}, u32[]{:S(2)}) async-start(bf16[32,32,256]{2,1,0:T(8,128)(2,1)} %bitcast.4), calls=%async_computation.1 | async-start | bytes 1048576 | tf_op jit(solution)/shard_map/all_to_all | solution.py:602
  68.0 0.3 shard_map.115.gate_ref
  68.3 15.2 %all-to-all-done.1 = bf16[32,32,256]{2,1,0:T(8,128)(2,1)S(1)} async-done(((bf16[32,32,256]{2,1,0:T(8,128)(2,1)}), bf16[32,32,256]{2,1,0:T(8,128)(2,1)S(1)}, u32[]{:S(2)}, u32[]{:S(2)}) %all-to-all-start.1) | async-done | bytes 524320 | tf_op jit(solution)/shard_map/all_to_all | solution.py:602
  83.6 1.9 %shard_map.116 = bf16[8,256,128]{2,1,0:T(8,128)(2,1)} custom-call(bf16[1024,256]{1,0:T(8,128)(2,1)S(1)} %bitcast.7, bf16[8,128,256]{2,1,0:T(8,128)(2,1)S(1)} %get-tuple-element.77.mid_ref, f32[8,128,256]{2,1,0:T(8,128)S(1)} %shard_map.115.gate_ref, bf16[128,128]{1,0:T(8,128)(2,1)S(1)} %get-tuple-element.80.out_w), custom_call_target="tpu_custom_call" | custom-call | flops 134217728 | bytes 2654208 | tf_op jit(solution)/shard_map/pallas_call | solution.py:439
  (1 shorter events, 0.0 us)
Async XLA Ops:
  2.5 10.8 %collective-permute-start = (bf16[160,256]{1,0:T(8,128)(2,1)S(1)}, bf16[160,256]{1,0:T(8,128)(2,1)S(1)}, u32[]{:S(2)}, u32[]{:S(2)}) collective-permute-start(bf16[160,256]{1,0:T(8,128)(2,1)S(1)} %get-tuple-element.48), channel_id=1, source_target_pairs={{0,24},{1,25},{2,26},{3,27},{4,28},{5,29},{6,30},{7,31},{8,16},{9,... | collective-permute-start | bytes 245768 | tf_op jit(solution)/shard_map/ppermute | solution.py:507
  7.6 6.9 %collective-permute-start.1 = (bf16[160,256]{1,0:T(8,128)(2,1)S(1)}, bf16[160,256]{1,0:T(8,128)(2,1)S(1)}, u32[]{:S(2)}, u32[]{:S(2)}) collective-permute-start(bf16[160,256]{1,0:T(8,128)(2,1)S(1)} %get-tuple-element.49), channel_id=1, source_target_pairs={{0,16},{1,17},{2,18},{3,19},{4,20},{5,21},{6,22},{7,23},{8,24},{9,... | collective-permute-start | bytes 245768 | tf_op jit(solution)/shard_map/ppermute | solution.py:507
  7.6 6.9 %collective-permute-start.2 = (bf16[160,256]{1,0:T(8,128)(2,1)S(1)}, bf16[160,256]{1,0:T(8,128)(2,1)S(1)}, u32[]{:S(2)}, u32[]{:S(2)}) collective-permute-start(bf16[160,256]{1,0:T(8,128)(2,1)S(1)} %get-tuple-element.50), channel_id=1, source_target_pairs={{0,8},{1,9},{2,10},{3,11},{4,12},{5,13},{6,14},{7,15},{8,0},{9,1},... | collective-permute-start | bytes 245768 | tf_op jit(solution)/shard_map/ppermute | solution.py:507
  8.2 6.2 %collective-permute-start.3 = (bf16[160,256]{1,0:T(8,128)(2,1)S(1)}, bf16[160,256]{1,0:T(8,128)(2,1)S(1)}, u32[]{:S(2)}, u32[]{:S(2)}) collective-permute-start(bf16[160,256]{1,0:T(8,128)(2,1)S(1)} %get-tuple-element.64.refs_0_), channel_id=1, source_target_pairs={{0,6},{1,7},{2,4},{3,5},{4,2},{5,3},{6,0},{7,1},{8,14},{9,15},{10,... | collective-permute-start | bytes 245768 | tf_op jit(solution)/shard_map/ppermute | solution.py:507
  14.7 14.0 %collective-permute-start.5 = (bf16[544,256]{1,0:T(8,128)(2,1)S(1)}, bf16[544,256]{1,0:T(8,128)(2,1)S(1)}, u32[]{:S(2)}, u32[]{:S(2)}) collective-permute-start(bf16[544,256]{1,0:T(8,128)(2,1)S(1)} %get-tuple-element.71), channel_id=1, source_target_pairs={{0,4},{1,5},{2,6},{3,7},{4,0},{5,1},{6,2},{7,3},{8,12},{9,13},{10,... | collective-permute-start | bytes 835592 | tf_op jit(solution)/shard_map/ppermute | solution.py:507
  16.3 13.0 %collective-permute-start.6 = (bf16[544,256]{1,0:T(8,128)(2,1)S(1)}, bf16[544,256]{1,0:T(8,128)(2,1)S(1)}, u32[]{:S(2)}, u32[]{:S(2)}) collective-permute-start(bf16[544,256]{1,0:T(8,128)(2,1)S(1)} %get-tuple-element.72), channel_id=1, source_target_pairs={{0,2},{1,3},{2,0},{3,1},{4,6},{5,7},{6,4},{7,5},{8,10},{9,11},{10,... | collective-permute-start | bytes 835592 | tf_op jit(solution)/shard_map/ppermute | solution.py:507
  17.8 10.6 %collective-permute-start.4 = (bf16[416,256]{1,0:T(8,128)(2,1)S(1)}, bf16[416,256]{1,0:T(8,128)(2,1)S(1)}, u32[]{:S(2)}, u32[]{:S(2)}) collective-permute-start(bf16[416,256]{1,0:T(8,128)(2,1)S(1)} %get-tuple-element.70), channel_id=1, source_target_pairs={{0,6},{1,7},{2,4},{3,5},{4,2},{5,3},{6,0},{7,1},{8,14},{9,15},{10,... | collective-permute-start | bytes 638984 | tf_op jit(solution)/shard_map/ppermute | solution.py:507
  18.3 11.1 %collective-permute-start.7 = (bf16[544,256]{1,0:T(8,128)(2,1)S(1)}, bf16[544,256]{1,0:T(8,128)(2,1)S(1)}, u32[]{:S(2)}, u32[]{:S(2)}) collective-permute-start(bf16[544,256]{1,0:T(8,128)(2,1)S(1)} %get-tuple-element.68.refs_0_), channel_id=1, source_target_pairs={{0,1},{1,0},{2,3},{3,2},{4,5},{5,4},{6,7},{7,6},{8,9},{9,8},{10,11... | collective-permute-start | bytes 835592 | tf_op jit(solution)/shard_map/ppermute | solution.py:507
  28.7 1.6 %collective-permute-start.8 = (bf16[544,256]{1,0:T(8,128)(2,1)S(1)}, bf16[544,256]{1,0:T(8,128)(2,1)S(1)}, u32[]{:S(2)}, u32[]{:S(2)}) collective-permute-start(bf16[544,256]{1,0:T(8,128)(2,1)S(1)} %shard_map.112.refs_1_), channel_id=1, source_target_pairs={{0,1},{1,0},{2,3},{3,2},{4,5},{5,4},{6,7},{7,6},{8,9},{9,8},{10,11... | collective-permute-start | bytes 835592 | tf_op jit(solution)/shard_map/ppermute | solution.py:507
  28.8 1.9 %collective-permute-start.9 = (bf16[544,256]{1,0:T(8,128)(2,1)S(1)}, bf16[544,256]{1,0:T(8,128)(2,1)S(1)}, u32[]{:S(2)}, u32[]{:S(2)}) collective-permute-start(bf16[544,256]{1,0:T(8,128)(2,1)S(1)} %collective-permute-done.5.refs_2_), channel_id=1, source_target_pairs={{0,1},{1,0},{2,3},{3,2},{4,5},{5,4},{6,7},{7,6},{8,9},{9,8},{10,11... | collective-permute-start | bytes 835592 | tf_op jit(solution)/shard_map/ppermute | solution.py:507
  29.2 1.8 %collective-permute-start.10 = (bf16[544,256]{1,0:T(8,128)(2,1)S(1)}, bf16[544,256]{1,0:T(8,128)(2,1)S(1)}, u32[]{:S(2)}, u32[]{:S(2)}) collective-permute-start(bf16[544,256]{1,0:T(8,128)(2,1)S(1)} %collective-permute-done.6.refs_3_), channel_id=1, source_target_pairs={{0,1},{1,0},{2,3},{3,2},{4,5},{5,4},{6,7},{7,6},{8,9},{9,8},{10,11... | collective-permute-start | bytes 835592 | tf_op jit(solution)/shard_map/ppermute | solution.py:507
  64.4 19.2 %all-to-all-start.1 = ((bf16[32,32,256]{2,1,0:T(8,128)(2,1)}), bf16[32,32,256]{2,1,0:T(8,128)(2,1)S(1)}, u32[]{:S(2)}, u32[]{:S(2)}) async-start(bf16[32,32,256]{2,1,0:T(8,128)(2,1)} %bitcast.4), calls=%async_computation.1 | async-start | bytes 1048576 | tf_op jit(solution)/shard_map/all_to_all | solution.py:602

commit v6 on v5

--- a/solution.py
+++ b/solution.py
@@ -337,8 +337,8 @@
 
 def pair_kernel(sizes, held, scale, *refs):
     n_core, rows, n_dev = sizes[2], sizes[3], sizes[4]
-    groups = refs[:-8]
-    pair_ref, out_w, tri_w, send_ref, mid_ref, norm_ref, outer, both = refs[-8:]
+    groups = refs[:-10]
+    pair_ref, out_w, tri_w, send_ref, own_ref, other_ref, mid_ref, norm_ref, outer, both = refs[-10:]
     factor = groups[0].shape[0] // held - n_core
     hidden = tri_w.shape[0] // 4
     core = lax.axis_index("seq") % n_core
@@ -365,35 +365,74 @@
             at = 2 * side * hidden
             gate = jax.nn.sigmoid(parts[at : at + hidden])
             both[side, i] = (gate * parts[at + hidden : at + 2 * hidden]).astype(BF16)
-    per = hidden // n_dev
+    half = n_dev // 2
+    chunk = hidden // half * rows
     some = 256 // rows
     shuffle = swap_rows(rows, some)
-    chunk = per * rows
-    for side in range(2):
-        for b in range(hidden // some):
-            block = jnp.concatenate(
-                [both[side, i, b * some : (b + 1) * some, :] for i in range(rows)], 0
-            )
-            block = mul(shuffle, block).astype(BF16)
-            for d in range(some // per):
-                to = ((b * some // per + d) * 2 + side) * chunk
-                send_ref[to : to + chunk, :] = block[d * chunk : (d + 1) * chunk]
-
-
-def product_kernel(sizes, per, recv_ref, send_ref, factors, total):
-    rows, n_dev = sizes[3], sizes[4]
-    chunk = per * rows
+    per = some * rows // chunk
+    for b in range(hidden // some):
+        left, right = (
+            mul(
+                shuffle,
+                jnp.concatenate(
+                    [both[side, i, b * some : (b + 1) * some, :] for i in range(rows)], 0
+                ),
+            ).astype(BF16)
+            for side in range(2)
+        )
+        for d in range(per):
+            for side in range(2):
+                to = (side * half + b * per + d) * chunk
+                send_ref[to : to + chunk, :] = right[d * chunk : (d + 1) * chunk]
+        for d in range(0, per, n_core):
+            to = (b * per + d) // n_core * chunk
+            even = left[d * chunk : (d + 1) * chunk]
+            odd = left[(d + 1) * chunk : (d + 2) * chunk]
+            own_ref[to : to + chunk, :] = jnp.where(core == 0, even, odd)
+            other_ref[to : to + chunk, :] = jnp.where(core == 0, odd, even)
+
+
+def half_index(sizes):
+    n_far, n_near, n_core, _, _ = sizes
+    n_y = n_near // 2
+    row = lax.axis_index("row") % n_far
+    return row * n_y + lax.axis_index("seq") // n_core
+
+
+def left_kernel(sizes, own_ref, came_ref, *out_refs):
+    n_core = sizes[2]
+    chunk = own_ref.shape[0] // len(out_refs)
+    core = lax.axis_index("seq") % n_core
+    here = half_index(sizes)
+    own_at = pl.multiple_of(core * chunk, chunk)
+    came_at = pl.multiple_of((1 - core) * chunk, chunk)
+    for k, ref in enumerate(out_refs):
+        at = pl.multiple_of((here ^ k) * chunk, chunk)
+        ref[pl.ds(own_at, chunk), :] = own_ref[pl.ds(at, chunk), :]
+        ref[pl.ds(came_at, chunk), :] = came_ref[pl.ds(at, chunk), :]
+
+
+def product_kernel(sizes, per, recv_ref, *refs):
+    n_core, rows, n_dev = sizes[2], sizes[3], sizes[4]
+    half, chunk = n_dev // 2, per * rows
+    chips = half // n_core
+    left_refs, (send_ref, left, right, total) = refs[:chips], refs[chips:]
+    here = half_index(sizes)
     for src in range(n_dev):
-        for side in range(2):
-            at = (src * 2 + side) * chunk
-            block = recv_ref[at : at + chunk, :].astype(F32)
+        block = recv_ref[src * chunk : (src + 1) * chunk, :].astype(F32)
+        for c in range(per):
+            right[c, src * rows : (src + 1) * rows, :] = block[c * rows : (c + 1) * rows]
+    for k, ref in enumerate(left_refs):
+        for core in range(n_core):
+            block = ref[core * chunk : (core + 1) * chunk, :].astype(F32)
+            at = pl.multiple_of(((here ^ k) * n_core + core) * rows, rows)
             for c in range(per):
-                factors[side, c, src * rows : (src + 1) * rows, :] = block[c * rows : (c + 1) * rows]
+                left[c, pl.ds(at, rows), :] = block[c * rows : (c + 1) * rows]
     for c in range(per):
-        prod = mul_t(factors[0, c].astype(BF16), factors[1, c].astype(BF16))
-        for dst in range(n_dev):
+        prod = mul_t(left[c].astype(BF16), right[c].astype(BF16))
+        for dst in range(half):
             total[dst, c * rows : (c + 1) * rows, :] = prod[dst * rows : (dst + 1) * rows]
-    for dst in range(n_dev):
+    for dst in range(half):
         send_ref[dst * chunk : (dst + 1) * chunk, :] = total[dst].astype(BF16)
 
 
@@ -496,7 +535,9 @@
     n_y = n_near // 2
     sizes = (n_far, n_near, n_core, rows, n_dev)
     held = n_far * seqs
-    per = hidden // n_dev
+    half = n_dev // 2
+    per = hidden // half
+    chips = half // n_core
 
     def exchange(value, row_bits, seq_bits):
         pairs = [
@@ -564,9 +605,15 @@
     near = [mine[0]] + near
     groups = near + [exchange(block, 0, 1) for block in near]
     scale = 1.0 / (held * n_near * n_core)
-    send, mid, normed = call(
+    send, own, other, mid, normed = call(
         functools.partial(pair_kernel, sizes, held, scale),
-        [(2 * hidden * rows, cols), (rows, width, cols), (rows, width, cols)],
+        [
+            (2 * hidden * rows, cols),
+            (chips * per * rows, cols),
+            (chips * per * rows, cols),
+            (rows, width, cols),
+            (rows, width, cols),
+        ],
         [
             pltpu.VMEM((rows, factor * factor, cols), BF16),
             pltpu.VMEM((2, rows, hidden, cols), BF16),
@@ -588,18 +635,35 @@
         gate_t,
     )
     recv = lax.all_to_all(send, BOTH, split_axis=0, concat_axis=0, tiled=True)
+    mine = call(
+        functools.partial(left_kernel, sizes),
+        [(n_core * per * rows, cols)] * chips,
+        [],
+        8,
+        0,
+        own,
+        exchange(other, 0, 1),
+    )
+    lefts = [mine[0]]
+    for k in range(1, chips):
+        lefts.append(exchange(mine[k], k // n_y, k % n_y * n_core))
     (send,) = call(
         functools.partial(product_kernel, sizes, per),
         [(hidden * rows, cols)],
         [
-            pltpu.VMEM((2, per, rows * n_dev, cols), F32),
-            pltpu.VMEM((n_dev, per * rows, cols), F32),
+            pltpu.VMEM((per, rows * half, cols), F32),
+            pltpu.VMEM((per, rows * n_dev, cols), F32),
+            pltpu.VMEM((half, per * rows, cols), F32),
         ],
         16,
-        2 * per * cols * cols * cols,
+        2 * per * cols * cols * cols // 2,
         recv,
-    )
-    recv = lax.all_to_all(send, BOTH, split_axis=0, concat_axis=0, tiled=True)
+        *lefts,
+    )
+    halves = [list(range(half)), list(range(half, n_dev))]
+    recv = lax.all_to_all(
+        send, BOTH, split_axis=0, concat_axis=0, tiled=True, axis_index_groups=halves
+    )
     (out,) = call(
         functools.partial(finish_kernel, sizes),
         [(rows, cols, width)],

time: 85.8 us -> 82.5 us (0.962)
  blocking collectives: 29.2 us -> 0 us
  starting transfers between devices: 16.2 us -> 32.5 us
  waiting for transfers between devices: 28.3 us -> 36.5 us
  Pallas kernels: 11.7 us -> 13 us
    all_to_all x1 -> x0, blocking collectives: 29.2 us -> none  [whole_channels(): recv = lax.all_to_all(send, BOTH, split_axis=0, concat_axis=0, tiled=True)]
    all_to_all x1, waiting for transfers between devices: 15.2 us -> 0.26 us  [whole_channels(): recv = lax.all_to_all(send, BOTH, split_axis=0, concat_axis=0, tiled=True)]
    ppermute x11 -> x19, waiting for transfers between devices: 13.1 us -> 26 us  [exchange(): return lax.ppermute(value, BOTH, pairs)]
    ppermute x11 -> x19, starting transfers between devices: 12.6 us -> 25.5 us  [exchange(): return lax.ppermute(value, BOTH, pairs)]
    all_to_all x0 -> x1, waiting for transfers between devices: none -> 10.2 us  [whole_channels(): lax.all_to_all(send, BOTH, split_axis=0, concat_axis=0, tiled=True, axis_...]
    all_to_all x0 -> x1, starting transfers between devices: none -> 3.91 us  [whole_channels(): lax.all_to_all(send, BOTH, split_axis=0, concat_axis=0, tiled=True, axis_...]
    pallas_call x8 -> x9, Pallas kernels: 11.7 us -> 13 us  [call(): pl.pallas_call(kernel, out_shape=out_shape, in_specs=[pl.BlockSpec(memory...]
  transfers between devices with their start and end apart: 12 -> 21, of which waited for: 6 -> 13; matrix products, arithmetic and copies ran while one was open for 0% -> 0% of each run, Pallas kernels for 3% -> 4%
where the time goes in v6:
time: 82.5 us; the launch traced here: 82.2 us
  waiting for transfers between devices  36.5 us (44%)
  starting transfers between devices  32.5 us (39%)
  Pallas kernels  13 us (16%)
    ppermute x19, waiting for transfers between devices, exchange(): return lax.ppermute(value, BOTH, pairs)  26 us
    ppermute x19, starting transfers between devices, exchange(): return lax.ppermute(value, BOTH, pairs)  25.5 us
    pallas_call x9, Pallas kernels, call(): pl.pallas_call(kernel, out_shape=out_shape, in_specs=[pl.BlockSpec(memory...  13 us
    all_to_all x1, waiting for transfers between devices, whole_channels(): lax.all_to_all(send, BOTH, split_axis=0, concat_axis=0, tiled=True, axis_...  10.2 us
    all_to_all x1, starting transfers between devices, whole_channels(): lax.all_to_all(send, BOTH, split_axis=0, concat_axis=0, tiled=True, axis_...  3.91 us
    all_to_all x1, starting transfers between devices, whole_channels(): recv = lax.all_to_all(send, BOTH, split_axis=0, concat_axis=0, tiled=True)  3.11 us
  transfers between devices with their start and end apart: 21, of which 13 were waited for; matrix products, arithmetic and copies ran while one was open for 0% of the time, Pallas kernels for 4%

profile of v6, /device:TPU:0, one launch (start us, length us, event | category | flops | bytes accessed | tf_op | source)
XLA Modules:
  0.0 82.2 jit_solution(2604581935687376089)
XLA Ops:
  0.0 2.5 %shard_map.109 = (bf16[160,256]{1,0:T(8,128)(2,1)S(1)}, bf16[160,256]{1,0:T(8,128)(2,1)S(1)}, bf16[160,256]{1,0:T(8,128)(2,1)S(1)}, bf16[160,256]{1,0:T(8,128)(2,1)S(1)}) custom-call(bf16[4,256,256]{2,1,0:T(8,128)(2,1)} %align_in.1, bf16[32,256]{1,0:T(8,128)(2,1)} %bitcast.8, bf16[32,256]{1,0:T(8,128)(2,1)} %bitcast.9), custom_call_target="tpu_custom_call" | custom-call | flops 33554432 | bytes 884736 | tf_op jit(solution)/shard_map/pallas_call | solution.py:478
  2.5 5.1 %collective-permute-start = (bf16[160,256]{1,0:T(8,128)(2,1)S(1)}, bf16[160,256]{1,0:T(8,128)(2,1)S(1)}, u32[]{:S(2)}, u32[]{:S(2)}) collective-permute-start(bf16[160,256]{1,0:T(8,128)(2,1)S(1)} %get-tuple-element.58), channel_id=1, source_target_pairs={{0,24},{1,25},{2,26},{3,27},{4,28},{5,29},{6,30},{7,31},{8,16},{9,... | collective-permute-start | bytes 245768 | tf_op jit(solution)/shard_map/ppermute | solution.py:548
  7.6 0.6 collective-permute-start.2
  8.2 2.6 %collective-permute-start.3 = (bf16[160,256]{1,0:T(8,128)(2,1)S(1)}, bf16[160,256]{1,0:T(8,128)(2,1)S(1)}, u32[]{:S(2)}, u32[]{:S(2)}) collective-permute-start(bf16[160,256]{1,0:T(8,128)(2,1)S(1)} %get-tuple-element.74.refs_0_), channel_id=1, source_target_pairs={{0,6},{1,7},{2,4},{3,5},{4,2},{5,3},{6,0},{7,1},{8,14},{9,15},{10,... | collective-permute-start | bytes 245768 | tf_op jit(solution)/shard_map/ppermute | solution.py:548
  10.8 2.5 %shard_map.110 = (bf16[8,128,256]{2,1,0:T(8,128)(2,1)S(1)}, bf16[128,1024]{1,0:T(8,128)(2,1)S(1)}, bf16[512,128]{1,0:T(8,128)(2,1)S(1)}, bf16[128,128]{1,0:T(8,128)(2,1)S(1)}, bf16[128,128]{1,0:T(8,128)(2,1)S(1)}) custom-call(bf16[8,256,128]{2,1,0:T(8,128)(2,1)} %refs_0_, bf16[1024,128]{1,0:T(8,128)(2,1)} %refs_1_, bf16[128,128]{1,0:T(8,128)(2,1)} %refs_2_, ...), custom_call_target="tpu_custom_call" | custom-call | flops 134217728 | bytes 1966080 | tf_op jit(solution)/shard_map/pallas_call | solution.py:478
  13.3 1.2 %collective-permute-done.1.refs_2_ = bf16[160,256]{1,0:T(8,128)(2,1)S(1)} collective-permute-done((bf16[160,256]{1,0:T(8,128)(2,1)S(1)}, bf16[160,256]{1,0:T(8,128)(2,1)S(1)}, u32[]{:S(2)}, u32[]{:S(2)}) %collective-permute-start.1) | collective-permute-done | bytes 81952 | tf_op jit(solution)/shard_map/ppermute | solution.py:548
  14.7 1.6 %collective-permute-start.5 = (bf16[544,256]{1,0:T(8,128)(2,1)S(1)}, bf16[544,256]{1,0:T(8,128)(2,1)S(1)}, u32[]{:S(2)}, u32[]{:S(2)}) collective-permute-start(bf16[544,256]{1,0:T(8,128)(2,1)S(1)} %get-tuple-element.81), channel_id=1, source_target_pairs={{0,4},{1,5},{2,6},{3,7},{4,0},{5,1},{6,2},{7,3},{8,12},{9,13},{10,... | collective-permute-start | bytes 835592 | tf_op jit(solution)/shard_map/ppermute | solution.py:548
  16.3 1.5 %collective-permute-start.6 = (bf16[544,256]{1,0:T(8,128)(2,1)S(1)}, bf16[544,256]{1,0:T(8,128)(2,1)S(1)}, u32[]{:S(2)}, u32[]{:S(2)}) collective-permute-start(bf16[544,256]{1,0:T(8,128)(2,1)S(1)} %get-tuple-element.82), channel_id=1, source_target_pairs={{0,2},{1,3},{2,0},{3,1},{4,6},{5,7},{6,4},{7,5},{8,10},{9,11},{10,... | collective-permute-start | bytes 835592 | tf_op jit(solution)/shard_map/ppermute | solution.py:548
  17.8 0.5 collective-permute-start.4
  18.3 10.1 %collective-permute-done.4.late_ref = bf16[416,256]{1,0:T(8,128)(2,1)S(1)} collective-permute-done((bf16[416,256]{1,0:T(8,128)(2,1)S(1)}, bf16[416,256]{1,0:T(8,128)(2,1)S(1)}, u32[]{:S(2)}, u32[]{:S(2)}) %collective-permute-start.4) | collective-permute-done | bytes 213024 | tf_op jit(solution)/shard_map/ppermute | solution.py:548
  28.8 0.5 collective-permute-start.9
  29.3 1.0 %collective-permute-done.8.refs_5_ = bf16[544,256]{1,0:T(8,128)(2,1)S(1)} collective-permute-done((bf16[544,256]{1,0:T(8,128)(2,1)S(1)}, bf16[544,256]{1,0:T(8,128)(2,1)S(1)}, u32[]{:S(2)}, u32[]{:S(2)}) %collective-permute-start.8) | collective-permute-done | bytes 278560 | tf_op jit(solution)/shard_map/ppermute | solution.py:548
  30.3 0.4 collective-permute-done.9.refs_6_
  30.7 0.4 collective-permute-done.10.refs_7_
  31.1 4.1 %shard_map.113 = (bf16[2048,256]{1,0:T(8,128)(2,1)}, bf16[512,256]{1,0:T(8,128)(2,1)S(1)}, bf16[512,256]{1,0:T(8,128)(2,1)S(1)}, bf16[8,128,256]{2,1,0:T(8,128)(2,1)S(1)}, bf16[8,128,256]{2,1,0:T(8,128)(2,1)S(1)}) custom-call(bf16[544,256]{1,0:T(8,128)(2,1)S(1)} %get-tuple-element.78.refs_0_, bf16[544,256]{1,0:T(8,128)(2,1)S(1)} %shard_map.112.refs_1_, ...), custom_call_target="tpu_custom_call" | custom-call | flops 1342177280 | bytes 5767168 | tf_op jit(solution)/shard_map/pallas_call | solution.py:478
  35.2 3.1 %all-to-all-start = ((bf16[32,64,256]{2,1,0:T(8,128)(2,1)}), bf16[32,64,256]{2,1,0:T(8,128)(2,1)S(1)}, u32[]{:S(2)}, u32[]{:S(2)}) async-start(bf16[32,64,256]{2,1,0:T(8,128)(2,1)} %bitcast.2), calls=%async_computation | async-start | bytes 2097152 | tf_op jit(solution)/shard_map/all_to_all | solution.py:637
  38.6 1.3 %collective-permute-done.11.came_ref = bf16[512,256]{1,0:T(8,128)(2,1)S(1)} collective-permute-done((bf16[512,256]{1,0:T(8,128)(2,1)S(1)}, bf16[512,256]{1,0:T(8,128)(2,1)S(1)}, u32[]{:S(2)}, u32[]{:S(2)}) %collective-permute-start.11) | collective-permute-done | bytes 262176 | tf_op jit(solution)/shard_map/ppermute | solution.py:548
  39.9 1.8 %collective-permute-start.12 = (bf16[128,256]{1,0:T(8,128)(2,1)S(1)}, bf16[128,256]{1,0:T(8,128)(2,1)S(1)}, u32[]{:S(2)}, u32[]{:S(2)}) collective-permute-start(bf16[128,256]{1,0:T(8,128)(2,1)S(1)} %get-tuple-element.90), channel_id=1, source_target_pairs={{0,2},{1,3},{2,0},{3,1},{4,6},{5,7},{6,4},{7,5},{8,10},{9,11},{10,... | collective-permute-start | bytes 196616 | tf_op jit(solution)/shard_map/ppermute | solution.py:548
  41.8 1.5 %collective-permute-start.13 = (bf16[128,256]{1,0:T(8,128)(2,1)S(1)}, bf16[128,256]{1,0:T(8,128)(2,1)S(1)}, u32[]{:S(2)}, u32[]{:S(2)}) collective-permute-start(bf16[128,256]{1,0:T(8,128)(2,1)S(1)} %get-tuple-element.91), channel_id=1, source_target_pairs={{0,4},{1,5},{2,6},{3,7},{4,0},{5,1},{6,2},{7,3},{8,12},{9,13},{10,... | collective-permute-start | bytes 196616 | tf_op jit(solution)/shard_map/ppermute | solution.py:548
  43.5 1.8 %collective-permute-start.15 = (bf16[128,256]{1,0:T(8,128)(2,1)S(1)}, bf16[128,256]{1,0:T(8,128)(2,1)S(1)}, u32[]{:S(2)}, u32[]{:S(2)}) collective-permute-start(bf16[128,256]{1,0:T(8,128)(2,1)S(1)} %get-tuple-element.93), channel_id=1, source_target_pairs={{0,8},{1,9},{2,10},{3,11},{4,12},{5,13},{6,14},{7,15},{8,0},{9,1},... | collective-permute-start | bytes 196616 | tf_op jit(solution)/shard_map/ppermute | solution.py:548
  45.2 1.5 %collective-permute-start.16 = (bf16[128,256]{1,0:T(8,128)(2,1)S(1)}, bf16[128,256]{1,0:T(8,128)(2,1)S(1)}, u32[]{:S(2)}, u32[]{:S(2)}) collective-permute-start(bf16[128,256]{1,0:T(8,128)(2,1)S(1)} %get-tuple-element.94), channel_id=1, source_target_pairs={{0,10},{1,11},{2,8},{3,9},{4,14},{5,15},{6,12},{7,13},{8,2},{9,3},... | collective-permute-start | bytes 196616 | tf_op jit(solution)/shard_map/ppermute | solution.py:548
  46.7 1.9 %collective-permute-done.12.refs_1_ = bf16[128,256]{1,0:T(8,128)(2,1)S(1)} collective-permute-done((bf16[128,256]{1,0:T(8,128)(2,1)S(1)}, bf16[128,256]{1,0:T(8,128)(2,1)S(1)}, u32[]{:S(2)}, u32[]{:S(2)}) %collective-permute-start.12) | collective-permute-done | bytes 65568 | tf_op jit(solution)/shard_map/ppermute | solution.py:548
  48.6 1.6 %collective-permute-start.17 = (bf16[128,256]{1,0:T(8,128)(2,1)S(1)}, bf16[128,256]{1,0:T(8,128)(2,1)S(1)}, u32[]{:S(2)}, u32[]{:S(2)}) collective-permute-start(bf16[128,256]{1,0:T(8,128)(2,1)S(1)} %get-tuple-element.95), channel_id=1, source_target_pairs={{0,12},{1,13},{2,14},{3,15},{4,8},{5,9},{6,10},{7,11},{8,4},{9,5},... | collective-permute-start | bytes 196616 | tf_op jit(solution)/shard_map/ppermute | solution.py:548
  50.2 4.3 %collective-permute-start.18 = (bf16[128,256]{1,0:T(8,128)(2,1)S(1)}, bf16[128,256]{1,0:T(8,128)(2,1)S(1)}, u32[]{:S(2)}, u32[]{:S(2)}) collective-permute-start(bf16[128,256]{1,0:T(8,128)(2,1)S(1)} %get-tuple-element.96), channel_id=1, source_target_pairs={{0,14},{1,15},{2,12},{3,13},{4,10},{5,11},{6,8},{7,9},{8,6},{9,7},... | collective-permute-start | bytes 196616 | tf_op jit(solution)/shard_map/ppermute | solution.py:548
  54.5 3.1 %collective-permute-done.15.refs_4_ = bf16[128,256]{1,0:T(8,128)(2,1)S(1)} collective-permute-done((bf16[128,256]{1,0:T(8,128)(2,1)S(1)}, bf16[128,256]{1,0:T(8,128)(2,1)S(1)}, u32[]{:S(2)}, u32[]{:S(2)}) %collective-permute-start.15) | collective-permute-done | bytes 65568 | tf_op jit(solution)/shard_map/ppermute | solution.py:548
  57.6 1.5 %collective-permute-done.16.refs_5_ = bf16[128,256]{1,0:T(8,128)(2,1)S(1)} collective-permute-done((bf16[128,256]{1,0:T(8,128)(2,1)S(1)}, bf16[128,256]{1,0:T(8,128)(2,1)S(1)}, u32[]{:S(2)}, u32[]{:S(2)}) %collective-permute-start.16) | collective-permute-done | bytes 65568 | tf_op jit(solution)/shard_map/ppermute | solution.py:548
  59.1 2.2 %collective-permute-done.17.refs_6_ = bf16[128,256]{1,0:T(8,128)(2,1)S(1)} collective-permute-done((bf16[128,256]{1,0:T(8,128)(2,1)S(1)}, bf16[128,256]{1,0:T(8,128)(2,1)S(1)}, u32[]{:S(2)}, u32[]{:S(2)}) %collective-permute-start.17) | collective-permute-done | bytes 65568 | tf_op jit(solution)/shard_map/ppermute | solution.py:548
  61.3 3.0 %collective-permute-done.18.refs_7_ = bf16[128,256]{1,0:T(8,128)(2,1)S(1)} collective-permute-done((bf16[128,256]{1,0:T(8,128)(2,1)S(1)}, bf16[128,256]{1,0:T(8,128)(2,1)S(1)}, u32[]{:S(2)}, u32[]{:S(2)}) %collective-permute-start.18) | collective-permute-done | bytes 65568 | tf_op jit(solution)/shard_map/ppermute | solution.py:548
  64.5 1.3 %shard_map.115 = bf16[1024,256]{1,0:T(8,128)(2,1)} custom-call(bf16[2048,256]{1,0:T(8,128)(2,1)S(1)} %bitcast.6, bf16[128,256]{1,0:T(8,128)(2,1)S(1)} %get-tuple-element.89.refs_0_, bf16[128,256]{1,0:T(8,128)(2,1)S(1)} %collective-permute-done.12.refs_1_, bf16[128,256]{1,0:T(8,128)(2,1)S(1)} %collective-permute-done.13.refs_2_, ...), custom_call_target="tpu_custom_call" | custom-call | flops 134217728 | bytes 2097152 | tf_op jit(solution)/shard_map/pallas_call | solution.py:478
  65.8 3.9 %all-to-all-start.1 = ((bf16[16,64,256]{2,1,0:T(8,128)(2,1)}), bf16[16,64,256]{2,1,0:T(8,128)(2,1)S(1)}, u32[]{:S(2)}, u32[]{:S(2)}) async-start(bf16[16,64,256]{2,1,0:T(8,128)(2,1)} %bitcast.4), calls=%async_computation.1 | async-start | bytes 1048576 | tf_op jit(solution)/shard_map/all_to_all | solution.py:664
  70.0 10.2 %all-to-all-done.1 = bf16[16,64,256]{2,1,0:T(8,128)(2,1)S(1)} async-done(((bf16[16,64,256]{2,1,0:T(8,128)(2,1)}), bf16[16,64,256]{2,1,0:T(8,128)(2,1)S(1)}, u32[]{:S(2)}, u32[]{:S(2)}) %all-to-all-start.1) | async-done | bytes 524320 | tf_op jit(solution)/shard_map/all_to_all | solution.py:664
  80.3 1.9 %shard_map.117 = bf16[8,256,128]{2,1,0:T(8,128)(2,1)} custom-call(bf16[1024,256]{1,0:T(8,128)(2,1)S(1)} %bitcast.7, bf16[8,128,256]{2,1,0:T(8,128)(2,1)S(1)} %get-tuple-element.97.mid_ref, f32[8,128,256]{2,1,0:T(8,128)S(1)} %shard_map.116.gate_ref, bf16[128,128]{1,0:T(8,128)(2,1)S(1)} %get-tuple-element.100.out_w), custom_call_target="tpu_custom_call" | custom-call | flops 134217728 | bytes 2654208 | tf_op jit(solution)/shard_map/pallas_call | solution.py:478
  (19 shorter events, 1.8 us)
Async XLA Ops:
  2.5 10.8 %collective-permute-start = (bf16[160,256]{1,0:T(8,128)(2,1)S(1)}, bf16[160,256]{1,0:T(8,128)(2,1)S(1)}, u32[]{:S(2)}, u32[]{:S(2)}) collective-permute-start(bf16[160,256]{1,0:T(8,128)(2,1)S(1)} %get-tuple-element.58), channel_id=1, source_target_pairs={{0,24},{1,25},{2,26},{3,27},{4,28},{5,29},{6,30},{7,31},{8,16},{9,... | collective-permute-start | bytes 245768 | tf_op jit(solution)/shard_map/ppermute | solution.py:548
  7.6 6.9 %collective-permute-start.1 = (bf16[160,256]{1,0:T(8,128)(2,1)S(1)}, bf16[160,256]{1,0:T(8,128)(2,1)S(1)}, u32[]{:S(2)}, u32[]{:S(2)}) collective-permute-start(bf16[160,256]{1,0:T(8,128)(2,1)S(1)} %get-tuple-element.59), channel_id=1, source_target_pairs={{0,16},{1,17},{2,18},{3,19},{4,20},{5,21},{6,22},{7,23},{8,24},{9,... | collective-permute-start | bytes 245768 | tf_op jit(solution)/shard_map/ppermute | solution.py:548
  7.6 6.9 %collective-permute-start.2 = (bf16[160,256]{1,0:T(8,128)(2,1)S(1)}, bf16[160,256]{1,0:T(8,128)(2,1)S(1)}, u32[]{:S(2)}, u32[]{:S(2)}) collective-permute-start(bf16[160,256]{1,0:T(8,128)(2,1)S(1)} %get-tuple-element.60), channel_id=1, source_target_pairs={{0,8},{1,9},{2,10},{3,11},{4,12},{5,13},{6,14},{7,15},{8,0},{9,1},... | collective-permute-start | bytes 245768 | tf_op jit(solution)/shard_map/ppermute | solution.py:548
  8.2 6.2 %collective-permute-start.3 = (bf16[160,256]{1,0:T(8,128)(2,1)S(1)}, bf16[160,256]{1,0:T(8,128)(2,1)S(1)}, u32[]{:S(2)}, u32[]{:S(2)}) collective-permute-start(bf16[160,256]{1,0:T(8,128)(2,1)S(1)} %get-tuple-element.74.refs_0_), channel_id=1, source_target_pairs={{0,6},{1,7},{2,4},{3,5},{4,2},{5,3},{6,0},{7,1},{8,14},{9,15},{10,... | collective-permute-start | bytes 245768 | tf_op jit(solution)/shard_map/ppermute | solution.py:548
  14.7 14.0 %collective-permute-start.5 = (bf16[544,256]{1,0:T(8,128)(2,1)S(1)}, bf16[544,256]{1,0:T(8,128)(2,1)S(1)}, u32[]{:S(2)}, u32[]{:S(2)}) collective-permute-start(bf16[544,256]{1,0:T(8,128)(2,1)S(1)} %get-tuple-element.81), channel_id=1, source_target_pairs={{0,4},{1,5},{2,6},{3,7},{4,0},{5,1},{6,2},{7,3},{8,12},{9,13},{10,... | collective-permute-start | bytes 835592 | tf_op jit(solution)/shard_map/ppermute | solution.py:548
  16.3 13.0 %collective-permute-start.6 = (bf16[544,256]{1,0:T(8,128)(2,1)S(1)}, bf16[544,256]{1,0:T(8,128)(2,1)S(1)}, u32[]{:S(2)}, u32[]{:S(2)}) collective-permute-start(bf16[544,256]{1,0:T(8,128)(2,1)S(1)} %get-tuple-element.82), channel_id=1, source_target_pairs={{0,2},{1,3},{2,0},{3,1},{4,6},{5,7},{6,4},{7,5},{8,10},{9,11},{10,... | collective-permute-start | bytes 835592 | tf_op jit(solution)/shard_map/ppermute | solution.py:548
  17.8 10.6 %collective-permute-start.4 = (bf16[416,256]{1,0:T(8,128)(2,1)S(1)}, bf16[416,256]{1,0:T(8,128)(2,1)S(1)}, u32[]{:S(2)}, u32[]{:S(2)}) collective-permute-start(bf16[416,256]{1,0:T(8,128)(2,1)S(1)} %get-tuple-element.80), channel_id=1, source_target_pairs={{0,6},{1,7},{2,4},{3,5},{4,2},{5,3},{6,0},{7,1},{8,14},{9,15},{10,... | collective-permute-start | bytes 638984 | tf_op jit(solution)/shard_map/ppermute | solution.py:548
  18.3 11.1 %collective-permute-start.7 = (bf16[544,256]{1,0:T(8,128)(2,1)S(1)}, bf16[544,256]{1,0:T(8,128)(2,1)S(1)}, u32[]{:S(2)}, u32[]{:S(2)}) collective-permute-start(bf16[544,256]{1,0:T(8,128)(2,1)S(1)} %get-tuple-element.78.refs_0_), channel_id=1, source_target_pairs={{0,1},{1,0},{2,3},{3,2},{4,5},{5,4},{6,7},{7,6},{8,9},{9,8},{10,11... | collective-permute-start | bytes 835592 | tf_op jit(solution)/shard_map/ppermute | solution.py:548
  28.7 1.6 %collective-permute-start.8 = (bf16[544,256]{1,0:T(8,128)(2,1)S(1)}, bf16[544,256]{1,0:T(8,128)(2,1)S(1)}, u32[]{:S(2)}, u32[]{:S(2)}) collective-permute-start(bf16[544,256]{1,0:T(8,128)(2,1)S(1)} %shard_map.112.refs_1_), channel_id=1, source_target_pairs={{0,1},{1,0},{2,3},{3,2},{4,5},{5,4},{6,7},{7,6},{8,9},{9,8},{10,11... | collective-permute-start | bytes 835592 | tf_op jit(solution)/shard_map/ppermute | solution.py:548
  28.8 1.9 %collective-permute-start.9 = (bf16[544,256]{1,0:T(8,128)(2,1)S(1)}, bf16[544,256]{1,0:T(8,128)(2,1)S(1)}, u32[]{:S(2)}, u32[]{:S(2)}) collective-permute-start(bf16[544,256]{1,0:T(8,128)(2,1)S(1)} %collective-permute-done.5.refs_2_), channel_id=1, source_target_pairs={{0,1},{1,0},{2,3},{3,2},{4,5},{5,4},{6,7},{7,6},{8,9},{9,8},{10,11... | collective-permute-start | bytes 835592 | tf_op jit(solution)/shard_map/ppermute | solution.py:548
  29.2 1.8 %collective-permute-start.10 = (bf16[544,256]{1,0:T(8,128)(2,1)S(1)}, bf16[544,256]{1,0:T(8,128)(2,1)S(1)}, u32[]{:S(2)}, u32[]{:S(2)}) collective-permute-start(bf16[544,256]{1,0:T(8,128)(2,1)S(1)} %collective-permute-done.6.refs_3_), channel_id=1, source_target_pairs={{0,1},{1,0},{2,3},{3,2},{4,5},{5,4},{6,7},{7,6},{8,9},{9,8},{10,11... | collective-permute-start | bytes 835592 | tf_op jit(solution)/shard_map/ppermute | solution.py:548
  35.2 29.4 %all-to-all-start = ((bf16[32,64,256]{2,1,0:T(8,128)(2,1)}), bf16[32,64,256]{2,1,0:T(8,128)(2,1)S(1)}, u32[]{:S(2)}, u32[]{:S(2)}) async-start(bf16[32,64,256]{2,1,0:T(8,128)(2,1)} %bitcast.2), calls=%async_computation | async-start | bytes 2097152 | tf_op jit(solution)/shard_map/all_to_all | solution.py:637
  38.3 1.6 %collective-permute-start.11 = (bf16[512,256]{1,0:T(8,128)(2,1)S(1)}, bf16[512,256]{1,0:T(8,128)(2,1)S(1)}, u32[]{:S(2)}, u32[]{:S(2)}) collective-permute-start(bf16[512,256]{1,0:T(8,128)(2,1)S(1)} %get-tuple-element.88), channel_id=1, source_target_pairs={{0,1},{1,0},{2,3},{3,2},{4,5},{5,4},{6,7},{7,6},{8,9},{9,8},{10,11... | collective-permute-start | bytes 786440 | tf_op jit(solution)/shard_map/ppermute | solution.py:548
  39.9 8.7 %collective-permute-start.12 = (bf16[128,256]{1,0:T(8,128)(2,1)S(1)}, bf16[128,256]{1,0:T(8,128)(2,1)S(1)}, u32[]{:S(2)}, u32[]{:S(2)}) collective-permute-start(bf16[128,256]{1,0:T(8,128)(2,1)S(1)} %get-tuple-element.90), channel_id=1, source_target_pairs={{0,2},{1,3},{2,0},{3,1},{4,6},{5,7},{6,4},{7,5},{8,10},{9,11},{10,... | collective-permute-start | bytes 196616 | tf_op jit(solution)/shard_map/ppermute | solution.py:548
  41.8 8.4 %collective-permute-start.13 = (bf16[128,256]{1,0:T(8,128)(2,1)S(1)}, bf16[128,256]{1,0:T(8,128)(2,1)S(1)}, u32[]{:S(2)}, u32[]{:S(2)}) collective-permute-start(bf16[128,256]{1,0:T(8,128)(2,1)S(1)} %get-tuple-element.91), channel_id=1, source_target_pairs={{0,4},{1,5},{2,6},{3,7},{4,0},{5,1},{6,2},{7,3},{8,12},{9,13},{10,... | collective-permute-start | bytes 196616 | tf_op jit(solution)/shard_map/ppermute | solution.py:548
  43.2 11.3 %collective-permute-start.14 = (bf16[128,256]{1,0:T(8,128)(2,1)S(1)}, bf16[128,256]{1,0:T(8,128)(2,1)S(1)}, u32[]{:S(2)}, u32[]{:S(2)}) collective-permute-start(bf16[128,256]{1,0:T(8,128)(2,1)S(1)} %get-tuple-element.92), channel_id=1, source_target_pairs={{0,6},{1,7},{2,4},{3,5},{4,2},{5,3},{6,0},{7,1},{8,14},{9,15},{10,... | collective-permute-start | bytes 196616 | tf_op jit(solution)/shard_map/ppermute | solution.py:548
  43.5 14.2 %collective-permute-start.15 = (bf16[128,256]{1,0:T(8,128)(2,1)S(1)}, bf16[128,256]{1,0:T(8,128)(2,1)S(1)}, u32[]{:S(2)}, u32[]{:S(2)}) collective-permute-start(bf16[128,256]{1,0:T(8,128)(2,1)S(1)} %get-tuple-element.93), channel_id=1, source_target_pairs={{0,8},{1,9},{2,10},{3,11},{4,12},{5,13},{6,14},{7,15},{8,0},{9,1},... | collective-permute-start | bytes 196616 | tf_op jit(solution)/shard_map/ppermute | solution.py:548
  45.2 13.9 %collective-permute-start.16 = (bf16[128,256]{1,0:T(8,128)(2,1)S(1)}, bf16[128,256]{1,0:T(8,128)(2,1)S(1)}, u32[]{:S(2)}, u32[]{:S(2)}) collective-permute-start(bf16[128,256]{1,0:T(8,128)(2,1)S(1)} %get-tuple-element.94), channel_id=1, source_target_pairs={{0,10},{1,11},{2,8},{3,9},{4,14},{5,15},{6,12},{7,13},{8,2},{9,3},... | collective-permute-start | bytes 196616 | tf_op jit(solution)/shard_map/ppermute | solution.py:548
  48.6 12.6 %collective-permute-start.17 = (bf16[128,256]{1,0:T(8,128)(2,1)S(1)}, bf16[128,256]{1,0:T(8,128)(2,1)S(1)}, u32[]{:S(2)}, u32[]{:S(2)}) collective-permute-start(bf16[128,256]{1,0:T(8,128)(2,1)S(1)} %get-tuple-element.95), channel_id=1, source_target_pairs={{0,12},{1,13},{2,14},{3,15},{4,8},{5,9},{6,10},{7,11},{8,4},{9,5},... | collective-permute-start | bytes 196616 | tf_op jit(solution)/shard_map/ppermute | solution.py:548
  50.2 14.1 %collective-permute-start.18 = (bf16[128,256]{1,0:T(8,128)(2,1)S(1)}, bf16[128,256]{1,0:T(8,128)(2,1)S(1)}, u32[]{:S(2)}, u32[]{:S(2)}) collective-permute-start(bf16[128,256]{1,0:T(8,128)(2,1)S(1)} %get-tuple-element.96), channel_id=1, source_target_pairs={{0,14},{1,15},{2,12},{3,13},{4,10},{5,11},{6,8},{7,9},{8,6},{9,7},... | collective-permute-start | bytes 196616 | tf_op jit(solution)/shard_map/ppermute | solution.py:548
  65.8 14.5 %all-to-all-start.1 = ((bf16[16,64,256]{2,1,0:T(8,128)(2,1)}), bf16[16,64,256]{2,1,0:T(8,128)(2,1)S(1)}, u32[]{:S(2)}, u32[]{:S(2)}) async-start(bf16[16,64,256]{2,1,0:T(8,128)(2,1)} %bitcast.4), calls=%async_computation.1 | async-start | bytes 1048576 | tf_op jit(solution)/shard_map/all_to_all | solution.py:664

commit v7 on v6

--- a/solution.py
+++ b/solution.py
@@ -337,8 +337,8 @@
 
 def pair_kernel(sizes, held, scale, *refs):
     n_core, rows, n_dev = sizes[2], sizes[3], sizes[4]
-    groups = refs[:-10]
-    pair_ref, out_w, tri_w, send_ref, own_ref, other_ref, mid_ref, norm_ref, outer, both = refs[-10:]
+    groups = refs[:-11]
+    pair_ref, out_w, tri_w, send_ref, left_ref, mid_ref, norm_ref, outer, both, right_ref, sems = refs[-11:]
     factor = groups[0].shape[0] // held - n_core
     hidden = tri_w.shape[0] // 4
     core = lax.axis_index("seq") % n_core
@@ -359,37 +359,33 @@
         mid_ref[i] = mid
         normed = normalize(mid.astype(F32), 0).astype(BF16)
         norm_ref[i] = normed
-    for i in range(rows):
-        parts = mul(tri_w[...], norm_ref[i])
-        for side in range(2):
-            at = 2 * side * hidden
-            gate = jax.nn.sigmoid(parts[at : at + hidden])
-            both[side, i] = (gate * parts[at + hidden : at + 2 * hidden]).astype(BF16)
     half = n_dev // 2
     chunk = hidden // half * rows
     some = 256 // rows
     shuffle = swap_rows(rows, some)
     per = some * rows // chunk
-    for b in range(hidden // some):
-        left, right = (
-            mul(
-                shuffle,
-                jnp.concatenate(
-                    [both[side, i, b * some : (b + 1) * some, :] for i in range(rows)], 0
-                ),
-            ).astype(BF16)
-            for side in range(2)
-        )
+
+    def by_channels(side):
+        at = 2 * side * hidden
+        for i in range(rows):
+            parts = mul(tri_w[at : at + 2 * hidden, :], norm_ref[i])
+            both[side, i] = (jax.nn.sigmoid(parts[:hidden]) * parts[hidden:]).astype(BF16)
+        blocks = [
+            jnp.concatenate([both[side, i, b * some : (b + 1) * some, :] for i in range(rows)], 0)
+            for b in range(hidden // some)
+        ]
+        return [mul(shuffle, block).astype(BF16) for block in blocks]
+
+    for b, block in enumerate(by_channels(1)):
+        right_ref[b * per * chunk : (b + 1) * per * chunk, :] = block
+    targets = [send_ref.at[pl.ds(h * half * chunk, half * chunk)] for h in range(2)]
+    copies = fetch(sems, [(right_ref, target) for target in targets])
+    for b, block in enumerate(by_channels(0)):
         for d in range(per):
-            for side in range(2):
-                to = (side * half + b * per + d) * chunk
-                send_ref[to : to + chunk, :] = right[d * chunk : (d + 1) * chunk]
-        for d in range(0, per, n_core):
-            to = (b * per + d) // n_core * chunk
-            even = left[d * chunk : (d + 1) * chunk]
-            odd = left[(d + 1) * chunk : (d + 2) * chunk]
-            own_ref[to : to + chunk, :] = jnp.where(core == 0, even, odd)
-            other_ref[to : to + chunk, :] = jnp.where(core == 0, odd, even)
+            to = (d % n_core * half + b * per + d) // n_core * chunk
+            left_ref[to : to + chunk, :] = block[d * chunk : (d + 1) * chunk]
+    for copy in copies:
+        copy.wait()
 
 
 def half_index(sizes):
@@ -401,15 +397,17 @@
 
 def left_kernel(sizes, own_ref, came_ref, *out_refs):
     n_core = sizes[2]
-    chunk = own_ref.shape[0] // len(out_refs)
+    chunk = own_ref.shape[0] // len(out_refs) // n_core
     core = lax.axis_index("seq") % n_core
     here = half_index(sizes)
-    own_at = pl.multiple_of(core * chunk, chunk)
-    came_at = pl.multiple_of((1 - core) * chunk, chunk)
+    rows = sizes[3]
+    per, cols = chunk // rows, own_ref.shape[1]
     for k, ref in enumerate(out_refs):
-        at = pl.multiple_of((here ^ k) * chunk, chunk)
-        ref[pl.ds(own_at, chunk), :] = own_ref[pl.ds(at, chunk), :]
-        ref[pl.ds(came_at, chunk), :] = came_ref[pl.ds(at, chunk), :]
+        at = pl.multiple_of((core * len(out_refs) + (here ^ k)) * chunk, chunk)
+        own = own_ref[pl.ds(at, chunk), :].astype(F32).reshape(per, rows, cols)
+        came = came_ref[pl.ds(at, chunk), :].astype(F32).reshape(per, rows, cols)
+        pair = [jnp.where(core == 0, own, came), jnp.where(core == 0, came, own)]
+        ref[...] = jnp.concatenate(pair, 1).reshape(n_core * chunk, cols).astype(BF16)
 
 
 def product_kernel(sizes, per, recv_ref, *refs):
@@ -423,13 +421,11 @@
         for c in range(per):
             right[c, src * rows : (src + 1) * rows, :] = block[c * rows : (c + 1) * rows]
     for k, ref in enumerate(left_refs):
-        for core in range(n_core):
-            block = ref[core * chunk : (core + 1) * chunk, :].astype(F32)
-            at = pl.multiple_of(((here ^ k) * n_core + core) * rows, rows)
-            for c in range(per):
-                left[c, pl.ds(at, rows), :] = block[c * rows : (c + 1) * rows]
+        at = pl.multiple_of((here ^ k) * n_core * rows, n_core * rows)
+        for c in range(per):
+            left[c, pl.ds(at, n_core * rows), :] = ref[c * n_core * rows : (c + 1) * n_core * rows, :]
     for c in range(per):
-        prod = mul_t(left[c].astype(BF16), right[c].astype(BF16))
+        prod = mul_t(left[c], right[c].astype(BF16))
         for dst in range(half):
             total[dst, c * rows : (c + 1) * rows, :] = prod[dst * rows : (dst + 1) * rows]
     for dst in range(half):
@@ -469,17 +465,21 @@
 
 
 def call(kernel, out_shape, scratch, grant, flops, *args, far_in=False, far_out=False):
-    spaces = [pltpu.HBM if far else pltpu.VMEM for far in (far_in, far_out)]
-    place = jax.ShapeDtypeStruct if far_out else pltpu.VMEM
-    out_shape = [place(*s) if isinstance(s[0], tuple) else place(s, BF16) for s in out_shape]
+    if isinstance(far_out, bool):
+        far_out = [far_out] * len(out_shape)
+    out_specs = [pl.BlockSpec(memory_space=pltpu.HBM if far else pltpu.VMEM) for far in far_out]
+    out_shape = [
+        (jax.ShapeDtypeStruct if far else pltpu.VMEM)(*(s if isinstance(s[0], tuple) else (s, BF16)))
+        for s, far in zip(out_shape, far_out, strict=True)
+    ]
     if far_in:
         args = [pltpu.with_memory_space_constraint(a, pltpu.HBM) for a in args]
     moved = sum(math.prod(a.shape) * jnp.dtype(a.dtype).itemsize for a in (*args, *out_shape))
     return pl.pallas_call(
         kernel,
         out_shape=out_shape,
-        in_specs=[pl.BlockSpec(memory_space=spaces[0])] * len(args),
-        out_specs=[pl.BlockSpec(memory_space=spaces[1])] * len(out_shape),
+        in_specs=[pl.BlockSpec(memory_space=pltpu.HBM if far_in else pltpu.VMEM)] * len(args),
+        out_specs=out_specs,
         scratch_shapes=scratch,
         compiler_params=pltpu.CompilerParams(vmem_limit_bytes=grant * 2**20),
         cost_estimate=pl.CostEstimate(flops=flops, bytes_accessed=moved, transcendentals=0),
@@ -605,18 +605,19 @@
     near = [mine[0]] + near
     groups = near + [exchange(block, 0, 1) for block in near]
     scale = 1.0 / (held * n_near * n_core)
-    send, own, other, mid, normed = call(
+    send, left, mid, normed = call(
         functools.partial(pair_kernel, sizes, held, scale),
         [
             (2 * hidden * rows, cols),
-            (chips * per * rows, cols),
-            (chips * per * rows, cols),
+            (hidden * rows, cols),
             (rows, width, cols),
             (rows, width, cols),
         ],
         [
             pltpu.VMEM((rows, factor * factor, cols), BF16),
             pltpu.VMEM((2, rows, hidden, cols), BF16),
+            pltpu.VMEM((hidden * rows, cols), BF16),
+            pltpu.SemaphoreType.DMA((2,)),
         ],
         16,
         4 * rows * cols * width * (factor * factor + hidden * 2),
@@ -624,6 +625,7 @@
         pair_t,
         out_t,
         tri_t,
+        far_out=(True, False, False, False),
     )
     (gate,) = call(
         gate_kernel,
@@ -641,8 +643,8 @@
         [],
         8,
         0,
-        own,
-        exchange(other, 0, 1),
+        left,
+        exchange(left, 0, 1),
     )
     lefts = [mine[0]]
     for k in range(1, chips):
@@ -651,7 +653,7 @@
         functools.partial(product_kernel, sizes, per),
         [(hidden * rows, cols)],
         [
-            pltpu.VMEM((per, rows * half, cols), F32),
+            pltpu.VMEM((per, rows * half, cols), BF16),
             pltpu.VMEM((per, rows * n_dev, cols), F32),
             pltpu.VMEM((half, per * rows, cols), F32),
         ],

time: 82.5 us -> 82.1 us (level)
  no operation moved by 1% of the time
where the time goes in v7:
time: 82.1 us; the launch traced here: 81.8 us
  waiting for transfers between devices  36.4 us (44%)
  starting transfers between devices  32.6 us (40%)
  Pallas kernels  12.6 us (15%)
    ppermute x19, waiting for transfers between devices, exchange(): return lax.ppermute(value, BOTH, pairs)  25.9 us
    ppermute x19, starting transfers between devices, exchange(): return lax.ppermute(value, BOTH, pairs)  25.6 us
    pallas_call x9, Pallas kernels, call(): pl.pallas_call(kernel, out_shape=out_shape, in_specs=[pl.BlockSpec(memory...  12.6 us
    all_to_all x1, waiting for transfers between devices, whole_channels(): lax.all_to_all(send, BOTH, split_axis=0, concat_axis=0, tiled=True, axis_...  10.2 us
    all_to_all x1, starting transfers between devices, whole_channels(): lax.all_to_all(send, BOTH, split_axis=0, concat_axis=0, tiled=True, axis_...  3.91 us
    all_to_all x1, starting transfers between devices, whole_channels(): recv = lax.all_to_all(send, BOTH, split_axis=0, concat_axis=0, tiled=True)  3.12 us
  transfers between devices with their start and end apart: 21, of which 13 were waited for; matrix products, arithmetic and copies ran while one was open for 0% of the time, Pallas kernels for 4%

profile of v7, /device:TPU:0, one launch (start us, length us, event | category | flops | bytes accessed | tf_op | source)
XLA Modules:
  0.0 81.8 jit_solution(15513838100363239896)
XLA Ops:
  0.0 2.5 %shard_map.109 = (bf16[160,256]{1,0:T(8,128)(2,1)S(1)}, bf16[160,256]{1,0:T(8,128)(2,1)S(1)}, bf16[160,256]{1,0:T(8,128)(2,1)S(1)}, bf16[160,256]{1,0:T(8,128)(2,1)S(1)}) custom-call(bf16[4,256,256]{2,1,0:T(8,128)(2,1)} %align_in.1, bf16[32,256]{1,0:T(8,128)(2,1)} %bitcast.8, bf16[32,256]{1,0:T(8,128)(2,1)} %bitcast.9), custom_call_target="tpu_custom_call" | custom-call | flops 33554432 | bytes 884736 | tf_op jit(solution)/shard_map/pallas_call | solution.py:478
  2.5 5.1 %collective-permute-start = (bf16[160,256]{1,0:T(8,128)(2,1)S(1)}, bf16[160,256]{1,0:T(8,128)(2,1)S(1)}, u32[]{:S(2)}, u32[]{:S(2)}) collective-permute-start(bf16[160,256]{1,0:T(8,128)(2,1)S(1)} %get-tuple-element.57), channel_id=1, source_target_pairs={{0,24},{1,25},{2,26},{3,27},{4,28},{5,29},{6,30},{7,31},{8,16},{9,... | collective-permute-start | bytes 245768 | tf_op jit(solution)/shard_map/ppermute | solution.py:548
  7.6 0.6 collective-permute-start.2
  8.2 2.6 %collective-permute-start.3 = (bf16[160,256]{1,0:T(8,128)(2,1)S(1)}, bf16[160,256]{1,0:T(8,128)(2,1)S(1)}, u32[]{:S(2)}, u32[]{:S(2)}) collective-permute-start(bf16[160,256]{1,0:T(8,128)(2,1)S(1)} %get-tuple-element.73.refs_0_), channel_id=1, source_target_pairs={{0,6},{1,7},{2,4},{3,5},{4,2},{5,3},{6,0},{7,1},{8,14},{9,15},{10,... | collective-permute-start | bytes 245768 | tf_op jit(solution)/shard_map/ppermute | solution.py:548
  10.8 2.5 %shard_map.110 = (bf16[8,128,256]{2,1,0:T(8,128)(2,1)S(1)}, bf16[128,1024]{1,0:T(8,128)(2,1)S(1)}, bf16[512,128]{1,0:T(8,128)(2,1)S(1)}, bf16[128,128]{1,0:T(8,128)(2,1)S(1)}, bf16[128,128]{1,0:T(8,128)(2,1)S(1)}) custom-call(bf16[8,256,128]{2,1,0:T(8,128)(2,1)} %refs_0_, bf16[1024,128]{1,0:T(8,128)(2,1)} %refs_1_, bf16[128,128]{1,0:T(8,128)(2,1)} %refs_2_, ...), custom_call_target="tpu_custom_call" | custom-call | flops 134217728 | bytes 1966080 | tf_op jit(solution)/shard_map/pallas_call | solution.py:478
  13.3 1.2 %collective-permute-done.1.refs_2_ = bf16[160,256]{1,0:T(8,128)(2,1)S(1)} collective-permute-done((bf16[160,256]{1,0:T(8,128)(2,1)S(1)}, bf16[160,256]{1,0:T(8,128)(2,1)S(1)}, u32[]{:S(2)}, u32[]{:S(2)}) %collective-permute-start.1) | collective-permute-done | bytes 81952 | tf_op jit(solution)/shard_map/ppermute | solution.py:548
  14.7 1.6 %collective-permute-start.5 = (bf16[544,256]{1,0:T(8,128)(2,1)S(1)}, bf16[544,256]{1,0:T(8,128)(2,1)S(1)}, u32[]{:S(2)}, u32[]{:S(2)}) collective-permute-start(bf16[544,256]{1,0:T(8,128)(2,1)S(1)} %get-tuple-element.80), channel_id=1, source_target_pairs={{0,4},{1,5},{2,6},{3,7},{4,0},{5,1},{6,2},{7,3},{8,12},{9,13},{10,... | collective-permute-start | bytes 835592 | tf_op jit(solution)/shard_map/ppermute | solution.py:548
  16.3 1.5 %collective-permute-start.6 = (bf16[544,256]{1,0:T(8,128)(2,1)S(1)}, bf16[544,256]{1,0:T(8,128)(2,1)S(1)}, u32[]{:S(2)}, u32[]{:S(2)}) collective-permute-start(bf16[544,256]{1,0:T(8,128)(2,1)S(1)} %get-tuple-element.81), channel_id=1, source_target_pairs={{0,2},{1,3},{2,0},{3,1},{4,6},{5,7},{6,4},{7,5},{8,10},{9,11},{10,... | collective-permute-start | bytes 835592 | tf_op jit(solution)/shard_map/ppermute | solution.py:548
  17.8 0.5 collective-permute-start.4
  18.3 10.1 %collective-permute-done.4.late_ref = bf16[416,256]{1,0:T(8,128)(2,1)S(1)} collective-permute-done((bf16[416,256]{1,0:T(8,128)(2,1)S(1)}, bf16[416,256]{1,0:T(8,128)(2,1)S(1)}, u32[]{:S(2)}, u32[]{:S(2)}) %collective-permute-start.4) | collective-permute-done | bytes 213024 | tf_op jit(solution)/shard_map/ppermute | solution.py:548
  28.8 0.5 collective-permute-start.9
  29.3 1.0 %collective-permute-done.8.refs_5_ = bf16[544,256]{1,0:T(8,128)(2,1)S(1)} collective-permute-done((bf16[544,256]{1,0:T(8,128)(2,1)S(1)}, bf16[544,256]{1,0:T(8,128)(2,1)S(1)}, u32[]{:S(2)}, u32[]{:S(2)}) %collective-permute-start.8) | collective-permute-done | bytes 278560 | tf_op jit(solution)/shard_map/ppermute | solution.py:548
  30.3 0.4 collective-permute-done.9.refs_6_
  30.7 0.4 collective-permute-done.10.refs_7_
  31.1 3.7 %shard_map.113 = (bf16[2048,256]{1,0:T(8,128)(2,1)}, bf16[1024,256]{1,0:T(8,128)(2,1)S(1)}, bf16[8,128,256]{2,1,0:T(8,128)(2,1)S(1)}, bf16[8,128,256]{2,1,0:T(8,128)(2,1)S(1)}) custom-call(bf16[544,256]{1,0:T(8,128)(2,1)S(1)} %get-tuple-element.77.refs_0_, bf16[544,256]{1,0:T(8,128)(2,1)S(1)} %shard_map.112.refs_1_, ...), custom_call_target="tpu_custom_call" | custom-call | flops 1342177280 | bytes 5767168 | tf_op jit(solution)/shard_map/pallas_call | solution.py:478
  34.8 3.1 %all-to-all-start = ((bf16[32,64,256]{2,1,0:T(8,128)(2,1)}), bf16[32,64,256]{2,1,0:T(8,128)(2,1)S(1)}, u32[]{:S(2)}, u32[]{:S(2)}) async-start(bf16[32,64,256]{2,1,0:T(8,128)(2,1)} %bitcast.2), calls=%async_computation | async-start | bytes 2097152 | tf_op jit(solution)/shard_map/all_to_all | solution.py:639
  37.9 0.3 collective-permute-start.11
  38.2 1.7 %collective-permute-done.11.came_ref = bf16[1024,256]{1,0:T(8,128)(2,1)S(1)} collective-permute-done((bf16[1024,256]{1,0:T(8,128)(2,1)S(1)}, bf16[1024,256]{1,0:T(8,128)(2,1)S(1)}, u32[]{:S(2)}, u32[]{:S(2)}) %collective-permute-start.11) | collective-permute-done | bytes 524320 | tf_op jit(solution)/shard_map/ppermute | solution.py:548
  40.0 1.8 %collective-permute-start.12 = (bf16[128,256]{1,0:T(8,128)(2,1)S(1)}, bf16[128,256]{1,0:T(8,128)(2,1)S(1)}, u32[]{:S(2)}, u32[]{:S(2)}) collective-permute-start(bf16[128,256]{1,0:T(8,128)(2,1)S(1)} %get-tuple-element.88), channel_id=1, source_target_pairs={{0,2},{1,3},{2,0},{3,1},{4,6},{5,7},{6,4},{7,5},{8,10},{9,11},{10,... | collective-permute-start | bytes 196616 | tf_op jit(solution)/shard_map/ppermute | solution.py:548
  41.8 1.5 %collective-permute-start.13 = (bf16[128,256]{1,0:T(8,128)(2,1)S(1)}, bf16[128,256]{1,0:T(8,128)(2,1)S(1)}, u32[]{:S(2)}, u32[]{:S(2)}) collective-permute-start(bf16[128,256]{1,0:T(8,128)(2,1)S(1)} %get-tuple-element.89), channel_id=1, source_target_pairs={{0,4},{1,5},{2,6},{3,7},{4,0},{5,1},{6,2},{7,3},{8,12},{9,13},{10,... | collective-permute-start | bytes 196616 | tf_op jit(solution)/shard_map/ppermute | solution.py:548
  43.5 1.8 %collective-permute-start.15 = (bf16[128,256]{1,0:T(8,128)(2,1)S(1)}, bf16[128,256]{1,0:T(8,128)(2,1)S(1)}, u32[]{:S(2)}, u32[]{:S(2)}) collective-permute-start(bf16[128,256]{1,0:T(8,128)(2,1)S(1)} %get-tuple-element.91), channel_id=1, source_target_pairs={{0,8},{1,9},{2,10},{3,11},{4,12},{5,13},{6,14},{7,15},{8,0},{9,1},... | collective-permute-start | bytes 196616 | tf_op jit(solution)/shard_map/ppermute | solution.py:548
  45.3 1.5 %collective-permute-start.16 = (bf16[128,256]{1,0:T(8,128)(2,1)S(1)}, bf16[128,256]{1,0:T(8,128)(2,1)S(1)}, u32[]{:S(2)}, u32[]{:S(2)}) collective-permute-start(bf16[128,256]{1,0:T(8,128)(2,1)S(1)} %get-tuple-element.92), channel_id=1, source_target_pairs={{0,10},{1,11},{2,8},{3,9},{4,14},{5,15},{6,12},{7,13},{8,2},{9,3},... | collective-permute-start | bytes 196616 | tf_op jit(solution)/shard_map/ppermute | solution.py:548
  46.8 2.9 %collective-permute-done.12.refs_1_ = bf16[128,256]{1,0:T(8,128)(2,1)S(1)} collective-permute-done((bf16[128,256]{1,0:T(8,128)(2,1)S(1)}, bf16[128,256]{1,0:T(8,128)(2,1)S(1)}, u32[]{:S(2)}, u32[]{:S(2)}) %collective-permute-start.12) | collective-permute-done | bytes 65568 | tf_op jit(solution)/shard_map/ppermute | solution.py:548
  49.8 5.8 %collective-permute-start.18 = (bf16[128,256]{1,0:T(8,128)(2,1)S(1)}, bf16[128,256]{1,0:T(8,128)(2,1)S(1)}, u32[]{:S(2)}, u32[]{:S(2)}) collective-permute-start(bf16[128,256]{1,0:T(8,128)(2,1)S(1)} %get-tuple-element.94), channel_id=1, source_target_pairs={{0,14},{1,15},{2,12},{3,13},{4,10},{5,11},{6,8},{7,9},{8,6},{9,7},... | collective-permute-start | bytes 196616 | tf_op jit(solution)/shard_map/ppermute | solution.py:548
  55.6 1.6 %collective-permute-done.15.refs_4_ = bf16[128,256]{1,0:T(8,128)(2,1)S(1)} collective-permute-done((bf16[128,256]{1,0:T(8,128)(2,1)S(1)}, bf16[128,256]{1,0:T(8,128)(2,1)S(1)}, u32[]{:S(2)}, u32[]{:S(2)}) %collective-permute-start.15) | collective-permute-done | bytes 65568 | tf_op jit(solution)/shard_map/ppermute | solution.py:548
  57.3 1.5 %collective-permute-done.16.refs_5_ = bf16[128,256]{1,0:T(8,128)(2,1)S(1)} collective-permute-done((bf16[128,256]{1,0:T(8,128)(2,1)S(1)}, bf16[128,256]{1,0:T(8,128)(2,1)S(1)}, u32[]{:S(2)}, u32[]{:S(2)}) %collective-permute-start.16) | collective-permute-done | bytes 65568 | tf_op jit(solution)/shard_map/ppermute | solution.py:548
  58.7 2.2 %collective-permute-done.17.refs_6_ = bf16[128,256]{1,0:T(8,128)(2,1)S(1)} collective-permute-done((bf16[128,256]{1,0:T(8,128)(2,1)S(1)}, bf16[128,256]{1,0:T(8,128)(2,1)S(1)}, u32[]{:S(2)}, u32[]{:S(2)}) %collective-permute-start.17) | collective-permute-done | bytes 65568 | tf_op jit(solution)/shard_map/ppermute | solution.py:548
  60.9 3.0 %collective-permute-done.18.refs_7_ = bf16[128,256]{1,0:T(8,128)(2,1)S(1)} collective-permute-done((bf16[128,256]{1,0:T(8,128)(2,1)S(1)}, bf16[128,256]{1,0:T(8,128)(2,1)S(1)}, u32[]{:S(2)}, u32[]{:S(2)}) %collective-permute-start.18) | collective-permute-done | bytes 65568 | tf_op jit(solution)/shard_map/ppermute | solution.py:548
  64.2 1.3 %shard_map.115 = bf16[1024,256]{1,0:T(8,128)(2,1)} custom-call(bf16[2048,256]{1,0:T(8,128)(2,1)S(1)} %bitcast.6, bf16[128,256]{1,0:T(8,128)(2,1)S(1)} %get-tuple-element.87.refs_0_, bf16[128,256]{1,0:T(8,128)(2,1)S(1)} %collective-permute-done.12.refs_1_, bf16[128,256]{1,0:T(8,128)(2,1)S(1)} %collective-permute-done.13.refs_2_, ...), custom_call_target="tpu_custom_call" | custom-call | flops 134217728 | bytes 2097152 | tf_op jit(solution)/shard_map/pallas_call | solution.py:478
  65.4 3.9 %all-to-all-start.1 = ((bf16[16,64,256]{2,1,0:T(8,128)(2,1)}), bf16[16,64,256]{2,1,0:T(8,128)(2,1)S(1)}, u32[]{:S(2)}, u32[]{:S(2)}) async-start(bf16[16,64,256]{2,1,0:T(8,128)(2,1)} %bitcast.4), calls=%async_computation.1 | async-start | bytes 1048576 | tf_op jit(solution)/shard_map/all_to_all | solution.py:666
  69.6 10.2 %all-to-all-done.1 = bf16[16,64,256]{2,1,0:T(8,128)(2,1)S(1)} async-done(((bf16[16,64,256]{2,1,0:T(8,128)(2,1)}), bf16[16,64,256]{2,1,0:T(8,128)(2,1)S(1)}, u32[]{:S(2)}, u32[]{:S(2)}) %all-to-all-start.1) | async-done | bytes 524320 | tf_op jit(solution)/shard_map/all_to_all | solution.py:666
  79.9 1.9 %shard_map.117 = bf16[8,256,128]{2,1,0:T(8,128)(2,1)} custom-call(bf16[1024,256]{1,0:T(8,128)(2,1)S(1)} %bitcast.7, bf16[8,128,256]{2,1,0:T(8,128)(2,1)S(1)} %get-tuple-element.95.mid_ref, f32[8,128,256]{2,1,0:T(8,128)S(1)} %shard_map.116.gate_ref, bf16[128,128]{1,0:T(8,128)(2,1)S(1)} %get-tuple-element.98.out_w), custom_call_target="tpu_custom_call" | custom-call | flops 134217728 | bytes 2654208 | tf_op jit(solution)/shard_map/pallas_call | solution.py:478
  (19 shorter events, 1.7 us)
Async XLA Ops:
  2.5 10.8 %collective-permute-start = (bf16[160,256]{1,0:T(8,128)(2,1)S(1)}, bf16[160,256]{1,0:T(8,128)(2,1)S(1)}, u32[]{:S(2)}, u32[]{:S(2)}) collective-permute-start(bf16[160,256]{1,0:T(8,128)(2,1)S(1)} %get-tuple-element.57), channel_id=1, source_target_pairs={{0,24},{1,25},{2,26},{3,27},{4,28},{5,29},{6,30},{7,31},{8,16},{9,... | collective-permute-start | bytes 245768 | tf_op jit(solution)/shard_map/ppermute | solution.py:548
  7.6 6.9 %collective-permute-start.1 = (bf16[160,256]{1,0:T(8,128)(2,1)S(1)}, bf16[160,256]{1,0:T(8,128)(2,1)S(1)}, u32[]{:S(2)}, u32[]{:S(2)}) collective-permute-start(bf16[160,256]{1,0:T(8,128)(2,1)S(1)} %get-tuple-element.58), channel_id=1, source_target_pairs={{0,16},{1,17},{2,18},{3,19},{4,20},{5,21},{6,22},{7,23},{8,24},{9,... | collective-permute-start | bytes 245768 | tf_op jit(solution)/shard_map/ppermute | solution.py:548
  7.6 6.9 %collective-permute-start.2 = (bf16[160,256]{1,0:T(8,128)(2,1)S(1)}, bf16[160,256]{1,0:T(8,128)(2,1)S(1)}, u32[]{:S(2)}, u32[]{:S(2)}) collective-permute-start(bf16[160,256]{1,0:T(8,128)(2,1)S(1)} %get-tuple-element.59), channel_id=1, source_target_pairs={{0,8},{1,9},{2,10},{3,11},{4,12},{5,13},{6,14},{7,15},{8,0},{9,1},... | collective-permute-start | bytes 245768 | tf_op jit(solution)/shard_map/ppermute | solution.py:548
  8.2 6.2 %collective-permute-start.3 = (bf16[160,256]{1,0:T(8,128)(2,1)S(1)}, bf16[160,256]{1,0:T(8,128)(2,1)S(1)}, u32[]{:S(2)}, u32[]{:S(2)}) collective-permute-start(bf16[160,256]{1,0:T(8,128)(2,1)S(1)} %get-tuple-element.73.refs_0_), channel_id=1, source_target_pairs={{0,6},{1,7},{2,4},{3,5},{4,2},{5,3},{6,0},{7,1},{8,14},{9,15},{10,... | collective-permute-start | bytes 245768 | tf_op jit(solution)/shard_map/ppermute | solution.py:548
  14.7 14.0 %collective-permute-start.5 = (bf16[544,256]{1,0:T(8,128)(2,1)S(1)}, bf16[544,256]{1,0:T(8,128)(2,1)S(1)}, u32[]{:S(2)}, u32[]{:S(2)}) collective-permute-start(bf16[544,256]{1,0:T(8,128)(2,1)S(1)} %get-tuple-element.80), channel_id=1, source_target_pairs={{0,4},{1,5},{2,6},{3,7},{4,0},{5,1},{6,2},{7,3},{8,12},{9,13},{10,... | collective-permute-start | bytes 835592 | tf_op jit(solution)/shard_map/ppermute | solution.py:548
  16.3 13.0 %collective-permute-start.6 = (bf16[544,256]{1,0:T(8,128)(2,1)S(1)}, bf16[544,256]{1,0:T(8,128)(2,1)S(1)}, u32[]{:S(2)}, u32[]{:S(2)}) collective-permute-start(bf16[544,256]{1,0:T(8,128)(2,1)S(1)} %get-tuple-element.81), channel_id=1, source_target_pairs={{0,2},{1,3},{2,0},{3,1},{4,6},{5,7},{6,4},{7,5},{8,10},{9,11},{10,... | collective-permute-start | bytes 835592 | tf_op jit(solution)/shard_map/ppermute | solution.py:548
  17.8 10.6 %collective-permute-start.4 = (bf16[416,256]{1,0:T(8,128)(2,1)S(1)}, bf16[416,256]{1,0:T(8,128)(2,1)S(1)}, u32[]{:S(2)}, u32[]{:S(2)}) collective-permute-start(bf16[416,256]{1,0:T(8,128)(2,1)S(1)} %get-tuple-element.79), channel_id=1, source_target_pairs={{0,6},{1,7},{2,4},{3,5},{4,2},{5,3},{6,0},{7,1},{8,14},{9,15},{10,... | collective-permute-start | bytes 638984 | tf_op jit(solution)/shard_map/ppermute | solution.py:548
  18.3 11.1 %collective-permute-start.7 = (bf16[544,256]{1,0:T(8,128)(2,1)S(1)}, bf16[544,256]{1,0:T(8,128)(2,1)S(1)}, u32[]{:S(2)}, u32[]{:S(2)}) collective-permute-start(bf16[544,256]{1,0:T(8,128)(2,1)S(1)} %get-tuple-element.77.refs_0_), channel_id=1, source_target_pairs={{0,1},{1,0},{2,3},{3,2},{4,5},{5,4},{6,7},{7,6},{8,9},{9,8},{10,11... | collective-permute-start | bytes 835592 | tf_op jit(solution)/shard_map/ppermute | solution.py:548
  28.7 1.6 %collective-permute-start.8 = (bf16[544,256]{1,0:T(8,128)(2,1)S(1)}, bf16[544,256]{1,0:T(8,128)(2,1)S(1)}, u32[]{:S(2)}, u32[]{:S(2)}) collective-permute-start(bf16[544,256]{1,0:T(8,128)(2,1)S(1)} %shard_map.112.refs_1_), channel_id=1, source_target_pairs={{0,1},{1,0},{2,3},{3,2},{4,5},{5,4},{6,7},{7,6},{8,9},{9,8},{10,11... | collective-permute-start | bytes 835592 | tf_op jit(solution)/shard_map/ppermute | solution.py:548
  28.8 1.9 %collective-permute-start.9 = (bf16[544,256]{1,0:T(8,128)(2,1)S(1)}, bf16[544,256]{1,0:T(8,128)(2,1)S(1)}, u32[]{:S(2)}, u32[]{:S(2)}) collective-permute-start(bf16[544,256]{1,0:T(8,128)(2,1)S(1)} %collective-permute-done.5.refs_2_), channel_id=1, source_target_pairs={{0,1},{1,0},{2,3},{3,2},{4,5},{5,4},{6,7},{7,6},{8,9},{9,8},{10,11... | collective-permute-start | bytes 835592 | tf_op jit(solution)/shard_map/ppermute | solution.py:548
  29.2 1.8 %collective-permute-start.10 = (bf16[544,256]{1,0:T(8,128)(2,1)S(1)}, bf16[544,256]{1,0:T(8,128)(2,1)S(1)}, u32[]{:S(2)}, u32[]{:S(2)}) collective-permute-start(bf16[544,256]{1,0:T(8,128)(2,1)S(1)} %collective-permute-done.6.refs_3_), channel_id=1, source_target_pairs={{0,1},{1,0},{2,3},{3,2},{4,5},{5,4},{6,7},{7,6},{8,9},{9,8},{10,11... | collective-permute-start | bytes 835592 | tf_op jit(solution)/shard_map/ppermute | solution.py:548
  34.8 29.4 %all-to-all-start = ((bf16[32,64,256]{2,1,0:T(8,128)(2,1)}), bf16[32,64,256]{2,1,0:T(8,128)(2,1)S(1)}, u32[]{:S(2)}, u32[]{:S(2)}) async-start(bf16[32,64,256]{2,1,0:T(8,128)(2,1)} %bitcast.2), calls=%async_computation | async-start | bytes 2097152 | tf_op jit(solution)/shard_map/all_to_all | solution.py:639
  37.9 2.0 %collective-permute-start.11 = (bf16[1024,256]{1,0:T(8,128)(2,1)S(1)}, bf16[1024,256]{1,0:T(8,128)(2,1)S(1)}, u32[]{:S(2)}, u32[]{:S(2)}) collective-permute-start(bf16[1024,256]{1,0:T(8,128)(2,1)S(1)} %get-tuple-element.86.own_ref), channel_id=1, source_target_pairs={{0,1},{1,0},{2,3},{3,2},{4,5},{5,4},{6,7},{7,6},{8,9},{9,8},{10,11... | collective-permute-start | bytes 1572872 | tf_op jit(solution)/shard_map/ppermute | solution.py:548
  40.0 9.7 %collective-permute-start.12 = (bf16[128,256]{1,0:T(8,128)(2,1)S(1)}, bf16[128,256]{1,0:T(8,128)(2,1)S(1)}, u32[]{:S(2)}, u32[]{:S(2)}) collective-permute-start(bf16[128,256]{1,0:T(8,128)(2,1)S(1)} %get-tuple-element.88), channel_id=1, source_target_pairs={{0,2},{1,3},{2,0},{3,1},{4,6},{5,7},{6,4},{7,5},{8,10},{9,11},{10,... | collective-permute-start | bytes 196616 | tf_op jit(solution)/shard_map/ppermute | solution.py:548
  41.8 8.0 %collective-permute-start.13 = (bf16[128,256]{1,0:T(8,128)(2,1)S(1)}, bf16[128,256]{1,0:T(8,128)(2,1)S(1)}, u32[]{:S(2)}, u32[]{:S(2)}) collective-permute-start(bf16[128,256]{1,0:T(8,128)(2,1)S(1)} %get-tuple-element.89), channel_id=1, source_target_pairs={{0,4},{1,5},{2,6},{3,7},{4,0},{5,1},{6,2},{7,3},{8,12},{9,13},{10,... | collective-permute-start | bytes 196616 | tf_op jit(solution)/shard_map/ppermute | solution.py:548
  43.3 12.4 %collective-permute-start.14 = (bf16[128,256]{1,0:T(8,128)(2,1)S(1)}, bf16[128,256]{1,0:T(8,128)(2,1)S(1)}, u32[]{:S(2)}, u32[]{:S(2)}) collective-permute-start(bf16[128,256]{1,0:T(8,128)(2,1)S(1)} %get-tuple-element.90), channel_id=1, source_target_pairs={{0,6},{1,7},{2,4},{3,5},{4,2},{5,3},{6,0},{7,1},{8,14},{9,15},{10,... | collective-permute-start | bytes 196616 | tf_op jit(solution)/shard_map/ppermute | solution.py:548
  43.5 13.7 %collective-permute-start.15 = (bf16[128,256]{1,0:T(8,128)(2,1)S(1)}, bf16[128,256]{1,0:T(8,128)(2,1)S(1)}, u32[]{:S(2)}, u32[]{:S(2)}) collective-permute-start(bf16[128,256]{1,0:T(8,128)(2,1)S(1)} %get-tuple-element.91), channel_id=1, source_target_pairs={{0,8},{1,9},{2,10},{3,11},{4,12},{5,13},{6,14},{7,15},{8,0},{9,1},... | collective-permute-start | bytes 196616 | tf_op jit(solution)/shard_map/ppermute | solution.py:548
  45.3 13.4 %collective-permute-start.16 = (bf16[128,256]{1,0:T(8,128)(2,1)S(1)}, bf16[128,256]{1,0:T(8,128)(2,1)S(1)}, u32[]{:S(2)}, u32[]{:S(2)}) collective-permute-start(bf16[128,256]{1,0:T(8,128)(2,1)S(1)} %get-tuple-element.92), channel_id=1, source_target_pairs={{0,10},{1,11},{2,8},{3,9},{4,14},{5,15},{6,12},{7,13},{8,2},{9,3},... | collective-permute-start | bytes 196616 | tf_op jit(solution)/shard_map/ppermute | solution.py:548
  49.7 11.2 %collective-permute-start.17 = (bf16[128,256]{1,0:T(8,128)(2,1)S(1)}, bf16[128,256]{1,0:T(8,128)(2,1)S(1)}, u32[]{:S(2)}, u32[]{:S(2)}) collective-permute-start(bf16[128,256]{1,0:T(8,128)(2,1)S(1)} %get-tuple-element.93), channel_id=1, source_target_pairs={{0,12},{1,13},{2,14},{3,15},{4,8},{5,9},{6,10},{7,11},{8,4},{9,5},... | collective-permute-start | bytes 196616 | tf_op jit(solution)/shard_map/ppermute | solution.py:548
  49.8 14.1 %collective-permute-start.18 = (bf16[128,256]{1,0:T(8,128)(2,1)S(1)}, bf16[128,256]{1,0:T(8,128)(2,1)S(1)}, u32[]{:S(2)}, u32[]{:S(2)}) collective-permute-start(bf16[128,256]{1,0:T(8,128)(2,1)S(1)} %get-tuple-element.94), channel_id=1, source_target_pairs={{0,14},{1,15},{2,12},{3,13},{4,10},{5,11},{6,8},{7,9},{8,6},{9,7},... | collective-permute-start | bytes 196616 | tf_op jit(solution)/shard_map/ppermute | solution.py:548
  65.4 14.5 %all-to-all-start.1 = ((bf16[16,64,256]{2,1,0:T(8,128)(2,1)}), bf16[16,64,256]{2,1,0:T(8,128)(2,1)S(1)}, u32[]{:S(2)}, u32[]{:S(2)}) async-start(bf16[16,64,256]{2,1,0:T(8,128)(2,1)} %bitcast.4), calls=%async_computation.1 | async-start | bytes 1048576 | tf_op jit(solution)/shard_map/all_to_all | solution.py:666

commit v8 on v7

--- a/solution.py
+++ b/solution.py
@@ -330,11 +330,6 @@
     final_t[...] = mul_t(eye, final_w[...]).astype(BF16)
 
 
-def gate_kernel(norm_ref, gate_w, gate_ref):
-    for i in range(norm_ref.shape[0]):
-        gate_ref[i] = jax.nn.sigmoid(mul(gate_w[...], norm_ref[i]))
-
-
 def pair_kernel(sizes, held, scale, *refs):
     n_core, rows, n_dev = sizes[2], sizes[3], sizes[4]
     groups = refs[:-11]
@@ -376,10 +371,16 @@
         ]
         return [mul(shuffle, block).astype(BF16) for block in blocks]
 
+    copies = []
     for b, block in enumerate(by_channels(1)):
         right_ref[b * per * chunk : (b + 1) * per * chunk, :] = block
-    targets = [send_ref.at[pl.ds(h * half * chunk, half * chunk)] for h in range(2)]
-    copies = fetch(sems, [(right_ref, target) for target in targets])
+        if b % 2 == 1:
+            size = 2 * per * chunk
+            source = right_ref.at[pl.ds((b - 1) * per * chunk, size)]
+            for h in range(2):
+                target = send_ref.at[pl.ds((h * half + (b - 1) * per) * chunk, size)]
+                copies.append(pltpu.make_async_copy(source, target, sems.at[len(copies)]))
+                copies[-1].start()
     for b, block in enumerate(by_channels(0)):
         for d in range(per):
             to = (d % n_core * half + b * per + d) // n_core * chunk
@@ -432,7 +433,7 @@
         send_ref[dst * chunk : (dst + 1) * chunk, :] = total[dst].astype(BF16)
 
 
-def finish_kernel(sizes, recv_ref, mid_ref, gate_ref, out_w, out_ref, apart, done_ref, sems):
+def finish_kernel(sizes, recv_ref, mid_ref, norm_ref, gate_w, out_w, out_ref, apart, done_ref, sems):
     rows = sizes[3]
     _, width, cols = mid_ref.shape
     hidden = out_w.shape[1]
@@ -454,8 +455,9 @@
             apart[i, b * some : (b + 1) * some, :] = normed[i * some : (i + 1) * some]
     eye = identity(cols)
     copies = []
+    gates = [jax.nn.sigmoid(mul(gate_w[...], norm_ref[i])) for i in range(rows)]
     updates = [mul(out_w[...], apart[i]) for i in range(rows)]
-    dones = [(mid_ref[i].astype(F32) + gate_ref[i] * updates[i]).astype(BF16) for i in range(rows)]
+    dones = [(mid_ref[i].astype(F32) + gates[i] * updates[i]).astype(BF16) for i in range(rows)]
     for i in range(rows):
         done_ref[i] = mul_t(eye, dones[i]).astype(BF16)
         copies.append(pltpu.make_async_copy(done_ref.at[i], out_ref.at[i], sems.at[i]))
@@ -617,7 +619,7 @@
             pltpu.VMEM((rows, factor * factor, cols), BF16),
             pltpu.VMEM((2, rows, hidden, cols), BF16),
             pltpu.VMEM((hidden * rows, cols), BF16),
-            pltpu.SemaphoreType.DMA((2,)),
+            pltpu.SemaphoreType.DMA((hidden * rows // 256,)),
         ],
         16,
         4 * rows * cols * width * (factor * factor + hidden * 2),
@@ -626,15 +628,6 @@
         out_t,
         tri_t,
         far_out=(True, False, False, False),
-    )
-    (gate,) = call(
-        gate_kernel,
-        [((rows, width, cols), F32)],
-        [],
-        8,
-        2 * rows * cols * width * width,
-        normed,
-        gate_t,
     )
     recv = lax.all_to_all(send, BOTH, split_axis=0, concat_axis=0, tiled=True)
     mine = call(
@@ -678,7 +671,8 @@
         4 * rows * cols * width * hidden,
         recv,
         mid,
-        gate,
+        normed,
+        gate_t,
         final_t,
         far_out=True,
     )

time: 82.1 us -> 81.1 us (0.988)
  blocking collectives: 0 us -> 14.3 us
  waiting for transfers between devices: 36.4 us -> 26.1 us
  starting transfers between devices: 32.6 us -> 28.7 us
  Pallas kernels: 12.6 us -> 11.6 us
    all_to_all x0 -> x1, blocking collectives: none -> 14.3 us  [whole_channels(): lax.all_to_all(send, BOTH, split_axis=0, concat_axis=0, tiled=True, axis_...]
    all_to_all x1 -> x0, waiting for transfers between devices: 10.2 us -> none  [whole_channels(): lax.all_to_all(send, BOTH, split_axis=0, concat_axis=0, tiled=True, axis_...]
    all_to_all x1 -> x0, starting transfers between devices: 3.91 us -> none  [whole_channels(): lax.all_to_all(send, BOTH, split_axis=0, concat_axis=0, tiled=True, axis_...]
    pallas_call x9 -> x8, Pallas kernels: 12.6 us -> 11.6 us  [call(): pl.pallas_call(kernel, out_shape=out_shape, in_specs=[pl.BlockSpec(memory...]
  transfers between devices with their start and end apart: 21 -> 20, of which waited for: 13 -> 12; matrix products, arithmetic and copies ran while one was open for 0% -> 0% of each run, Pallas kernels for 4% -> 3%
where the time goes in v8:
time: 81.1 us; the launch traced here: 80.8 us
  starting transfers between devices  28.7 us (35%)
  waiting for transfers between devices  26.1 us (32%)
  blocking collectives  14.3 us (18%)
  Pallas kernels  11.6 us (14%)
    ppermute x19, waiting for transfers between devices, exchange(): return lax.ppermute(value, BOTH, pairs)  25.9 us
    ppermute x19, starting transfers between devices, exchange(): return lax.ppermute(value, BOTH, pairs)  25.6 us
    all_to_all x1, blocking collectives, whole_channels(): lax.all_to_all(send, BOTH, split_axis=0, concat_axis=0, tiled=True, axis_...  14.3 us
    pallas_call x8, Pallas kernels, call(): pl.pallas_call(kernel, out_shape=out_shape, in_specs=[pl.BlockSpec(memory...  11.6 us
    all_to_all x1, starting transfers between devices, whole_channels(): recv = lax.all_to_all(send, BOTH, split_axis=0, concat_axis=0, tiled=True)  3.12 us
  transfers between devices with their start and end apart: 20, of which 12 were waited for; matrix products, arithmetic and copies ran while one was open for 0% of the time, Pallas kernels for 3%

profile of v8, /device:TPU:0, one launch (start us, length us, event | category | flops | bytes accessed | tf_op | source)
XLA Modules:
  0.0 80.8 jit_solution(8857503112712360165)
XLA Ops:
  0.0 2.5 %shard_map.109 = (bf16[160,256]{1,0:T(8,128)(2,1)S(1)}, bf16[160,256]{1,0:T(8,128)(2,1)S(1)}, bf16[160,256]{1,0:T(8,128)(2,1)S(1)}, bf16[160,256]{1,0:T(8,128)(2,1)S(1)}) custom-call(bf16[4,256,256]{2,1,0:T(8,128)(2,1)} %align_in.1, bf16[32,256]{1,0:T(8,128)(2,1)} %bitcast.9, bf16[32,256]{1,0:T(8,128)(2,1)} %bitcast.10), custom_call_target="tpu_custom_call" | custom-call | flops 33554432 | bytes 884736 | tf_op jit(solution)/shard_map/pallas_call | solution.py:480
  2.5 5.1 %collective-permute-start = (bf16[160,256]{1,0:T(8,128)(2,1)S(1)}, bf16[160,256]{1,0:T(8,128)(2,1)S(1)}, u32[]{:S(2)}, u32[]{:S(2)}) collective-permute-start(bf16[160,256]{1,0:T(8,128)(2,1)S(1)} %get-tuple-element.57), channel_id=1, source_target_pairs={{0,24},{1,25},{2,26},{3,27},{4,28},{5,29},{6,30},{7,31},{8,16},{9,... | collective-permute-start | bytes 245768 | tf_op jit(solution)/shard_map/ppermute | solution.py:550
  7.6 0.6 collective-permute-start.2
  8.2 2.6 %collective-permute-start.3 = (bf16[160,256]{1,0:T(8,128)(2,1)S(1)}, bf16[160,256]{1,0:T(8,128)(2,1)S(1)}, u32[]{:S(2)}, u32[]{:S(2)}) collective-permute-start(bf16[160,256]{1,0:T(8,128)(2,1)S(1)} %get-tuple-element.73.refs_0_), channel_id=1, source_target_pairs={{0,6},{1,7},{2,4},{3,5},{4,2},{5,3},{6,0},{7,1},{8,14},{9,15},{10,... | collective-permute-start | bytes 245768 | tf_op jit(solution)/shard_map/ppermute | solution.py:550
  10.8 2.5 %shard_map.110 = (bf16[8,128,256]{2,1,0:T(8,128)(2,1)S(1)}, bf16[128,1024]{1,0:T(8,128)(2,1)S(1)}, bf16[512,128]{1,0:T(8,128)(2,1)S(1)}, bf16[128,128]{1,0:T(8,128)(2,1)S(1)}, bf16[128,128]{1,0:T(8,128)(2,1)S(1)}) custom-call(bf16[8,256,128]{2,1,0:T(8,128)(2,1)} %refs_0_, bf16[1024,128]{1,0:T(8,128)(2,1)} %refs_1_, bf16[128,128]{1,0:T(8,128)(2,1)} %refs_2_, ...), custom_call_target="tpu_custom_call" | custom-call | flops 134217728 | bytes 1966080 | tf_op jit(solution)/shard_map/pallas_call | solution.py:480
  13.3 1.2 %collective-permute-done.1.refs_2_ = bf16[160,256]{1,0:T(8,128)(2,1)S(1)} collective-permute-done((bf16[160,256]{1,0:T(8,128)(2,1)S(1)}, bf16[160,256]{1,0:T(8,128)(2,1)S(1)}, u32[]{:S(2)}, u32[]{:S(2)}) %collective-permute-start.1) | collective-permute-done | bytes 81952 | tf_op jit(solution)/shard_map/ppermute | solution.py:550
  14.4 0.3 shard_map.111
  14.7 1.6 %collective-permute-start.5 = (bf16[544,256]{1,0:T(8,128)(2,1)S(1)}, bf16[544,256]{1,0:T(8,128)(2,1)S(1)}, u32[]{:S(2)}, u32[]{:S(2)}) collective-permute-start(bf16[544,256]{1,0:T(8,128)(2,1)S(1)} %get-tuple-element.80), channel_id=1, source_target_pairs={{0,4},{1,5},{2,6},{3,7},{4,0},{5,1},{6,2},{7,3},{8,12},{9,13},{10,... | collective-permute-start | bytes 835592 | tf_op jit(solution)/shard_map/ppermute | solution.py:550
  16.3 1.5 %collective-permute-start.6 = (bf16[544,256]{1,0:T(8,128)(2,1)S(1)}, bf16[544,256]{1,0:T(8,128)(2,1)S(1)}, u32[]{:S(2)}, u32[]{:S(2)}) collective-permute-start(bf16[544,256]{1,0:T(8,128)(2,1)S(1)} %get-tuple-element.81), channel_id=1, source_target_pairs={{0,2},{1,3},{2,0},{3,1},{4,6},{5,7},{6,4},{7,5},{8,10},{9,11},{10,... | collective-permute-start | bytes 835592 | tf_op jit(solution)/shard_map/ppermute | solution.py:550
  17.8 0.5 collective-permute-start.4
  18.3 10.1 %collective-permute-done.4.late_ref = bf16[416,256]{1,0:T(8,128)(2,1)S(1)} collective-permute-done((bf16[416,256]{1,0:T(8,128)(2,1)S(1)}, bf16[416,256]{1,0:T(8,128)(2,1)S(1)}, u32[]{:S(2)}, u32[]{:S(2)}) %collective-permute-start.4) | collective-permute-done | bytes 213024 | tf_op jit(solution)/shard_map/ppermute | solution.py:550
  28.8 0.5 collective-permute-start.9
  29.3 1.0 %collective-permute-done.8.refs_5_ = bf16[544,256]{1,0:T(8,128)(2,1)S(1)} collective-permute-done((bf16[544,256]{1,0:T(8,128)(2,1)S(1)}, bf16[544,256]{1,0:T(8,128)(2,1)S(1)}, u32[]{:S(2)}, u32[]{:S(2)}) %collective-permute-start.8) | collective-permute-done | bytes 278560 | tf_op jit(solution)/shard_map/ppermute | solution.py:550
  30.3 0.4 collective-permute-done.9.refs_6_
  30.7 0.4 collective-permute-done.10.refs_7_
  31.1 3.6 %shard_map.113 = (bf16[2048,256]{1,0:T(8,128)(2,1)}, bf16[1024,256]{1,0:T(8,128)(2,1)S(1)}, bf16[8,128,256]{2,1,0:T(8,128)(2,1)S(1)}, bf16[8,128,256]{2,1,0:T(8,128)(2,1)S(1)}) custom-call(bf16[544,256]{1,0:T(8,128)(2,1)S(1)} %get-tuple-element.77.refs_0_, bf16[544,256]{1,0:T(8,128)(2,1)S(1)} %shard_map.112.refs_1_, ...), custom_call_target="tpu_custom_call" | custom-call | flops 1342177280 | bytes 5767168 | tf_op jit(solution)/shard_map/pallas_call | solution.py:480
  34.7 3.1 %all-to-all-start = ((bf16[32,64,256]{2,1,0:T(8,128)(2,1)}), bf16[32,64,256]{2,1,0:T(8,128)(2,1)S(1)}, u32[]{:S(2)}, u32[]{:S(2)}) async-start(bf16[32,64,256]{2,1,0:T(8,128)(2,1)} %bitcast.2), calls=%async_computation | async-start | bytes 2097152 | tf_op jit(solution)/shard_map/all_to_all | solution.py:632
  37.9 0.3 collective-permute-start.11
  38.2 1.7 %collective-permute-done.11.came_ref = bf16[1024,256]{1,0:T(8,128)(2,1)S(1)} collective-permute-done((bf16[1024,256]{1,0:T(8,128)(2,1)S(1)}, bf16[1024,256]{1,0:T(8,128)(2,1)S(1)}, u32[]{:S(2)}, u32[]{:S(2)}) %collective-permute-start.11) | collective-permute-done | bytes 524320 | tf_op jit(solution)/shard_map/ppermute | solution.py:550
  39.9 1.8 %collective-permute-start.12 = (bf16[128,256]{1,0:T(8,128)(2,1)S(1)}, bf16[128,256]{1,0:T(8,128)(2,1)S(1)}, u32[]{:S(2)}, u32[]{:S(2)}) collective-permute-start(bf16[128,256]{1,0:T(8,128)(2,1)S(1)} %get-tuple-element.88), channel_id=1, source_target_pairs={{0,2},{1,3},{2,0},{3,1},{4,6},{5,7},{6,4},{7,5},{8,10},{9,11},{10,... | collective-permute-start | bytes 196616 | tf_op jit(solution)/shard_map/ppermute | solution.py:550
  41.8 1.5 %collective-permute-start.13 = (bf16[128,256]{1,0:T(8,128)(2,1)S(1)}, bf16[128,256]{1,0:T(8,128)(2,1)S(1)}, u32[]{:S(2)}, u32[]{:S(2)}) collective-permute-start(bf16[128,256]{1,0:T(8,128)(2,1)S(1)} %get-tuple-element.89), channel_id=1, source_target_pairs={{0,4},{1,5},{2,6},{3,7},{4,0},{5,1},{6,2},{7,3},{8,12},{9,13},{10,... | collective-permute-start | bytes 196616 | tf_op jit(solution)/shard_map/ppermute | solution.py:550
  43.5 1.8 %collective-permute-start.15 = (bf16[128,256]{1,0:T(8,128)(2,1)S(1)}, bf16[128,256]{1,0:T(8,128)(2,1)S(1)}, u32[]{:S(2)}, u32[]{:S(2)}) collective-permute-start(bf16[128,256]{1,0:T(8,128)(2,1)S(1)} %get-tuple-element.91), channel_id=1, source_target_pairs={{0,8},{1,9},{2,10},{3,11},{4,12},{5,13},{6,14},{7,15},{8,0},{9,1},... | collective-permute-start | bytes 196616 | tf_op jit(solution)/shard_map/ppermute | solution.py:550
  45.3 1.5 %collective-permute-start.16 = (bf16[128,256]{1,0:T(8,128)(2,1)S(1)}, bf16[128,256]{1,0:T(8,128)(2,1)S(1)}, u32[]{:S(2)}, u32[]{:S(2)}) collective-permute-start(bf16[128,256]{1,0:T(8,128)(2,1)S(1)} %get-tuple-element.92), channel_id=1, source_target_pairs={{0,10},{1,11},{2,8},{3,9},{4,14},{5,15},{6,12},{7,13},{8,2},{9,3},... | collective-permute-start | bytes 196616 | tf_op jit(solution)/shard_map/ppermute | solution.py:550
  46.7 2.9 %collective-permute-done.12.refs_1_ = bf16[128,256]{1,0:T(8,128)(2,1)S(1)} collective-permute-done((bf16[128,256]{1,0:T(8,128)(2,1)S(1)}, bf16[128,256]{1,0:T(8,128)(2,1)S(1)}, u32[]{:S(2)}, u32[]{:S(2)}) %collective-permute-start.12) | collective-permute-done | bytes 65568 | tf_op jit(solution)/shard_map/ppermute | solution.py:550
  49.8 5.8 %collective-permute-start.18 = (bf16[128,256]{1,0:T(8,128)(2,1)S(1)}, bf16[128,256]{1,0:T(8,128)(2,1)S(1)}, u32[]{:S(2)}, u32[]{:S(2)}) collective-permute-start(bf16[128,256]{1,0:T(8,128)(2,1)S(1)} %get-tuple-element.94), channel_id=1, source_target_pairs={{0,14},{1,15},{2,12},{3,13},{4,10},{5,11},{6,8},{7,9},{8,6},{9,7},... | collective-permute-start | bytes 196616 | tf_op jit(solution)/shard_map/ppermute | solution.py:550
  55.6 1.6 %collective-permute-done.15.refs_4_ = bf16[128,256]{1,0:T(8,128)(2,1)S(1)} collective-permute-done((bf16[128,256]{1,0:T(8,128)(2,1)S(1)}, bf16[128,256]{1,0:T(8,128)(2,1)S(1)}, u32[]{:S(2)}, u32[]{:S(2)}) %collective-permute-start.15) | collective-permute-done | bytes 65568 | tf_op jit(solution)/shard_map/ppermute | solution.py:550
  57.2 1.5 %collective-permute-done.16.refs_5_ = bf16[128,256]{1,0:T(8,128)(2,1)S(1)} collective-permute-done((bf16[128,256]{1,0:T(8,128)(2,1)S(1)}, bf16[128,256]{1,0:T(8,128)(2,1)S(1)}, u32[]{:S(2)}, u32[]{:S(2)}) %collective-permute-start.16) | collective-permute-done | bytes 65568 | tf_op jit(solution)/shard_map/ppermute | solution.py:550
  58.7 2.2 %collective-permute-done.17.refs_6_ = bf16[128,256]{1,0:T(8,128)(2,1)S(1)} collective-permute-done((bf16[128,256]{1,0:T(8,128)(2,1)S(1)}, bf16[128,256]{1,0:T(8,128)(2,1)S(1)}, u32[]{:S(2)}, u32[]{:S(2)}) %collective-permute-start.17) | collective-permute-done | bytes 65568 | tf_op jit(solution)/shard_map/ppermute | solution.py:550
  60.8 3.0 %collective-permute-done.18.refs_7_ = bf16[128,256]{1,0:T(8,128)(2,1)S(1)} collective-permute-done((bf16[128,256]{1,0:T(8,128)(2,1)S(1)}, bf16[128,256]{1,0:T(8,128)(2,1)S(1)}, u32[]{:S(2)}, u32[]{:S(2)}) %collective-permute-start.18) | collective-permute-done | bytes 65568 | tf_op jit(solution)/shard_map/ppermute | solution.py:550
  64.1 0.5 shard_map.115
  64.6 14.3 %all_to_all.22 = bf16[16,64,256]{2,1,0:T(8,128)(2,1)S(1)} all-to-all(bf16[16,64,256]{2,1,0:T(8,128)(2,1)S(1)} %bitcast.7), channel_id=1, replica_groups={{0,1,2,3,4,5,6,7,8,9,10,11,12,13,14,15},{16,17,18,19,20,21,22,23,24,25,..., dimensions={0} | all-to-all | bytes 1048576 | tf_op jit(solution)/shard_map/all_to_all | solution.py:659
  78.8 2.0 %shard_map.116 = bf16[8,256,128]{2,1,0:T(8,128)(2,1)} custom-call(bf16[1024,256]{1,0:T(8,128)(2,1)S(1)} %bitcast.8, bf16[8,128,256]{2,1,0:T(8,128)(2,1)S(1)} %get-tuple-element.95.mid_ref, bf16[8,128,256]{2,1,0:T(8,128)(2,1)S(1)} %get-tuple-element.96.norm_ref, bf16[128,128]{1,0:T(8,128)(2,1)S(1)} %get-tuple-element.97.gate_w, ...), custom_call_target="tpu_custom_call" | custom-call | flops 134217728 | bytes 2162688 | tf_op jit(solution)/shard_map/pallas_call | solution.py:480
  (17 shorter events, 1.2 us)
Async XLA Ops:
  2.5 10.8 %collective-permute-start = (bf16[160,256]{1,0:T(8,128)(2,1)S(1)}, bf16[160,256]{1,0:T(8,128)(2,1)S(1)}, u32[]{:S(2)}, u32[]{:S(2)}) collective-permute-start(bf16[160,256]{1,0:T(8,128)(2,1)S(1)} %get-tuple-element.57), channel_id=1, source_target_pairs={{0,24},{1,25},{2,26},{3,27},{4,28},{5,29},{6,30},{7,31},{8,16},{9,... | collective-permute-start | bytes 245768 | tf_op jit(solution)/shard_map/ppermute | solution.py:550
  7.6 6.9 %collective-permute-start.1 = (bf16[160,256]{1,0:T(8,128)(2,1)S(1)}, bf16[160,256]{1,0:T(8,128)(2,1)S(1)}, u32[]{:S(2)}, u32[]{:S(2)}) collective-permute-start(bf16[160,256]{1,0:T(8,128)(2,1)S(1)} %get-tuple-element.58), channel_id=1, source_target_pairs={{0,16},{1,17},{2,18},{3,19},{4,20},{5,21},{6,22},{7,23},{8,24},{9,... | collective-permute-start | bytes 245768 | tf_op jit(solution)/shard_map/ppermute | solution.py:550
  7.6 6.9 %collective-permute-start.2 = (bf16[160,256]{1,0:T(8,128)(2,1)S(1)}, bf16[160,256]{1,0:T(8,128)(2,1)S(1)}, u32[]{:S(2)}, u32[]{:S(2)}) collective-permute-start(bf16[160,256]{1,0:T(8,128)(2,1)S(1)} %get-tuple-element.59), channel_id=1, source_target_pairs={{0,8},{1,9},{2,10},{3,11},{4,12},{5,13},{6,14},{7,15},{8,0},{9,1},... | collective-permute-start | bytes 245768 | tf_op jit(solution)/shard_map/ppermute | solution.py:550
  8.2 6.2 %collective-permute-start.3 = (bf16[160,256]{1,0:T(8,128)(2,1)S(1)}, bf16[160,256]{1,0:T(8,128)(2,1)S(1)}, u32[]{:S(2)}, u32[]{:S(2)}) collective-permute-start(bf16[160,256]{1,0:T(8,128)(2,1)S(1)} %get-tuple-element.73.refs_0_), channel_id=1, source_target_pairs={{0,6},{1,7},{2,4},{3,5},{4,2},{5,3},{6,0},{7,1},{8,14},{9,15},{10,... | collective-permute-start | bytes 245768 | tf_op jit(solution)/shard_map/ppermute | solution.py:550
  14.7 14.0 %collective-permute-start.5 = (bf16[544,256]{1,0:T(8,128)(2,1)S(1)}, bf16[544,256]{1,0:T(8,128)(2,1)S(1)}, u32[]{:S(2)}, u32[]{:S(2)}) collective-permute-start(bf16[544,256]{1,0:T(8,128)(2,1)S(1)} %get-tuple-element.80), channel_id=1, source_target_pairs={{0,4},{1,5},{2,6},{3,7},{4,0},{5,1},{6,2},{7,3},{8,12},{9,13},{10,... | collective-permute-start | bytes 835592 | tf_op jit(solution)/shard_map/ppermute | solution.py:550
  16.3 13.0 %collective-permute-start.6 = (bf16[544,256]{1,0:T(8,128)(2,1)S(1)}, bf16[544,256]{1,0:T(8,128)(2,1)S(1)}, u32[]{:S(2)}, u32[]{:S(2)}) collective-permute-start(bf16[544,256]{1,0:T(8,128)(2,1)S(1)} %get-tuple-element.81), channel_id=1, source_target_pairs={{0,2},{1,3},{2,0},{3,1},{4,6},{5,7},{6,4},{7,5},{8,10},{9,11},{10,... | collective-permute-start | bytes 835592 | tf_op jit(solution)/shard_map/ppermute | solution.py:550
  17.8 10.6 %collective-permute-start.4 = (bf16[416,256]{1,0:T(8,128)(2,1)S(1)}, bf16[416,256]{1,0:T(8,128)(2,1)S(1)}, u32[]{:S(2)}, u32[]{:S(2)}) collective-permute-start(bf16[416,256]{1,0:T(8,128)(2,1)S(1)} %get-tuple-element.79), channel_id=1, source_target_pairs={{0,6},{1,7},{2,4},{3,5},{4,2},{5,3},{6,0},{7,1},{8,14},{9,15},{10,... | collective-permute-start | bytes 638984 | tf_op jit(solution)/shard_map/ppermute | solution.py:550
  18.3 11.1 %collective-permute-start.7 = (bf16[544,256]{1,0:T(8,128)(2,1)S(1)}, bf16[544,256]{1,0:T(8,128)(2,1)S(1)}, u32[]{:S(2)}, u32[]{:S(2)}) collective-permute-start(bf16[544,256]{1,0:T(8,128)(2,1)S(1)} %get-tuple-element.77.refs_0_), channel_id=1, source_target_pairs={{0,1},{1,0},{2,3},{3,2},{4,5},{5,4},{6,7},{7,6},{8,9},{9,8},{10,11... | collective-permute-start | bytes 835592 | tf_op jit(solution)/shard_map/ppermute | solution.py:550
  28.7 1.6 %collective-permute-start.8 = (bf16[544,256]{1,0:T(8,128)(2,1)S(1)}, bf16[544,256]{1,0:T(8,128)(2,1)S(1)}, u32[]{:S(2)}, u32[]{:S(2)}) collective-permute-start(bf16[544,256]{1,0:T(8,128)(2,1)S(1)} %shard_map.112.refs_1_), channel_id=1, source_target_pairs={{0,1},{1,0},{2,3},{3,2},{4,5},{5,4},{6,7},{7,6},{8,9},{9,8},{10,11... | collective-permute-start | bytes 835592 | tf_op jit(solution)/shard_map/ppermute | solution.py:550
  28.8 1.9 %collective-permute-start.9 = (bf16[544,256]{1,0:T(8,128)(2,1)S(1)}, bf16[544,256]{1,0:T(8,128)(2,1)S(1)}, u32[]{:S(2)}, u32[]{:S(2)}) collective-permute-start(bf16[544,256]{1,0:T(8,128)(2,1)S(1)} %collective-permute-done.5.refs_2_), channel_id=1, source_target_pairs={{0,1},{1,0},{2,3},{3,2},{4,5},{5,4},{6,7},{7,6},{8,9},{9,8},{10,11... | collective-permute-start | bytes 835592 | tf_op jit(solution)/shard_map/ppermute | solution.py:550
  29.2 1.8 %collective-permute-start.10 = (bf16[544,256]{1,0:T(8,128)(2,1)S(1)}, bf16[544,256]{1,0:T(8,128)(2,1)S(1)}, u32[]{:S(2)}, u32[]{:S(2)}) collective-permute-start(bf16[544,256]{1,0:T(8,128)(2,1)S(1)} %collective-permute-done.6.refs_3_), channel_id=1, source_target_pairs={{0,1},{1,0},{2,3},{3,2},{4,5},{5,4},{6,7},{7,6},{8,9},{9,8},{10,11... | collective-permute-start | bytes 835592 | tf_op jit(solution)/shard_map/ppermute | solution.py:550
  34.7 29.4 %all-to-all-start = ((bf16[32,64,256]{2,1,0:T(8,128)(2,1)}), bf16[32,64,256]{2,1,0:T(8,128)(2,1)S(1)}, u32[]{:S(2)}, u32[]{:S(2)}) async-start(bf16[32,64,256]{2,1,0:T(8,128)(2,1)} %bitcast.2), calls=%async_computation | async-start | bytes 2097152 | tf_op jit(solution)/shard_map/all_to_all | solution.py:632
  37.9 2.0 %collective-permute-start.11 = (bf16[1024,256]{1,0:T(8,128)(2,1)S(1)}, bf16[1024,256]{1,0:T(8,128)(2,1)S(1)}, u32[]{:S(2)}, u32[]{:S(2)}) collective-permute-start(bf16[1024,256]{1,0:T(8,128)(2,1)S(1)} %get-tuple-element.86.own_ref), channel_id=1, source_target_pairs={{0,1},{1,0},{2,3},{3,2},{4,5},{5,4},{6,7},{7,6},{8,9},{9,8},{10,11... | collective-permute-start | bytes 1572872 | tf_op jit(solution)/shard_map/ppermute | solution.py:550
  39.9 9.7 %collective-permute-start.12 = (bf16[128,256]{1,0:T(8,128)(2,1)S(1)}, bf16[128,256]{1,0:T(8,128)(2,1)S(1)}, u32[]{:S(2)}, u32[]{:S(2)}) collective-permute-start(bf16[128,256]{1,0:T(8,128)(2,1)S(1)} %get-tuple-element.88), channel_id=1, source_target_pairs={{0,2},{1,3},{2,0},{3,1},{4,6},{5,7},{6,4},{7,5},{8,10},{9,11},{10,... | collective-permute-start | bytes 196616 | tf_op jit(solution)/shard_map/ppermute | solution.py:550
  41.8 8.0 %collective-permute-start.13 = (bf16[128,256]{1,0:T(8,128)(2,1)S(1)}, bf16[128,256]{1,0:T(8,128)(2,1)S(1)}, u32[]{:S(2)}, u32[]{:S(2)}) collective-permute-start(bf16[128,256]{1,0:T(8,128)(2,1)S(1)} %get-tuple-element.89), channel_id=1, source_target_pairs={{0,4},{1,5},{2,6},{3,7},{4,0},{5,1},{6,2},{7,3},{8,12},{9,13},{10,... | collective-permute-start | bytes 196616 | tf_op jit(solution)/shard_map/ppermute | solution.py:550
  43.2 12.4 %collective-permute-start.14 = (bf16[128,256]{1,0:T(8,128)(2,1)S(1)}, bf16[128,256]{1,0:T(8,128)(2,1)S(1)}, u32[]{:S(2)}, u32[]{:S(2)}) collective-permute-start(bf16[128,256]{1,0:T(8,128)(2,1)S(1)} %get-tuple-element.90), channel_id=1, source_target_pairs={{0,6},{1,7},{2,4},{3,5},{4,2},{5,3},{6,0},{7,1},{8,14},{9,15},{10,... | collective-permute-start | bytes 196616 | tf_op jit(solution)/shard_map/ppermute | solution.py:550
  43.5 13.7 %collective-permute-start.15 = (bf16[128,256]{1,0:T(8,128)(2,1)S(1)}, bf16[128,256]{1,0:T(8,128)(2,1)S(1)}, u32[]{:S(2)}, u32[]{:S(2)}) collective-permute-start(bf16[128,256]{1,0:T(8,128)(2,1)S(1)} %get-tuple-element.91), channel_id=1, source_target_pairs={{0,8},{1,9},{2,10},{3,11},{4,12},{5,13},{6,14},{7,15},{8,0},{9,1},... | collective-permute-start | bytes 196616 | tf_op jit(solution)/shard_map/ppermute | solution.py:550
  45.3 13.4 %collective-permute-start.16 = (bf16[128,256]{1,0:T(8,128)(2,1)S(1)}, bf16[128,256]{1,0:T(8,128)(2,1)S(1)}, u32[]{:S(2)}, u32[]{:S(2)}) collective-permute-start(bf16[128,256]{1,0:T(8,128)(2,1)S(1)} %get-tuple-element.92), channel_id=1, source_target_pairs={{0,10},{1,11},{2,8},{3,9},{4,14},{5,15},{6,12},{7,13},{8,2},{9,3},... | collective-permute-start | bytes 196616 | tf_op jit(solution)/shard_map/ppermute | solution.py:550
  49.6 11.2 %collective-permute-start.17 = (bf16[128,256]{1,0:T(8,128)(2,1)S(1)}, bf16[128,256]{1,0:T(8,128)(2,1)S(1)}, u32[]{:S(2)}, u32[]{:S(2)}) collective-permute-start(bf16[128,256]{1,0:T(8,128)(2,1)S(1)} %get-tuple-element.93), channel_id=1, source_target_pairs={{0,12},{1,13},{2,14},{3,15},{4,8},{5,9},{6,10},{7,11},{8,4},{9,5},... | collective-permute-start | bytes 196616 | tf_op jit(solution)/shard_map/ppermute | solution.py:550
  49.8 14.1 %collective-permute-start.18 = (bf16[128,256]{1,0:T(8,128)(2,1)S(1)}, bf16[128,256]{1,0:T(8,128)(2,1)S(1)}, u32[]{:S(2)}, u32[]{:S(2)}) collective-permute-start(bf16[128,256]{1,0:T(8,128)(2,1)S(1)} %get-tuple-element.94), channel_id=1, source_target_pairs={{0,14},{1,15},{2,12},{3,13},{4,10},{5,11},{6,8},{7,9},{8,6},{9,7},... | collective-permute-start | bytes 196616 | tf_op jit(solution)/shard_map/ppermute | solution.py:550

commit v9 on v8

--- a/solution.py
+++ b/solution.py
@@ -448,16 +448,18 @@
     spread = sum(jnp.sum((piece(b) - mean) ** 2, 0) for b in range(blocks)) * (1.0 / hidden)
     factor = lax.rsqrt(spread + EPS)
     shuffle = swap_rows(some, rows)
+    normed = [
+        ((piece(b) - mean) * factor).reshape(count, cols).astype(BF16) for b in range(blocks)
+    ]
+    normed = [mul(shuffle, block).astype(BF16) for block in normed]
     for b in range(blocks):
-        normed = ((piece(b) - mean) * factor).reshape(count, cols).astype(BF16)
-        normed = mul(shuffle, normed).astype(BF16)
         for i in range(rows):
-            apart[i, b * some : (b + 1) * some, :] = normed[i * some : (i + 1) * some]
+            apart[i, b * some : (b + 1) * some, :] = normed[b][i * some : (i + 1) * some]
     eye = identity(cols)
     copies = []
-    gates = [jax.nn.sigmoid(mul(gate_w[...], norm_ref[i])) for i in range(rows)]
+    gates = [mul(gate_w[...], norm_ref[i]) for i in range(rows)]
     updates = [mul(out_w[...], apart[i]) for i in range(rows)]
-    dones = [(mid_ref[i].astype(F32) + gates[i] * updates[i]).astype(BF16) for i in range(rows)]
+    dones = [(mid_ref[i].astype(F32) + jax.nn.sigmoid(gates[i]) * updates[i]).astype(BF16) for i in range(rows)]
     for i in range(rows):
         done_ref[i] = mul_t(eye, dones[i]).astype(BF16)
         copies.append(pltpu.make_async_copy(done_ref.at[i], out_ref.at[i], sems.at[i]))
@@ -566,7 +568,7 @@
 
     far = [exchange(mine[k], 2 * k, 0) for k in range(n_far - 1, 0, -1)]
     early = to_near(mine[0], n_near - 1)
-    far = [mine[0]] + far
+    far = [mine[0], far[0], far[2], far[1]]
     prepared = call(
         functools.partial(prepare_kernel, factor),
         [

time: 81.1 us -> 81 us (level)
  starting transfers between devices: 28.7 us -> 30.1 us
  waiting for transfers between devices: 26.1 us -> 24.8 us
    all_to_all x1, starting transfers between devices: 3.12 us -> 4.45 us  [whole_channels(): recv = lax.all_to_all(send, BOTH, split_axis=0, concat_axis=0, tiled=True)]
    ppermute x19, waiting for transfers between devices: 25.9 us -> 24.6 us  [exchange(): return lax.ppermute(value, BOTH, pairs)]
where the time goes in v9:
time: 81 us; the launch traced here: 80.8 us
  starting transfers between devices  30.1 us (37%)
  waiting for transfers between devices  24.8 us (31%)
  blocking collectives  14.3 us (18%)
  Pallas kernels  11.5 us (14%)
    ppermute x19, starting transfers between devices, exchange(): return lax.ppermute(value, BOTH, pairs)  25.6 us
    ppermute x19, waiting for transfers between devices, exchange(): return lax.ppermute(value, BOTH, pairs)  24.6 us
    all_to_all x1, blocking collectives, whole_channels(): lax.all_to_all(send, BOTH, split_axis=0, concat_axis=0, tiled=True, axis_...  14.3 us
    pallas_call x8, Pallas kernels, call(): pl.pallas_call(kernel, out_shape=out_shape, in_specs=[pl.BlockSpec(memory...  11.5 us
    all_to_all x1, starting transfers between devices, whole_channels(): recv = lax.all_to_all(send, BOTH, split_axis=0, concat_axis=0, tiled=True)  4.45 us
  transfers between devices with their start and end apart: 20, of which 12 were waited for; matrix products, arithmetic and copies ran while one was open for 0% of the time, Pallas kernels for 3%

profile of v9, /device:TPU:0, one launch (start us, length us, event | category | flops | bytes accessed | tf_op | source)
XLA Modules:
  0.0 80.8 jit_solution(14509097341017696258)
XLA Ops:
  0.0 2.5 %shard_map.109 = (bf16[160,256]{1,0:T(8,128)(2,1)S(1)}, bf16[160,256]{1,0:T(8,128)(2,1)S(1)}, bf16[160,256]{1,0:T(8,128)(2,1)S(1)}, bf16[160,256]{1,0:T(8,128)(2,1)S(1)}) custom-call(bf16[4,256,256]{2,1,0:T(8,128)(2,1)} %align_in.1, bf16[32,256]{1,0:T(8,128)(2,1)} %bitcast.9, bf16[32,256]{1,0:T(8,128)(2,1)} %bitcast.10), custom_call_target="tpu_custom_call" | custom-call | flops 33554432 | bytes 884736 | tf_op jit(solution)/shard_map/pallas_call | solution.py:482
  2.5 5.1 %collective-permute-start = (bf16[160,256]{1,0:T(8,128)(2,1)S(1)}, bf16[160,256]{1,0:T(8,128)(2,1)S(1)}, u32[]{:S(2)}, u32[]{:S(2)}) collective-permute-start(bf16[160,256]{1,0:T(8,128)(2,1)S(1)} %get-tuple-element.57), channel_id=1, source_target_pairs={{0,24},{1,25},{2,26},{3,27},{4,28},{5,29},{6,30},{7,31},{8,16},{9,... | collective-permute-start | bytes 245768 | tf_op jit(solution)/shard_map/ppermute | solution.py:552
  7.6 0.6 collective-permute-start.2
  8.2 2.6 %collective-permute-start.3 = (bf16[160,256]{1,0:T(8,128)(2,1)S(1)}, bf16[160,256]{1,0:T(8,128)(2,1)S(1)}, u32[]{:S(2)}, u32[]{:S(2)}) collective-permute-start(bf16[160,256]{1,0:T(8,128)(2,1)S(1)} %get-tuple-element.73.refs_0_), channel_id=1, source_target_pairs={{0,6},{1,7},{2,4},{3,5},{4,2},{5,3},{6,0},{7,1},{8,14},{9,15},{10,... | collective-permute-start | bytes 245768 | tf_op jit(solution)/shard_map/ppermute | solution.py:552
  10.8 2.5 %shard_map.110 = (bf16[8,128,256]{2,1,0:T(8,128)(2,1)S(1)}, bf16[128,1024]{1,0:T(8,128)(2,1)S(1)}, bf16[512,128]{1,0:T(8,128)(2,1)S(1)}, bf16[128,128]{1,0:T(8,128)(2,1)S(1)}, bf16[128,128]{1,0:T(8,128)(2,1)S(1)}) custom-call(bf16[8,256,128]{2,1,0:T(8,128)(2,1)} %refs_0_, bf16[1024,128]{1,0:T(8,128)(2,1)} %refs_1_, bf16[128,128]{1,0:T(8,128)(2,1)} %refs_2_, ...), custom_call_target="tpu_custom_call" | custom-call | flops 134217728 | bytes 1966080 | tf_op jit(solution)/shard_map/pallas_call | solution.py:482
  13.3 0.5 collective-permute-done.1.refs_2_
  13.8 0.3 shard_map.111
  14.1 1.7 %collective-permute-start.5 = (bf16[544,256]{1,0:T(8,128)(2,1)S(1)}, bf16[544,256]{1,0:T(8,128)(2,1)S(1)}, u32[]{:S(2)}, u32[]{:S(2)}) collective-permute-start(bf16[544,256]{1,0:T(8,128)(2,1)S(1)} %get-tuple-element.80), channel_id=1, source_target_pairs={{0,4},{1,5},{2,6},{3,7},{4,0},{5,1},{6,2},{7,3},{8,12},{9,13},{10,... | collective-permute-start | bytes 835592 | tf_op jit(solution)/shard_map/ppermute | solution.py:552
  15.8 1.5 %collective-permute-start.6 = (bf16[544,256]{1,0:T(8,128)(2,1)S(1)}, bf16[544,256]{1,0:T(8,128)(2,1)S(1)}, u32[]{:S(2)}, u32[]{:S(2)}) collective-permute-start(bf16[544,256]{1,0:T(8,128)(2,1)S(1)} %get-tuple-element.81), channel_id=1, source_target_pairs={{0,2},{1,3},{2,0},{3,1},{4,6},{5,7},{6,4},{7,5},{8,10},{9,11},{10,... | collective-permute-start | bytes 835592 | tf_op jit(solution)/shard_map/ppermute | solution.py:552
  17.3 0.4 collective-permute-start.4
  17.7 9.4 %collective-permute-done.4.late_ref = bf16[416,256]{1,0:T(8,128)(2,1)S(1)} collective-permute-done((bf16[416,256]{1,0:T(8,128)(2,1)S(1)}, bf16[416,256]{1,0:T(8,128)(2,1)S(1)}, u32[]{:S(2)}, u32[]{:S(2)}) %collective-permute-start.4) | collective-permute-done | bytes 213024 | tf_op jit(solution)/shard_map/ppermute | solution.py:552
  27.4 0.5 collective-permute-start.9
  28.0 1.0 %collective-permute-done.8.refs_5_ = bf16[544,256]{1,0:T(8,128)(2,1)S(1)} collective-permute-done((bf16[544,256]{1,0:T(8,128)(2,1)S(1)}, bf16[544,256]{1,0:T(8,128)(2,1)S(1)}, u32[]{:S(2)}, u32[]{:S(2)}) %collective-permute-start.8) | collective-permute-done | bytes 278560 | tf_op jit(solution)/shard_map/ppermute | solution.py:552
  29.0 0.4 collective-permute-done.9.refs_6_
  29.4 0.4 collective-permute-done.10.refs_7_
  29.8 3.6 %shard_map.113 = (bf16[2048,256]{1,0:T(8,128)(2,1)}, bf16[1024,256]{1,0:T(8,128)(2,1)S(1)}, bf16[8,128,256]{2,1,0:T(8,128)(2,1)S(1)}, bf16[8,128,256]{2,1,0:T(8,128)(2,1)S(1)}) custom-call(bf16[544,256]{1,0:T(8,128)(2,1)S(1)} %get-tuple-element.77.refs_0_, bf16[544,256]{1,0:T(8,128)(2,1)S(1)} %shard_map.112.refs_1_, ...), custom_call_target="tpu_custom_call" | custom-call | flops 1342177280 | bytes 5767168 | tf_op jit(solution)/shard_map/pallas_call | solution.py:482
  33.4 4.5 %all-to-all-start = ((bf16[32,64,256]{2,1,0:T(8,128)(2,1)}), bf16[32,64,256]{2,1,0:T(8,128)(2,1)S(1)}, u32[]{:S(2)}, u32[]{:S(2)}) async-start(bf16[32,64,256]{2,1,0:T(8,128)(2,1)} %bitcast.2), calls=%async_computation | async-start | bytes 2097152 | tf_op jit(solution)/shard_map/all_to_all | solution.py:634
  37.9 0.3 collective-permute-start.11
  38.2 1.7 %collective-permute-done.11.came_ref = bf16[1024,256]{1,0:T(8,128)(2,1)S(1)} collective-permute-done((bf16[1024,256]{1,0:T(8,128)(2,1)S(1)}, bf16[1024,256]{1,0:T(8,128)(2,1)S(1)}, u32[]{:S(2)}, u32[]{:S(2)}) %collective-permute-start.11) | collective-permute-done | bytes 524320 | tf_op jit(solution)/shard_map/ppermute | solution.py:552
  39.9 1.8 %collective-permute-start.12 = (bf16[128,256]{1,0:T(8,128)(2,1)S(1)}, bf16[128,256]{1,0:T(8,128)(2,1)S(1)}, u32[]{:S(2)}, u32[]{:S(2)}) collective-permute-start(bf16[128,256]{1,0:T(8,128)(2,1)S(1)} %get-tuple-element.88), channel_id=1, source_target_pairs={{0,2},{1,3},{2,0},{3,1},{4,6},{5,7},{6,4},{7,5},{8,10},{9,11},{10,... | collective-permute-start | bytes 196616 | tf_op jit(solution)/shard_map/ppermute | solution.py:552
  41.8 1.5 %collective-permute-start.13 = (bf16[128,256]{1,0:T(8,128)(2,1)S(1)}, bf16[128,256]{1,0:T(8,128)(2,1)S(1)}, u32[]{:S(2)}, u32[]{:S(2)}) collective-permute-start(bf16[128,256]{1,0:T(8,128)(2,1)S(1)} %get-tuple-element.89), channel_id=1, source_target_pairs={{0,4},{1,5},{2,6},{3,7},{4,0},{5,1},{6,2},{7,3},{8,12},{9,13},{10,... | collective-permute-start | bytes 196616 | tf_op jit(solution)/shard_map/ppermute | solution.py:552
  43.5 1.8 %collective-permute-start.15 = (bf16[128,256]{1,0:T(8,128)(2,1)S(1)}, bf16[128,256]{1,0:T(8,128)(2,1)S(1)}, u32[]{:S(2)}, u32[]{:S(2)}) collective-permute-start(bf16[128,256]{1,0:T(8,128)(2,1)S(1)} %get-tuple-element.91), channel_id=1, source_target_pairs={{0,8},{1,9},{2,10},{3,11},{4,12},{5,13},{6,14},{7,15},{8,0},{9,1},... | collective-permute-start | bytes 196616 | tf_op jit(solution)/shard_map/ppermute | solution.py:552
  45.2 1.5 %collective-permute-start.16 = (bf16[128,256]{1,0:T(8,128)(2,1)S(1)}, bf16[128,256]{1,0:T(8,128)(2,1)S(1)}, u32[]{:S(2)}, u32[]{:S(2)}) collective-permute-start(bf16[128,256]{1,0:T(8,128)(2,1)S(1)} %get-tuple-element.92), channel_id=1, source_target_pairs={{0,10},{1,11},{2,8},{3,9},{4,14},{5,15},{6,12},{7,13},{8,2},{9,3},... | collective-permute-start | bytes 196616 | tf_op jit(solution)/shard_map/ppermute | solution.py:552
  46.7 2.9 %collective-permute-done.12.refs_1_ = bf16[128,256]{1,0:T(8,128)(2,1)S(1)} collective-permute-done((bf16[128,256]{1,0:T(8,128)(2,1)S(1)}, bf16[128,256]{1,0:T(8,128)(2,1)S(1)}, u32[]{:S(2)}, u32[]{:S(2)}) %collective-permute-start.12) | collective-permute-done | bytes 65568 | tf_op jit(solution)/shard_map/ppermute | solution.py:552
  49.8 5.8 %collective-permute-start.18 = (bf16[128,256]{1,0:T(8,128)(2,1)S(1)}, bf16[128,256]{1,0:T(8,128)(2,1)S(1)}, u32[]{:S(2)}, u32[]{:S(2)}) collective-permute-start(bf16[128,256]{1,0:T(8,128)(2,1)S(1)} %get-tuple-element.94), channel_id=1, source_target_pairs={{0,14},{1,15},{2,12},{3,13},{4,10},{5,11},{6,8},{7,9},{8,6},{9,7},... | collective-permute-start | bytes 196616 | tf_op jit(solution)/shard_map/ppermute | solution.py:552
  55.6 1.6 %collective-permute-done.15.refs_4_ = bf16[128,256]{1,0:T(8,128)(2,1)S(1)} collective-permute-done((bf16[128,256]{1,0:T(8,128)(2,1)S(1)}, bf16[128,256]{1,0:T(8,128)(2,1)S(1)}, u32[]{:S(2)}, u32[]{:S(2)}) %collective-permute-start.15) | collective-permute-done | bytes 65568 | tf_op jit(solution)/shard_map/ppermute | solution.py:552
  57.2 1.5 %collective-permute-done.16.refs_5_ = bf16[128,256]{1,0:T(8,128)(2,1)S(1)} collective-permute-done((bf16[128,256]{1,0:T(8,128)(2,1)S(1)}, bf16[128,256]{1,0:T(8,128)(2,1)S(1)}, u32[]{:S(2)}, u32[]{:S(2)}) %collective-permute-start.16) | collective-permute-done | bytes 65568 | tf_op jit(solution)/shard_map/ppermute | solution.py:552
  58.7 2.2 %collective-permute-done.17.refs_6_ = bf16[128,256]{1,0:T(8,128)(2,1)S(1)} collective-permute-done((bf16[128,256]{1,0:T(8,128)(2,1)S(1)}, bf16[128,256]{1,0:T(8,128)(2,1)S(1)}, u32[]{:S(2)}, u32[]{:S(2)}) %collective-permute-start.17) | collective-permute-done | bytes 65568 | tf_op jit(solution)/shard_map/ppermute | solution.py:552
  60.8 3.0 %collective-permute-done.18.refs_7_ = bf16[128,256]{1,0:T(8,128)(2,1)S(1)} collective-permute-done((bf16[128,256]{1,0:T(8,128)(2,1)S(1)}, bf16[128,256]{1,0:T(8,128)(2,1)S(1)}, u32[]{:S(2)}, u32[]{:S(2)}) %collective-permute-start.18) | collective-permute-done | bytes 65568 | tf_op jit(solution)/shard_map/ppermute | solution.py:552
  64.1 0.5 shard_map.115
  64.6 14.3 %all_to_all.22 = bf16[16,64,256]{2,1,0:T(8,128)(2,1)S(1)} all-to-all(bf16[16,64,256]{2,1,0:T(8,128)(2,1)S(1)} %bitcast.7), channel_id=1, replica_groups={{0,1,2,3,4,5,6,7,8,9,10,11,12,13,14,15},{16,17,18,19,20,21,22,23,24,25,..., dimensions={0} | all-to-all | bytes 1048576 | tf_op jit(solution)/shard_map/all_to_all | solution.py:661
  78.8 1.9 %shard_map.116 = bf16[8,256,128]{2,1,0:T(8,128)(2,1)} custom-call(bf16[1024,256]{1,0:T(8,128)(2,1)S(1)} %bitcast.8, bf16[8,128,256]{2,1,0:T(8,128)(2,1)S(1)} %get-tuple-element.95.mid_ref, bf16[8,128,256]{2,1,0:T(8,128)(2,1)S(1)} %get-tuple-element.96.norm_ref, bf16[128,128]{1,0:T(8,128)(2,1)S(1)} %get-tuple-element.97.gate_w, ...), custom_call_target="tpu_custom_call" | custom-call | flops 134217728 | bytes 2162688 | tf_op jit(solution)/shard_map/pallas_call | solution.py:482
  (17 shorter events, 1.1 us)
Async XLA Ops:
  2.5 10.8 %collective-permute-start = (bf16[160,256]{1,0:T(8,128)(2,1)S(1)}, bf16[160,256]{1,0:T(8,128)(2,1)S(1)}, u32[]{:S(2)}, u32[]{:S(2)}) collective-permute-start(bf16[160,256]{1,0:T(8,128)(2,1)S(1)} %get-tuple-element.57), channel_id=1, source_target_pairs={{0,24},{1,25},{2,26},{3,27},{4,28},{5,29},{6,30},{7,31},{8,16},{9,... | collective-permute-start | bytes 245768 | tf_op jit(solution)/shard_map/ppermute | solution.py:552
  7.6 6.2 %collective-permute-start.1 = (bf16[160,256]{1,0:T(8,128)(2,1)S(1)}, bf16[160,256]{1,0:T(8,128)(2,1)S(1)}, u32[]{:S(2)}, u32[]{:S(2)}) collective-permute-start(bf16[160,256]{1,0:T(8,128)(2,1)S(1)} %get-tuple-element.58), channel_id=1, source_target_pairs={{0,8},{1,9},{2,10},{3,11},{4,12},{5,13},{6,14},{7,15},{8,0},{9,1},... | collective-permute-start | bytes 245768 | tf_op jit(solution)/shard_map/ppermute | solution.py:552
  7.6 6.2 %collective-permute-start.2 = (bf16[160,256]{1,0:T(8,128)(2,1)S(1)}, bf16[160,256]{1,0:T(8,128)(2,1)S(1)}, u32[]{:S(2)}, u32[]{:S(2)}) collective-permute-start(bf16[160,256]{1,0:T(8,128)(2,1)S(1)} %get-tuple-element.59), channel_id=1, source_target_pairs={{0,16},{1,17},{2,18},{3,19},{4,20},{5,21},{6,22},{7,23},{8,24},{9,... | collective-permute-start | bytes 245768 | tf_op jit(solution)/shard_map/ppermute | solution.py:552
  8.2 5.6 %collective-permute-start.3 = (bf16[160,256]{1,0:T(8,128)(2,1)S(1)}, bf16[160,256]{1,0:T(8,128)(2,1)S(1)}, u32[]{:S(2)}, u32[]{:S(2)}) collective-permute-start(bf16[160,256]{1,0:T(8,128)(2,1)S(1)} %get-tuple-element.73.refs_0_), channel_id=1, source_target_pairs={{0,6},{1,7},{2,4},{3,5},{4,2},{5,3},{6,0},{7,1},{8,14},{9,15},{10,... | collective-permute-start | bytes 245768 | tf_op jit(solution)/shard_map/ppermute | solution.py:552
  14.1 13.3 %collective-permute-start.5 = (bf16[544,256]{1,0:T(8,128)(2,1)S(1)}, bf16[544,256]{1,0:T(8,128)(2,1)S(1)}, u32[]{:S(2)}, u32[]{:S(2)}) collective-permute-start(bf16[544,256]{1,0:T(8,128)(2,1)S(1)} %get-tuple-element.80), channel_id=1, source_target_pairs={{0,4},{1,5},{2,6},{3,7},{4,0},{5,1},{6,2},{7,3},{8,12},{9,13},{10,... | collective-permute-start | bytes 835592 | tf_op jit(solution)/shard_map/ppermute | solution.py:552
  15.8 12.1 %collective-permute-start.6 = (bf16[544,256]{1,0:T(8,128)(2,1)S(1)}, bf16[544,256]{1,0:T(8,128)(2,1)S(1)}, u32[]{:S(2)}, u32[]{:S(2)}) collective-permute-start(bf16[544,256]{1,0:T(8,128)(2,1)S(1)} %get-tuple-element.81), channel_id=1, source_target_pairs={{0,2},{1,3},{2,0},{3,1},{4,6},{5,7},{6,4},{7,5},{8,10},{9,11},{10,... | collective-permute-start | bytes 835592 | tf_op jit(solution)/shard_map/ppermute | solution.py:552
  17.3 9.8 %collective-permute-start.4 = (bf16[416,256]{1,0:T(8,128)(2,1)S(1)}, bf16[416,256]{1,0:T(8,128)(2,1)S(1)}, u32[]{:S(2)}, u32[]{:S(2)}) collective-permute-start(bf16[416,256]{1,0:T(8,128)(2,1)S(1)} %get-tuple-element.79), channel_id=1, source_target_pairs={{0,6},{1,7},{2,4},{3,5},{4,2},{5,3},{6,0},{7,1},{8,14},{9,15},{10,... | collective-permute-start | bytes 638984 | tf_op jit(solution)/shard_map/ppermute | solution.py:552
  17.6 10.4 %collective-permute-start.7 = (bf16[544,256]{1,0:T(8,128)(2,1)S(1)}, bf16[544,256]{1,0:T(8,128)(2,1)S(1)}, u32[]{:S(2)}, u32[]{:S(2)}) collective-permute-start(bf16[544,256]{1,0:T(8,128)(2,1)S(1)} %get-tuple-element.77.refs_0_), channel_id=1, source_target_pairs={{0,1},{1,0},{2,3},{3,2},{4,5},{5,4},{6,7},{7,6},{8,9},{9,8},{10,11... | collective-permute-start | bytes 835592 | tf_op jit(solution)/shard_map/ppermute | solution.py:552
  27.3 1.6 %collective-permute-start.8 = (bf16[544,256]{1,0:T(8,128)(2,1)S(1)}, bf16[544,256]{1,0:T(8,128)(2,1)S(1)}, u32[]{:S(2)}, u32[]{:S(2)}) collective-permute-start(bf16[544,256]{1,0:T(8,128)(2,1)S(1)} %shard_map.112.refs_1_), channel_id=1, source_target_pairs={{0,1},{1,0},{2,3},{3,2},{4,5},{5,4},{6,7},{7,6},{8,9},{9,8},{10,11... | collective-permute-start | bytes 835592 | tf_op jit(solution)/shard_map/ppermute | solution.py:552
  27.4 1.9 %collective-permute-start.9 = (bf16[544,256]{1,0:T(8,128)(2,1)S(1)}, bf16[544,256]{1,0:T(8,128)(2,1)S(1)}, u32[]{:S(2)}, u32[]{:S(2)}) collective-permute-start(bf16[544,256]{1,0:T(8,128)(2,1)S(1)} %collective-permute-done.5.refs_2_), channel_id=1, source_target_pairs={{0,1},{1,0},{2,3},{3,2},{4,5},{5,4},{6,7},{7,6},{8,9},{9,8},{10,11... | collective-permute-start | bytes 835592 | tf_op jit(solution)/shard_map/ppermute | solution.py:552
  27.9 1.8 %collective-permute-start.10 = (bf16[544,256]{1,0:T(8,128)(2,1)S(1)}, bf16[544,256]{1,0:T(8,128)(2,1)S(1)}, u32[]{:S(2)}, u32[]{:S(2)}) collective-permute-start(bf16[544,256]{1,0:T(8,128)(2,1)S(1)} %collective-permute-done.6.refs_3_), channel_id=1, source_target_pairs={{0,1},{1,0},{2,3},{3,2},{4,5},{5,4},{6,7},{7,6},{8,9},{9,8},{10,11... | collective-permute-start | bytes 835592 | tf_op jit(solution)/shard_map/ppermute | solution.py:552
  33.4 30.7 %all-to-all-start = ((bf16[32,64,256]{2,1,0:T(8,128)(2,1)}), bf16[32,64,256]{2,1,0:T(8,128)(2,1)S(1)}, u32[]{:S(2)}, u32[]{:S(2)}) async-start(bf16[32,64,256]{2,1,0:T(8,128)(2,1)} %bitcast.2), calls=%async_computation | async-start | bytes 2097152 | tf_op jit(solution)/shard_map/all_to_all | solution.py:634
  37.9 2.0 %collective-permute-start.11 = (bf16[1024,256]{1,0:T(8,128)(2,1)S(1)}, bf16[1024,256]{1,0:T(8,128)(2,1)S(1)}, u32[]{:S(2)}, u32[]{:S(2)}) collective-permute-start(bf16[1024,256]{1,0:T(8,128)(2,1)S(1)} %get-tuple-element.86.own_ref), channel_id=1, source_target_pairs={{0,1},{1,0},{2,3},{3,2},{4,5},{5,4},{6,7},{7,6},{8,9},{9,8},{10,11... | collective-permute-start | bytes 1572872 | tf_op jit(solution)/shard_map/ppermute | solution.py:552
  39.9 9.7 %collective-permute-start.12 = (bf16[128,256]{1,0:T(8,128)(2,1)S(1)}, bf16[128,256]{1,0:T(8,128)(2,1)S(1)}, u32[]{:S(2)}, u32[]{:S(2)}) collective-permute-start(bf16[128,256]{1,0:T(8,128)(2,1)S(1)} %get-tuple-element.88), channel_id=1, source_target_pairs={{0,2},{1,3},{2,0},{3,1},{4,6},{5,7},{6,4},{7,5},{8,10},{9,11},{10,... | collective-permute-start | bytes 196616 | tf_op jit(solution)/shard_map/ppermute | solution.py:552
  41.8 8.0 %collective-permute-start.13 = (bf16[128,256]{1,0:T(8,128)(2,1)S(1)}, bf16[128,256]{1,0:T(8,128)(2,1)S(1)}, u32[]{:S(2)}, u32[]{:S(2)}) collective-permute-start(bf16[128,256]{1,0:T(8,128)(2,1)S(1)} %get-tuple-element.89), channel_id=1, source_target_pairs={{0,4},{1,5},{2,6},{3,7},{4,0},{5,1},{6,2},{7,3},{8,12},{9,13},{10,... | collective-permute-start | bytes 196616 | tf_op jit(solution)/shard_map/ppermute | solution.py:552
  43.2 12.4 %collective-permute-start.14 = (bf16[128,256]{1,0:T(8,128)(2,1)S(1)}, bf16[128,256]{1,0:T(8,128)(2,1)S(1)}, u32[]{:S(2)}, u32[]{:S(2)}) collective-permute-start(bf16[128,256]{1,0:T(8,128)(2,1)S(1)} %get-tuple-element.90), channel_id=1, source_target_pairs={{0,6},{1,7},{2,4},{3,5},{4,2},{5,3},{6,0},{7,1},{8,14},{9,15},{10,... | collective-permute-start | bytes 196616 | tf_op jit(solution)/shard_map/ppermute | solution.py:552
  43.5 13.7 %collective-permute-start.15 = (bf16[128,256]{1,0:T(8,128)(2,1)S(1)}, bf16[128,256]{1,0:T(8,128)(2,1)S(1)}, u32[]{:S(2)}, u32[]{:S(2)}) collective-permute-start(bf16[128,256]{1,0:T(8,128)(2,1)S(1)} %get-tuple-element.91), channel_id=1, source_target_pairs={{0,8},{1,9},{2,10},{3,11},{4,12},{5,13},{6,14},{7,15},{8,0},{9,1},... | collective-permute-start | bytes 196616 | tf_op jit(solution)/shard_map/ppermute | solution.py:552
  45.2 13.4 %collective-permute-start.16 = (bf16[128,256]{1,0:T(8,128)(2,1)S(1)}, bf16[128,256]{1,0:T(8,128)(2,1)S(1)}, u32[]{:S(2)}, u32[]{:S(2)}) collective-permute-start(bf16[128,256]{1,0:T(8,128)(2,1)S(1)} %get-tuple-element.92), channel_id=1, source_target_pairs={{0,10},{1,11},{2,8},{3,9},{4,14},{5,15},{6,12},{7,13},{8,2},{9,3},... | collective-permute-start | bytes 196616 | tf_op jit(solution)/shard_map/ppermute | solution.py:552
  49.6 11.2 %collective-permute-start.17 = (bf16[128,256]{1,0:T(8,128)(2,1)S(1)}, bf16[128,256]{1,0:T(8,128)(2,1)S(1)}, u32[]{:S(2)}, u32[]{:S(2)}) collective-permute-start(bf16[128,256]{1,0:T(8,128)(2,1)S(1)} %get-tuple-element.93), channel_id=1, source_target_pairs={{0,12},{1,13},{2,14},{3,15},{4,8},{5,9},{6,10},{7,11},{8,4},{9,5},... | collective-permute-start | bytes 196616 | tf_op jit(solution)/shard_map/ppermute | solution.py:552
  49.8 14.1 %collective-permute-start.18 = (bf16[128,256]{1,0:T(8,128)(2,1)S(1)}, bf16[128,256]{1,0:T(8,128)(2,1)S(1)}, u32[]{:S(2)}, u32[]{:S(2)}) collective-permute-start(bf16[128,256]{1,0:T(8,128)(2,1)S(1)} %get-tuple-element.94), channel_id=1, source_target_pairs={{0,14},{1,15},{2,12},{3,13},{4,10},{5,11},{6,8},{7,9},{8,6},{9,7},... | collective-permute-start | bytes 196616 | tf_op jit(solution)/shard_map/ppermute | solution.py:552

commit v10 on v9

--- a/solution.py
+++ b/solution.py
@@ -347,9 +347,12 @@
             for p in range(0, factor, 16):
                 at = (q // 16 * (factor // 16) + p // 16) * 256 + q % 16 * 16
                 outer[i, at : at + 16, :] = block[i * factor + p : i * factor + p + 16]
-    updates = [mul(out_w[...], outer[i]) for i in range(rows)]
+    updates = [
+        mul(out_w[...], jnp.concatenate([outer[i], outer[i + 1]], 1)) for i in range(0, rows, 2)
+    ]
+    cols = pair_ref.shape[2]
     for i in range(rows):
-        update = updates[i]
+        update = updates[i // 2][:, i % 2 * cols : (i % 2 + 1) * cols]
         mid = (pair_ref[i].astype(F32) + update * scale).astype(BF16)
         mid_ref[i] = mid
         normed = normalize(mid.astype(F32), 0).astype(BF16)
@@ -584,7 +587,7 @@
         *weights,
         far_in=True,
     )
-    far, early, prepared = lax.optimization_barrier((far, early, prepared))
+    early, far, prepared = lax.optimization_barrier((early, far, prepared))
     pair_t, out_t, tri_t, gate_t, final_t = prepared
     message = ((factor + n_core) * held, cols)
     late = ((n_far - 1) * seqs * factor + n_core * held, cols)

time: 81 us -> 81 us (level)
  no operation moved by 1% of the time
where the time goes in v10:
time: 81 us; the launch traced here: 80.8 us
  starting transfers between devices  30.1 us (37%)
  waiting for transfers between devices  24.8 us (31%)
  blocking collectives  14.3 us (18%)
  Pallas kernels  11.5 us (14%)
    ppermute x19, starting transfers between devices, exchange(): return lax.ppermute(value, BOTH, pairs)  25.6 us
    ppermute x19, waiting for transfers between devices, exchange(): return lax.ppermute(value, BOTH, pairs)  24.6 us
    all_to_all x1, blocking collectives, whole_channels(): lax.all_to_all(send, BOTH, split_axis=0, concat_axis=0, tiled=True, axis_...  14.3 us
    pallas_call x8, Pallas kernels, call(): pl.pallas_call(kernel, out_shape=out_shape, in_specs=[pl.BlockSpec(memory...  11.5 us
    all_to_all x1, starting transfers between devices, whole_channels(): recv = lax.all_to_all(send, BOTH, split_axis=0, concat_axis=0, tiled=True)  4.45 us
  transfers between devices with their start and end apart: 20, of which 12 were waited for; matrix products, arithmetic and copies ran while one was open for 0% of the time, Pallas kernels for 3%

profile of v10, /device:TPU:0, one launch (start us, length us, event | category | flops | bytes accessed | tf_op | source)
XLA Modules:
  0.0 80.8 jit_solution(14509097341017696258)
XLA Ops:
  0.0 2.5 %shard_map.109 = (bf16[160,256]{1,0:T(8,128)(2,1)S(1)}, bf16[160,256]{1,0:T(8,128)(2,1)S(1)}, bf16[160,256]{1,0:T(8,128)(2,1)S(1)}, bf16[160,256]{1,0:T(8,128)(2,1)S(1)}) custom-call(bf16[4,256,256]{2,1,0:T(8,128)(2,1)} %align_in.1, bf16[32,256]{1,0:T(8,128)(2,1)} %bitcast.9, bf16[32,256]{1,0:T(8,128)(2,1)} %bitcast.10), custom_call_target="tpu_custom_call" | custom-call | flops 33554432 | bytes 884736 | tf_op jit(solution)/shard_map/pallas_call | solution.py:485
  2.5 5.1 %collective-permute-start.1 = (bf16[160,256]{1,0:T(8,128)(2,1)S(1)}, bf16[160,256]{1,0:T(8,128)(2,1)S(1)}, u32[]{:S(2)}, u32[]{:S(2)}) collective-permute-start(bf16[160,256]{1,0:T(8,128)(2,1)S(1)} %get-tuple-element.57), channel_id=1, source_target_pairs={{0,24},{1,25},{2,26},{3,27},{4,28},{5,29},{6,30},{7,31},{8,16},{9,... | collective-permute-start | bytes 245768 | tf_op jit(solution)/shard_map/ppermute | solution.py:555
  7.6 0.6 collective-permute-start.3
  8.2 2.6 %collective-permute-start = (bf16[160,256]{1,0:T(8,128)(2,1)S(1)}, bf16[160,256]{1,0:T(8,128)(2,1)S(1)}, u32[]{:S(2)}, u32[]{:S(2)}) collective-permute-start(bf16[160,256]{1,0:T(8,128)(2,1)S(1)} %get-tuple-element.73.refs_0_), channel_id=1, source_target_pairs={{0,6},{1,7},{2,4},{3,5},{4,2},{5,3},{6,0},{7,1},{8,14},{9,15},{10,... | collective-permute-start | bytes 245768 | tf_op jit(solution)/shard_map/ppermute | solution.py:555
  10.8 2.5 %shard_map.110 = (bf16[8,128,256]{2,1,0:T(8,128)(2,1)S(1)}, bf16[128,1024]{1,0:T(8,128)(2,1)S(1)}, bf16[512,128]{1,0:T(8,128)(2,1)S(1)}, bf16[128,128]{1,0:T(8,128)(2,1)S(1)}, bf16[128,128]{1,0:T(8,128)(2,1)S(1)}) custom-call(bf16[8,256,128]{2,1,0:T(8,128)(2,1)} %refs_0_, bf16[1024,128]{1,0:T(8,128)(2,1)} %refs_1_, bf16[128,128]{1,0:T(8,128)(2,1)} %refs_2_, ...), custom_call_target="tpu_custom_call" | custom-call | flops 134217728 | bytes 1966080 | tf_op jit(solution)/shard_map/pallas_call | solution.py:485
  13.3 0.5 collective-permute-done.2.refs_2_
  13.8 0.3 shard_map.111
  14.1 1.7 %collective-permute-start.5 = (bf16[544,256]{1,0:T(8,128)(2,1)S(1)}, bf16[544,256]{1,0:T(8,128)(2,1)S(1)}, u32[]{:S(2)}, u32[]{:S(2)}) collective-permute-start(bf16[544,256]{1,0:T(8,128)(2,1)S(1)} %get-tuple-element.80), channel_id=1, source_target_pairs={{0,4},{1,5},{2,6},{3,7},{4,0},{5,1},{6,2},{7,3},{8,12},{9,13},{10,... | collective-permute-start | bytes 835592 | tf_op jit(solution)/shard_map/ppermute | solution.py:555
  15.8 1.5 %collective-permute-start.6 = (bf16[544,256]{1,0:T(8,128)(2,1)S(1)}, bf16[544,256]{1,0:T(8,128)(2,1)S(1)}, u32[]{:S(2)}, u32[]{:S(2)}) collective-permute-start(bf16[544,256]{1,0:T(8,128)(2,1)S(1)} %get-tuple-element.81), channel_id=1, source_target_pairs={{0,2},{1,3},{2,0},{3,1},{4,6},{5,7},{6,4},{7,5},{8,10},{9,11},{10,... | collective-permute-start | bytes 835592 | tf_op jit(solution)/shard_map/ppermute | solution.py:555
  17.3 0.4 collective-permute-start.4
  17.7 9.4 %collective-permute-done.4.late_ref = bf16[416,256]{1,0:T(8,128)(2,1)S(1)} collective-permute-done((bf16[416,256]{1,0:T(8,128)(2,1)S(1)}, bf16[416,256]{1,0:T(8,128)(2,1)S(1)}, u32[]{:S(2)}, u32[]{:S(2)}) %collective-permute-start.4) | collective-permute-done | bytes 213024 | tf_op jit(solution)/shard_map/ppermute | solution.py:555
  27.4 0.5 collective-permute-start.9
  28.0 1.0 %collective-permute-done.8.refs_5_ = bf16[544,256]{1,0:T(8,128)(2,1)S(1)} collective-permute-done((bf16[544,256]{1,0:T(8,128)(2,1)S(1)}, bf16[544,256]{1,0:T(8,128)(2,1)S(1)}, u32[]{:S(2)}, u32[]{:S(2)}) %collective-permute-start.8) | collective-permute-done | bytes 278560 | tf_op jit(solution)/shard_map/ppermute | solution.py:555
  29.0 0.4 collective-permute-done.9.refs_6_
  29.4 0.4 collective-permute-done.10.refs_7_
  29.8 3.6 %shard_map.113 = (bf16[2048,256]{1,0:T(8,128)(2,1)}, bf16[1024,256]{1,0:T(8,128)(2,1)S(1)}, bf16[8,128,256]{2,1,0:T(8,128)(2,1)S(1)}, bf16[8,128,256]{2,1,0:T(8,128)(2,1)S(1)}) custom-call(bf16[544,256]{1,0:T(8,128)(2,1)S(1)} %get-tuple-element.77.refs_0_, bf16[544,256]{1,0:T(8,128)(2,1)S(1)} %shard_map.112.refs_1_, ...), custom_call_target="tpu_custom_call" | custom-call | flops 1342177280 | bytes 5767168 | tf_op jit(solution)/shard_map/pallas_call | solution.py:485
  33.4 4.5 %all-to-all-start = ((bf16[32,64,256]{2,1,0:T(8,128)(2,1)}), bf16[32,64,256]{2,1,0:T(8,128)(2,1)S(1)}, u32[]{:S(2)}, u32[]{:S(2)}) async-start(bf16[32,64,256]{2,1,0:T(8,128)(2,1)} %bitcast.2), calls=%async_computation | async-start | bytes 2097152 | tf_op jit(solution)/shard_map/all_to_all | solution.py:637
  37.9 0.3 collective-permute-start.11
  38.2 1.7 %collective-permute-done.11.came_ref = bf16[1024,256]{1,0:T(8,128)(2,1)S(1)} collective-permute-done((bf16[1024,256]{1,0:T(8,128)(2,1)S(1)}, bf16[1024,256]{1,0:T(8,128)(2,1)S(1)}, u32[]{:S(2)}, u32[]{:S(2)}) %collective-permute-start.11) | collective-permute-done | bytes 524320 | tf_op jit(solution)/shard_map/ppermute | solution.py:555
  39.9 1.8 %collective-permute-start.12 = (bf16[128,256]{1,0:T(8,128)(2,1)S(1)}, bf16[128,256]{1,0:T(8,128)(2,1)S(1)}, u32[]{:S(2)}, u32[]{:S(2)}) collective-permute-start(bf16[128,256]{1,0:T(8,128)(2,1)S(1)} %get-tuple-element.88), channel_id=1, source_target_pairs={{0,2},{1,3},{2,0},{3,1},{4,6},{5,7},{6,4},{7,5},{8,10},{9,11},{10,... | collective-permute-start | bytes 196616 | tf_op jit(solution)/shard_map/ppermute | solution.py:555
  41.8 1.5 %collective-permute-start.13 = (bf16[128,256]{1,0:T(8,128)(2,1)S(1)}, bf16[128,256]{1,0:T(8,128)(2,1)S(1)}, u32[]{:S(2)}, u32[]{:S(2)}) collective-permute-start(bf16[128,256]{1,0:T(8,128)(2,1)S(1)} %get-tuple-element.89), channel_id=1, source_target_pairs={{0,4},{1,5},{2,6},{3,7},{4,0},{5,1},{6,2},{7,3},{8,12},{9,13},{10,... | collective-permute-start | bytes 196616 | tf_op jit(solution)/shard_map/ppermute | solution.py:555
  43.5 1.8 %collective-permute-start.15 = (bf16[128,256]{1,0:T(8,128)(2,1)S(1)}, bf16[128,256]{1,0:T(8,128)(2,1)S(1)}, u32[]{:S(2)}, u32[]{:S(2)}) collective-permute-start(bf16[128,256]{1,0:T(8,128)(2,1)S(1)} %get-tuple-element.91), channel_id=1, source_target_pairs={{0,8},{1,9},{2,10},{3,11},{4,12},{5,13},{6,14},{7,15},{8,0},{9,1},... | collective-permute-start | bytes 196616 | tf_op jit(solution)/shard_map/ppermute | solution.py:555
  45.2 1.5 %collective-permute-start.16 = (bf16[128,256]{1,0:T(8,128)(2,1)S(1)}, bf16[128,256]{1,0:T(8,128)(2,1)S(1)}, u32[]{:S(2)}, u32[]{:S(2)}) collective-permute-start(bf16[128,256]{1,0:T(8,128)(2,1)S(1)} %get-tuple-element.92), channel_id=1, source_target_pairs={{0,10},{1,11},{2,8},{3,9},{4,14},{5,15},{6,12},{7,13},{8,2},{9,3},... | collective-permute-start | bytes 196616 | tf_op jit(solution)/shard_map/ppermute | solution.py:555
  46.7 2.9 %collective-permute-done.12.refs_1_ = bf16[128,256]{1,0:T(8,128)(2,1)S(1)} collective-permute-done((bf16[128,256]{1,0:T(8,128)(2,1)S(1)}, bf16[128,256]{1,0:T(8,128)(2,1)S(1)}, u32[]{:S(2)}, u32[]{:S(2)}) %collective-permute-start.12) | collective-permute-done | bytes 65568 | tf_op jit(solution)/shard_map/ppermute | solution.py:555
  49.8 5.8 %collective-permute-start.18 = (bf16[128,256]{1,0:T(8,128)(2,1)S(1)}, bf16[128,256]{1,0:T(8,128)(2,1)S(1)}, u32[]{:S(2)}, u32[]{:S(2)}) collective-permute-start(bf16[128,256]{1,0:T(8,128)(2,1)S(1)} %get-tuple-element.94), channel_id=1, source_target_pairs={{0,14},{1,15},{2,12},{3,13},{4,10},{5,11},{6,8},{7,9},{8,6},{9,7},... | collective-permute-start | bytes 196616 | tf_op jit(solution)/shard_map/ppermute | solution.py:555
  55.6 1.6 %collective-permute-done.15.refs_4_ = bf16[128,256]{1,0:T(8,128)(2,1)S(1)} collective-permute-done((bf16[128,256]{1,0:T(8,128)(2,1)S(1)}, bf16[128,256]{1,0:T(8,128)(2,1)S(1)}, u32[]{:S(2)}, u32[]{:S(2)}) %collective-permute-start.15) | collective-permute-done | bytes 65568 | tf_op jit(solution)/shard_map/ppermute | solution.py:555
  57.2 1.5 %collective-permute-done.16.refs_5_ = bf16[128,256]{1,0:T(8,128)(2,1)S(1)} collective-permute-done((bf16[128,256]{1,0:T(8,128)(2,1)S(1)}, bf16[128,256]{1,0:T(8,128)(2,1)S(1)}, u32[]{:S(2)}, u32[]{:S(2)}) %collective-permute-start.16) | collective-permute-done | bytes 65568 | tf_op jit(solution)/shard_map/ppermute | solution.py:555
  58.7 2.2 %collective-permute-done.17.refs_6_ = bf16[128,256]{1,0:T(8,128)(2,1)S(1)} collective-permute-done((bf16[128,256]{1,0:T(8,128)(2,1)S(1)}, bf16[128,256]{1,0:T(8,128)(2,1)S(1)}, u32[]{:S(2)}, u32[]{:S(2)}) %collective-permute-start.17) | collective-permute-done | bytes 65568 | tf_op jit(solution)/shard_map/ppermute | solution.py:555
  60.8 3.0 %collective-permute-done.18.refs_7_ = bf16[128,256]{1,0:T(8,128)(2,1)S(1)} collective-permute-done((bf16[128,256]{1,0:T(8,128)(2,1)S(1)}, bf16[128,256]{1,0:T(8,128)(2,1)S(1)}, u32[]{:S(2)}, u32[]{:S(2)}) %collective-permute-start.18) | collective-permute-done | bytes 65568 | tf_op jit(solution)/shard_map/ppermute | solution.py:555
  64.1 0.5 shard_map.115
  64.6 14.3 %all_to_all.22 = bf16[16,64,256]{2,1,0:T(8,128)(2,1)S(1)} all-to-all(bf16[16,64,256]{2,1,0:T(8,128)(2,1)S(1)} %bitcast.7), channel_id=1, replica_groups={{0,1,2,3,4,5,6,7,8,9,10,11,12,13,14,15},{16,17,18,19,20,21,22,23,24,25,..., dimensions={0} | all-to-all | bytes 1048576 | tf_op jit(solution)/shard_map/all_to_all | solution.py:664
  78.8 1.9 %shard_map.116 = bf16[8,256,128]{2,1,0:T(8,128)(2,1)} custom-call(bf16[1024,256]{1,0:T(8,128)(2,1)S(1)} %bitcast.8, bf16[8,128,256]{2,1,0:T(8,128)(2,1)S(1)} %get-tuple-element.95.mid_ref, bf16[8,128,256]{2,1,0:T(8,128)(2,1)S(1)} %get-tuple-element.96.norm_ref, bf16[128,128]{1,0:T(8,128)(2,1)S(1)} %get-tuple-element.97.gate_w, ...), custom_call_target="tpu_custom_call" | custom-call | flops 134217728 | bytes 2162688 | tf_op jit(solution)/shard_map/pallas_call | solution.py:485
  (17 shorter events, 1.1 us)
Async XLA Ops:
  2.5 10.8 %collective-permute-start.1 = (bf16[160,256]{1,0:T(8,128)(2,1)S(1)}, bf16[160,256]{1,0:T(8,128)(2,1)S(1)}, u32[]{:S(2)}, u32[]{:S(2)}) collective-permute-start(bf16[160,256]{1,0:T(8,128)(2,1)S(1)} %get-tuple-element.57), channel_id=1, source_target_pairs={{0,24},{1,25},{2,26},{3,27},{4,28},{5,29},{6,30},{7,31},{8,16},{9,... | collective-permute-start | bytes 245768 | tf_op jit(solution)/shard_map/ppermute | solution.py:555
  7.6 6.2 %collective-permute-start.2 = (bf16[160,256]{1,0:T(8,128)(2,1)S(1)}, bf16[160,256]{1,0:T(8,128)(2,1)S(1)}, u32[]{:S(2)}, u32[]{:S(2)}) collective-permute-start(bf16[160,256]{1,0:T(8,128)(2,1)S(1)} %get-tuple-element.58), channel_id=1, source_target_pairs={{0,8},{1,9},{2,10},{3,11},{4,12},{5,13},{6,14},{7,15},{8,0},{9,1},... | collective-permute-start | bytes 245768 | tf_op jit(solution)/shard_map/ppermute | solution.py:555
  7.6 6.2 %collective-permute-start.3 = (bf16[160,256]{1,0:T(8,128)(2,1)S(1)}, bf16[160,256]{1,0:T(8,128)(2,1)S(1)}, u32[]{:S(2)}, u32[]{:S(2)}) collective-permute-start(bf16[160,256]{1,0:T(8,128)(2,1)S(1)} %get-tuple-element.59), channel_id=1, source_target_pairs={{0,16},{1,17},{2,18},{3,19},{4,20},{5,21},{6,22},{7,23},{8,24},{9,... | collective-permute-start | bytes 245768 | tf_op jit(solution)/shard_map/ppermute | solution.py:555
  8.2 5.6 %collective-permute-start = (bf16[160,256]{1,0:T(8,128)(2,1)S(1)}, bf16[160,256]{1,0:T(8,128)(2,1)S(1)}, u32[]{:S(2)}, u32[]{:S(2)}) collective-permute-start(bf16[160,256]{1,0:T(8,128)(2,1)S(1)} %get-tuple-element.73.refs_0_), channel_id=1, source_target_pairs={{0,6},{1,7},{2,4},{3,5},{4,2},{5,3},{6,0},{7,1},{8,14},{9,15},{10,... | collective-permute-start | bytes 245768 | tf_op jit(solution)/shard_map/ppermute | solution.py:555
  14.1 13.3 %collective-permute-start.5 = (bf16[544,256]{1,0:T(8,128)(2,1)S(1)}, bf16[544,256]{1,0:T(8,128)(2,1)S(1)}, u32[]{:S(2)}, u32[]{:S(2)}) collective-permute-start(bf16[544,256]{1,0:T(8,128)(2,1)S(1)} %get-tuple-element.80), channel_id=1, source_target_pairs={{0,4},{1,5},{2,6},{3,7},{4,0},{5,1},{6,2},{7,3},{8,12},{9,13},{10,... | collective-permute-start | bytes 835592 | tf_op jit(solution)/shard_map/ppermute | solution.py:555
  15.8 12.1 %collective-permute-start.6 = (bf16[544,256]{1,0:T(8,128)(2,1)S(1)}, bf16[544,256]{1,0:T(8,128)(2,1)S(1)}, u32[]{:S(2)}, u32[]{:S(2)}) collective-permute-start(bf16[544,256]{1,0:T(8,128)(2,1)S(1)} %get-tuple-element.81), channel_id=1, source_target_pairs={{0,2},{1,3},{2,0},{3,1},{4,6},{5,7},{6,4},{7,5},{8,10},{9,11},{10,... | collective-permute-start | bytes 835592 | tf_op jit(solution)/shard_map/ppermute | solution.py:555
  17.3 9.8 %collective-permute-start.4 = (bf16[416,256]{1,0:T(8,128)(2,1)S(1)}, bf16[416,256]{1,0:T(8,128)(2,1)S(1)}, u32[]{:S(2)}, u32[]{:S(2)}) collective-permute-start(bf16[416,256]{1,0:T(8,128)(2,1)S(1)} %get-tuple-element.79), channel_id=1, source_target_pairs={{0,6},{1,7},{2,4},{3,5},{4,2},{5,3},{6,0},{7,1},{8,14},{9,15},{10,... | collective-permute-start | bytes 638984 | tf_op jit(solution)/shard_map/ppermute | solution.py:555
  17.6 10.4 %collective-permute-start.7 = (bf16[544,256]{1,0:T(8,128)(2,1)S(1)}, bf16[544,256]{1,0:T(8,128)(2,1)S(1)}, u32[]{:S(2)}, u32[]{:S(2)}) collective-permute-start(bf16[544,256]{1,0:T(8,128)(2,1)S(1)} %get-tuple-element.77.refs_0_), channel_id=1, source_target_pairs={{0,1},{1,0},{2,3},{3,2},{4,5},{5,4},{6,7},{7,6},{8,9},{9,8},{10,11... | collective-permute-start | bytes 835592 | tf_op jit(solution)/shard_map/ppermute | solution.py:555
  27.3 1.6 %collective-permute-start.8 = (bf16[544,256]{1,0:T(8,128)(2,1)S(1)}, bf16[544,256]{1,0:T(8,128)(2,1)S(1)}, u32[]{:S(2)}, u32[]{:S(2)}) collective-permute-start(bf16[544,256]{1,0:T(8,128)(2,1)S(1)} %shard_map.112.refs_1_), channel_id=1, source_target_pairs={{0,1},{1,0},{2,3},{3,2},{4,5},{5,4},{6,7},{7,6},{8,9},{9,8},{10,11... | collective-permute-start | bytes 835592 | tf_op jit(solution)/shard_map/ppermute | solution.py:555
  27.4 1.9 %collective-permute-start.9 = (bf16[544,256]{1,0:T(8,128)(2,1)S(1)}, bf16[544,256]{1,0:T(8,128)(2,1)S(1)}, u32[]{:S(2)}, u32[]{:S(2)}) collective-permute-start(bf16[544,256]{1,0:T(8,128)(2,1)S(1)} %collective-permute-done.5.refs_2_), channel_id=1, source_target_pairs={{0,1},{1,0},{2,3},{3,2},{4,5},{5,4},{6,7},{7,6},{8,9},{9,8},{10,11... | collective-permute-start | bytes 835592 | tf_op jit(solution)/shard_map/ppermute | solution.py:555
  27.9 1.8 %collective-permute-start.10 = (bf16[544,256]{1,0:T(8,128)(2,1)S(1)}, bf16[544,256]{1,0:T(8,128)(2,1)S(1)}, u32[]{:S(2)}, u32[]{:S(2)}) collective-permute-start(bf16[544,256]{1,0:T(8,128)(2,1)S(1)} %collective-permute-done.6.refs_3_), channel_id=1, source_target_pairs={{0,1},{1,0},{2,3},{3,2},{4,5},{5,4},{6,7},{7,6},{8,9},{9,8},{10,11... | collective-permute-start | bytes 835592 | tf_op jit(solution)/shard_map/ppermute | solution.py:555
  33.4 30.7 %all-to-all-start = ((bf16[32,64,256]{2,1,0:T(8,128)(2,1)}), bf16[32,64,256]{2,1,0:T(8,128)(2,1)S(1)}, u32[]{:S(2)}, u32[]{:S(2)}) async-start(bf16[32,64,256]{2,1,0:T(8,128)(2,1)} %bitcast.2), calls=%async_computation | async-start | bytes 2097152 | tf_op jit(solution)/shard_map/all_to_all | solution.py:637
  37.9 2.0 %collective-permute-start.11 = (bf16[1024,256]{1,0:T(8,128)(2,1)S(1)}, bf16[1024,256]{1,0:T(8,128)(2,1)S(1)}, u32[]{:S(2)}, u32[]{:S(2)}) collective-permute-start(bf16[1024,256]{1,0:T(8,128)(2,1)S(1)} %get-tuple-element.86.own_ref), channel_id=1, source_target_pairs={{0,1},{1,0},{2,3},{3,2},{4,5},{5,4},{6,7},{7,6},{8,9},{9,8},{10,11... | collective-permute-start | bytes 1572872 | tf_op jit(solution)/shard_map/ppermute | solution.py:555
  39.9 9.7 %collective-permute-start.12 = (bf16[128,256]{1,0:T(8,128)(2,1)S(1)}, bf16[128,256]{1,0:T(8,128)(2,1)S(1)}, u32[]{:S(2)}, u32[]{:S(2)}) collective-permute-start(bf16[128,256]{1,0:T(8,128)(2,1)S(1)} %get-tuple-element.88), channel_id=1, source_target_pairs={{0,2},{1,3},{2,0},{3,1},{4,6},{5,7},{6,4},{7,5},{8,10},{9,11},{10,... | collective-permute-start | bytes 196616 | tf_op jit(solution)/shard_map/ppermute | solution.py:555
  41.8 8.0 %collective-permute-start.13 = (bf16[128,256]{1,0:T(8,128)(2,1)S(1)}, bf16[128,256]{1,0:T(8,128)(2,1)S(1)}, u32[]{:S(2)}, u32[]{:S(2)}) collective-permute-start(bf16[128,256]{1,0:T(8,128)(2,1)S(1)} %get-tuple-element.89), channel_id=1, source_target_pairs={{0,4},{1,5},{2,6},{3,7},{4,0},{5,1},{6,2},{7,3},{8,12},{9,13},{10,... | collective-permute-start | bytes 196616 | tf_op jit(solution)/shard_map/ppermute | solution.py:555
  43.2 12.4 %collective-permute-start.14 = (bf16[128,256]{1,0:T(8,128)(2,1)S(1)}, bf16[128,256]{1,0:T(8,128)(2,1)S(1)}, u32[]{:S(2)}, u32[]{:S(2)}) collective-permute-start(bf16[128,256]{1,0:T(8,128)(2,1)S(1)} %get-tuple-element.90), channel_id=1, source_target_pairs={{0,6},{1,7},{2,4},{3,5},{4,2},{5,3},{6,0},{7,1},{8,14},{9,15},{10,... | collective-permute-start | bytes 196616 | tf_op jit(solution)/shard_map/ppermute | solution.py:555
  43.5 13.7 %collective-permute-start.15 = (bf16[128,256]{1,0:T(8,128)(2,1)S(1)}, bf16[128,256]{1,0:T(8,128)(2,1)S(1)}, u32[]{:S(2)}, u32[]{:S(2)}) collective-permute-start(bf16[128,256]{1,0:T(8,128)(2,1)S(1)} %get-tuple-element.91), channel_id=1, source_target_pairs={{0,8},{1,9},{2,10},{3,11},{4,12},{5,13},{6,14},{7,15},{8,0},{9,1},... | collective-permute-start | bytes 196616 | tf_op jit(solution)/shard_map/ppermute | solution.py:555
  45.2 13.4 %collective-permute-start.16 = (bf16[128,256]{1,0:T(8,128)(2,1)S(1)}, bf16[128,256]{1,0:T(8,128)(2,1)S(1)}, u32[]{:S(2)}, u32[]{:S(2)}) collective-permute-start(bf16[128,256]{1,0:T(8,128)(2,1)S(1)} %get-tuple-element.92), channel_id=1, source_target_pairs={{0,10},{1,11},{2,8},{3,9},{4,14},{5,15},{6,12},{7,13},{8,2},{9,3},... | collective-permute-start | bytes 196616 | tf_op jit(solution)/shard_map/ppermute | solution.py:555
  49.6 11.2 %collective-permute-start.17 = (bf16[128,256]{1,0:T(8,128)(2,1)S(1)}, bf16[128,256]{1,0:T(8,128)(2,1)S(1)}, u32[]{:S(2)}, u32[]{:S(2)}) collective-permute-start(bf16[128,256]{1,0:T(8,128)(2,1)S(1)} %get-tuple-element.93), channel_id=1, source_target_pairs={{0,12},{1,13},{2,14},{3,15},{4,8},{5,9},{6,10},{7,11},{8,4},{9,5},... | collective-permute-start | bytes 196616 | tf_op jit(solution)/shard_map/ppermute | solution.py:555
  49.8 14.1 %collective-permute-start.18 = (bf16[128,256]{1,0:T(8,128)(2,1)S(1)}, bf16[128,256]{1,0:T(8,128)(2,1)S(1)}, u32[]{:S(2)}, u32[]{:S(2)}) collective-permute-start(bf16[128,256]{1,0:T(8,128)(2,1)S(1)} %get-tuple-element.94), channel_id=1, source_target_pairs={{0,14},{1,15},{2,12},{3,13},{4,10},{5,11},{6,8},{7,9},{8,6},{9,7},... | collective-permute-start | bytes 196616 | tf_op jit(solution)/shard_map/ppermute | solution.py:555

commit v11 on v10

--- a/solution.py
+++ b/solution.py
@@ -365,9 +365,10 @@
 
     def by_channels(side):
         at = 2 * side * hidden
+        parts = [mul(tri_w[at : at + 2 * hidden, :], norm_ref[i]) for i in range(rows)]
         for i in range(rows):
-            parts = mul(tri_w[at : at + 2 * hidden, :], norm_ref[i])
-            both[side, i] = (jax.nn.sigmoid(parts[:hidden]) * parts[hidden:]).astype(BF16)
+            gate = jax.nn.sigmoid(parts[i][:hidden])
+            both[side, i] = (gate * parts[i][hidden:]).astype(BF16)
         blocks = [
             jnp.concatenate([both[side, i, b * some : (b + 1) * some, :] for i in range(rows)], 0)
             for b in range(hidden // some)

time: 81 us -> 81 us (level)
  no operation moved by 1% of the time
where the time goes in v11:
time: 81 us; the launch traced here: 80.8 us
  starting transfers between devices  30.1 us (37%)
  waiting for transfers between devices  24.8 us (31%)
  blocking collectives  14.3 us (18%)
  Pallas kernels  11.5 us (14%)
    ppermute x19, starting transfers between devices, exchange(): return lax.ppermute(value, BOTH, pairs)  25.6 us
    ppermute x19, waiting for transfers between devices, exchange(): return lax.ppermute(value, BOTH, pairs)  24.6 us
    all_to_all x1, blocking collectives, whole_channels(): lax.all_to_all(send, BOTH, split_axis=0, concat_axis=0, tiled=True, axis_...  14.3 us
    pallas_call x8, Pallas kernels, call(): pl.pallas_call(kernel, out_shape=out_shape, in_specs=[pl.BlockSpec(memory...  11.5 us
    all_to_all x1, starting transfers between devices, whole_channels(): recv = lax.all_to_all(send, BOTH, split_axis=0, concat_axis=0, tiled=True)  4.45 us
  transfers between devices with their start and end apart: 20, of which 12 were waited for; matrix products, arithmetic and copies ran while one was open for 0% of the time, Pallas kernels for 3%

profile of v11, /device:TPU:0, one launch (start us, length us, event | category | flops | bytes accessed | tf_op | source)
XLA Modules:
  0.0 80.8 jit_solution(13799288695701859606)
XLA Ops:
  0.0 2.5 %shard_map.109 = (bf16[160,256]{1,0:T(8,128)(2,1)S(1)}, bf16[160,256]{1,0:T(8,128)(2,1)S(1)}, bf16[160,256]{1,0:T(8,128)(2,1)S(1)}, bf16[160,256]{1,0:T(8,128)(2,1)S(1)}) custom-call(bf16[4,256,256]{2,1,0:T(8,128)(2,1)} %align_in.1, bf16[32,256]{1,0:T(8,128)(2,1)} %bitcast.9, bf16[32,256]{1,0:T(8,128)(2,1)} %bitcast.10), custom_call_target="tpu_custom_call" | custom-call | flops 33554432 | bytes 884736 | tf_op jit(solution)/shard_map/pallas_call | solution.py:486
  2.5 5.1 %collective-permute-start.1 = (bf16[160,256]{1,0:T(8,128)(2,1)S(1)}, bf16[160,256]{1,0:T(8,128)(2,1)S(1)}, u32[]{:S(2)}, u32[]{:S(2)}) collective-permute-start(bf16[160,256]{1,0:T(8,128)(2,1)S(1)} %get-tuple-element.57), channel_id=1, source_target_pairs={{0,24},{1,25},{2,26},{3,27},{4,28},{5,29},{6,30},{7,31},{8,16},{9,... | collective-permute-start | bytes 245768 | tf_op jit(solution)/shard_map/ppermute | solution.py:556
  7.6 0.6 collective-permute-start.3
  8.2 2.6 %collective-permute-start = (bf16[160,256]{1,0:T(8,128)(2,1)S(1)}, bf16[160,256]{1,0:T(8,128)(2,1)S(1)}, u32[]{:S(2)}, u32[]{:S(2)}) collective-permute-start(bf16[160,256]{1,0:T(8,128)(2,1)S(1)} %get-tuple-element.73.refs_0_), channel_id=1, source_target_pairs={{0,6},{1,7},{2,4},{3,5},{4,2},{5,3},{6,0},{7,1},{8,14},{9,15},{10,... | collective-permute-start | bytes 245768 | tf_op jit(solution)/shard_map/ppermute | solution.py:556
  10.8 2.5 %shard_map.110 = (bf16[8,128,256]{2,1,0:T(8,128)(2,1)S(1)}, bf16[128,1024]{1,0:T(8,128)(2,1)S(1)}, bf16[512,128]{1,0:T(8,128)(2,1)S(1)}, bf16[128,128]{1,0:T(8,128)(2,1)S(1)}, bf16[128,128]{1,0:T(8,128)(2,1)S(1)}) custom-call(bf16[8,256,128]{2,1,0:T(8,128)(2,1)} %refs_0_, bf16[1024,128]{1,0:T(8,128)(2,1)} %refs_1_, bf16[128,128]{1,0:T(8,128)(2,1)} %refs_2_, ...), custom_call_target="tpu_custom_call" | custom-call | flops 134217728 | bytes 1966080 | tf_op jit(solution)/shard_map/pallas_call | solution.py:486
  13.3 0.5 collective-permute-done.2.refs_2_
  13.8 0.3 shard_map.111
  14.1 1.7 %collective-permute-start.5 = (bf16[544,256]{1,0:T(8,128)(2,1)S(1)}, bf16[544,256]{1,0:T(8,128)(2,1)S(1)}, u32[]{:S(2)}, u32[]{:S(2)}) collective-permute-start(bf16[544,256]{1,0:T(8,128)(2,1)S(1)} %get-tuple-element.80), channel_id=1, source_target_pairs={{0,4},{1,5},{2,6},{3,7},{4,0},{5,1},{6,2},{7,3},{8,12},{9,13},{10,... | collective-permute-start | bytes 835592 | tf_op jit(solution)/shard_map/ppermute | solution.py:556
  15.8 1.5 %collective-permute-start.6 = (bf16[544,256]{1,0:T(8,128)(2,1)S(1)}, bf16[544,256]{1,0:T(8,128)(2,1)S(1)}, u32[]{:S(2)}, u32[]{:S(2)}) collective-permute-start(bf16[544,256]{1,0:T(8,128)(2,1)S(1)} %get-tuple-element.81), channel_id=1, source_target_pairs={{0,2},{1,3},{2,0},{3,1},{4,6},{5,7},{6,4},{7,5},{8,10},{9,11},{10,... | collective-permute-start | bytes 835592 | tf_op jit(solution)/shard_map/ppermute | solution.py:556
  17.3 0.4 collective-permute-start.4
  17.7 9.4 %collective-permute-done.4.late_ref = bf16[416,256]{1,0:T(8,128)(2,1)S(1)} collective-permute-done((bf16[416,256]{1,0:T(8,128)(2,1)S(1)}, bf16[416,256]{1,0:T(8,128)(2,1)S(1)}, u32[]{:S(2)}, u32[]{:S(2)}) %collective-permute-start.4) | collective-permute-done | bytes 213024 | tf_op jit(solution)/shard_map/ppermute | solution.py:556
  27.4 0.5 collective-permute-start.9
  28.0 1.0 %collective-permute-done.8.refs_5_ = bf16[544,256]{1,0:T(8,128)(2,1)S(1)} collective-permute-done((bf16[544,256]{1,0:T(8,128)(2,1)S(1)}, bf16[544,256]{1,0:T(8,128)(2,1)S(1)}, u32[]{:S(2)}, u32[]{:S(2)}) %collective-permute-start.8) | collective-permute-done | bytes 278560 | tf_op jit(solution)/shard_map/ppermute | solution.py:556
  29.0 0.4 collective-permute-done.9.refs_6_
  29.4 0.4 collective-permute-done.10.refs_7_
  29.8 3.6 %shard_map.113 = (bf16[2048,256]{1,0:T(8,128)(2,1)}, bf16[1024,256]{1,0:T(8,128)(2,1)S(1)}, bf16[8,128,256]{2,1,0:T(8,128)(2,1)S(1)}, bf16[8,128,256]{2,1,0:T(8,128)(2,1)S(1)}) custom-call(bf16[544,256]{1,0:T(8,128)(2,1)S(1)} %get-tuple-element.77.refs_0_, bf16[544,256]{1,0:T(8,128)(2,1)S(1)} %shard_map.112.refs_1_, ...), custom_call_target="tpu_custom_call" | custom-call | flops 1342177280 | bytes 5767168 | tf_op jit(solution)/shard_map/pallas_call | solution.py:486
  33.4 4.5 %all-to-all-start = ((bf16[32,64,256]{2,1,0:T(8,128)(2,1)}), bf16[32,64,256]{2,1,0:T(8,128)(2,1)S(1)}, u32[]{:S(2)}, u32[]{:S(2)}) async-start(bf16[32,64,256]{2,1,0:T(8,128)(2,1)} %bitcast.2), calls=%async_computation | async-start | bytes 2097152 | tf_op jit(solution)/shard_map/all_to_all | solution.py:638
  37.9 0.3 collective-permute-start.11
  38.2 1.7 %collective-permute-done.11.came_ref = bf16[1024,256]{1,0:T(8,128)(2,1)S(1)} collective-permute-done((bf16[1024,256]{1,0:T(8,128)(2,1)S(1)}, bf16[1024,256]{1,0:T(8,128)(2,1)S(1)}, u32[]{:S(2)}, u32[]{:S(2)}) %collective-permute-start.11) | collective-permute-done | bytes 524320 | tf_op jit(solution)/shard_map/ppermute | solution.py:556
  39.9 1.8 %collective-permute-start.12 = (bf16[128,256]{1,0:T(8,128)(2,1)S(1)}, bf16[128,256]{1,0:T(8,128)(2,1)S(1)}, u32[]{:S(2)}, u32[]{:S(2)}) collective-permute-start(bf16[128,256]{1,0:T(8,128)(2,1)S(1)} %get-tuple-element.88), channel_id=1, source_target_pairs={{0,2},{1,3},{2,0},{3,1},{4,6},{5,7},{6,4},{7,5},{8,10},{9,11},{10,... | collective-permute-start | bytes 196616 | tf_op jit(solution)/shard_map/ppermute | solution.py:556
  41.8 1.5 %collective-permute-start.13 = (bf16[128,256]{1,0:T(8,128)(2,1)S(1)}, bf16[128,256]{1,0:T(8,128)(2,1)S(1)}, u32[]{:S(2)}, u32[]{:S(2)}) collective-permute-start(bf16[128,256]{1,0:T(8,128)(2,1)S(1)} %get-tuple-element.89), channel_id=1, source_target_pairs={{0,4},{1,5},{2,6},{3,7},{4,0},{5,1},{6,2},{7,3},{8,12},{9,13},{10,... | collective-permute-start | bytes 196616 | tf_op jit(solution)/shard_map/ppermute | solution.py:556
  43.5 1.8 %collective-permute-start.15 = (bf16[128,256]{1,0:T(8,128)(2,1)S(1)}, bf16[128,256]{1,0:T(8,128)(2,1)S(1)}, u32[]{:S(2)}, u32[]{:S(2)}) collective-permute-start(bf16[128,256]{1,0:T(8,128)(2,1)S(1)} %get-tuple-element.91), channel_id=1, source_target_pairs={{0,8},{1,9},{2,10},{3,11},{4,12},{5,13},{6,14},{7,15},{8,0},{9,1},... | collective-permute-start | bytes 196616 | tf_op jit(solution)/shard_map/ppermute | solution.py:556
  45.2 1.5 %collective-permute-start.16 = (bf16[128,256]{1,0:T(8,128)(2,1)S(1)}, bf16[128,256]{1,0:T(8,128)(2,1)S(1)}, u32[]{:S(2)}, u32[]{:S(2)}) collective-permute-start(bf16[128,256]{1,0:T(8,128)(2,1)S(1)} %get-tuple-element.92), channel_id=1, source_target_pairs={{0,10},{1,11},{2,8},{3,9},{4,14},{5,15},{6,12},{7,13},{8,2},{9,3},... | collective-permute-start | bytes 196616 | tf_op jit(solution)/shard_map/ppermute | solution.py:556
  46.7 2.9 %collective-permute-done.12.refs_1_ = bf16[128,256]{1,0:T(8,128)(2,1)S(1)} collective-permute-done((bf16[128,256]{1,0:T(8,128)(2,1)S(1)}, bf16[128,256]{1,0:T(8,128)(2,1)S(1)}, u32[]{:S(2)}, u32[]{:S(2)}) %collective-permute-start.12) | collective-permute-done | bytes 65568 | tf_op jit(solution)/shard_map/ppermute | solution.py:556
  49.8 5.8 %collective-permute-start.18 = (bf16[128,256]{1,0:T(8,128)(2,1)S(1)}, bf16[128,256]{1,0:T(8,128)(2,1)S(1)}, u32[]{:S(2)}, u32[]{:S(2)}) collective-permute-start(bf16[128,256]{1,0:T(8,128)(2,1)S(1)} %get-tuple-element.94), channel_id=1, source_target_pairs={{0,14},{1,15},{2,12},{3,13},{4,10},{5,11},{6,8},{7,9},{8,6},{9,7},... | collective-permute-start | bytes 196616 | tf_op jit(solution)/shard_map/ppermute | solution.py:556
  55.6 1.6 %collective-permute-done.15.refs_4_ = bf16[128,256]{1,0:T(8,128)(2,1)S(1)} collective-permute-done((bf16[128,256]{1,0:T(8,128)(2,1)S(1)}, bf16[128,256]{1,0:T(8,128)(2,1)S(1)}, u32[]{:S(2)}, u32[]{:S(2)}) %collective-permute-start.15) | collective-permute-done | bytes 65568 | tf_op jit(solution)/shard_map/ppermute | solution.py:556
  57.2 1.5 %collective-permute-done.16.refs_5_ = bf16[128,256]{1,0:T(8,128)(2,1)S(1)} collective-permute-done((bf16[128,256]{1,0:T(8,128)(2,1)S(1)}, bf16[128,256]{1,0:T(8,128)(2,1)S(1)}, u32[]{:S(2)}, u32[]{:S(2)}) %collective-permute-start.16) | collective-permute-done | bytes 65568 | tf_op jit(solution)/shard_map/ppermute | solution.py:556
  58.7 2.2 %collective-permute-done.17.refs_6_ = bf16[128,256]{1,0:T(8,128)(2,1)S(1)} collective-permute-done((bf16[128,256]{1,0:T(8,128)(2,1)S(1)}, bf16[128,256]{1,0:T(8,128)(2,1)S(1)}, u32[]{:S(2)}, u32[]{:S(2)}) %collective-permute-start.17) | collective-permute-done | bytes 65568 | tf_op jit(solution)/shard_map/ppermute | solution.py:556
  60.8 3.0 %collective-permute-done.18.refs_7_ = bf16[128,256]{1,0:T(8,128)(2,1)S(1)} collective-permute-done((bf16[128,256]{1,0:T(8,128)(2,1)S(1)}, bf16[128,256]{1,0:T(8,128)(2,1)S(1)}, u32[]{:S(2)}, u32[]{:S(2)}) %collective-permute-start.18) | collective-permute-done | bytes 65568 | tf_op jit(solution)/shard_map/ppermute | solution.py:556
  64.1 0.5 shard_map.115
  64.6 14.3 %all_to_all.22 = bf16[16,64,256]{2,1,0:T(8,128)(2,1)S(1)} all-to-all(bf16[16,64,256]{2,1,0:T(8,128)(2,1)S(1)} %bitcast.7), channel_id=1, replica_groups={{0,1,2,3,4,5,6,7,8,9,10,11,12,13,14,15},{16,17,18,19,20,21,22,23,24,25,..., dimensions={0} | all-to-all | bytes 1048576 | tf_op jit(solution)/shard_map/all_to_all | solution.py:665
  78.8 1.9 %shard_map.116 = bf16[8,256,128]{2,1,0:T(8,128)(2,1)} custom-call(bf16[1024,256]{1,0:T(8,128)(2,1)S(1)} %bitcast.8, bf16[8,128,256]{2,1,0:T(8,128)(2,1)S(1)} %get-tuple-element.95.mid_ref, bf16[8,128,256]{2,1,0:T(8,128)(2,1)S(1)} %get-tuple-element.96.norm_ref, bf16[128,128]{1,0:T(8,128)(2,1)S(1)} %get-tuple-element.97.gate_w, ...), custom_call_target="tpu_custom_call" | custom-call | flops 134217728 | bytes 2162688 | tf_op jit(solution)/shard_map/pallas_call | solution.py:486
  (17 shorter events, 1.1 us)
Async XLA Ops:
  2.5 10.8 %collective-permute-start.1 = (bf16[160,256]{1,0:T(8,128)(2,1)S(1)}, bf16[160,256]{1,0:T(8,128)(2,1)S(1)}, u32[]{:S(2)}, u32[]{:S(2)}) collective-permute-start(bf16[160,256]{1,0:T(8,128)(2,1)S(1)} %get-tuple-element.57), channel_id=1, source_target_pairs={{0,24},{1,25},{2,26},{3,27},{4,28},{5,29},{6,30},{7,31},{8,16},{9,... | collective-permute-start | bytes 245768 | tf_op jit(solution)/shard_map/ppermute | solution.py:556
  7.6 6.2 %collective-permute-start.2 = (bf16[160,256]{1,0:T(8,128)(2,1)S(1)}, bf16[160,256]{1,0:T(8,128)(2,1)S(1)}, u32[]{:S(2)}, u32[]{:S(2)}) collective-permute-start(bf16[160,256]{1,0:T(8,128)(2,1)S(1)} %get-tuple-element.58), channel_id=1, source_target_pairs={{0,8},{1,9},{2,10},{3,11},{4,12},{5,13},{6,14},{7,15},{8,0},{9,1},... | collective-permute-start | bytes 245768 | tf_op jit(solution)/shard_map/ppermute | solution.py:556
  7.6 6.2 %collective-permute-start.3 = (bf16[160,256]{1,0:T(8,128)(2,1)S(1)}, bf16[160,256]{1,0:T(8,128)(2,1)S(1)}, u32[]{:S(2)}, u32[]{:S(2)}) collective-permute-start(bf16[160,256]{1,0:T(8,128)(2,1)S(1)} %get-tuple-element.59), channel_id=1, source_target_pairs={{0,16},{1,17},{2,18},{3,19},{4,20},{5,21},{6,22},{7,23},{8,24},{9,... | collective-permute-start | bytes 245768 | tf_op jit(solution)/shard_map/ppermute | solution.py:556
  8.2 5.6 %collective-permute-start = (bf16[160,256]{1,0:T(8,128)(2,1)S(1)}, bf16[160,256]{1,0:T(8,128)(2,1)S(1)}, u32[]{:S(2)}, u32[]{:S(2)}) collective-permute-start(bf16[160,256]{1,0:T(8,128)(2,1)S(1)} %get-tuple-element.73.refs_0_), channel_id=1, source_target_pairs={{0,6},{1,7},{2,4},{3,5},{4,2},{5,3},{6,0},{7,1},{8,14},{9,15},{10,... | collective-permute-start | bytes 245768 | tf_op jit(solution)/shard_map/ppermute | solution.py:556
  14.1 13.3 %collective-permute-start.5 = (bf16[544,256]{1,0:T(8,128)(2,1)S(1)}, bf16[544,256]{1,0:T(8,128)(2,1)S(1)}, u32[]{:S(2)}, u32[]{:S(2)}) collective-permute-start(bf16[544,256]{1,0:T(8,128)(2,1)S(1)} %get-tuple-element.80), channel_id=1, source_target_pairs={{0,4},{1,5},{2,6},{3,7},{4,0},{5,1},{6,2},{7,3},{8,12},{9,13},{10,... | collective-permute-start | bytes 835592 | tf_op jit(solution)/shard_map/ppermute | solution.py:556
  15.8 12.1 %collective-permute-start.6 = (bf16[544,256]{1,0:T(8,128)(2,1)S(1)}, bf16[544,256]{1,0:T(8,128)(2,1)S(1)}, u32[]{:S(2)}, u32[]{:S(2)}) collective-permute-start(bf16[544,256]{1,0:T(8,128)(2,1)S(1)} %get-tuple-element.81), channel_id=1, source_target_pairs={{0,2},{1,3},{2,0},{3,1},{4,6},{5,7},{6,4},{7,5},{8,10},{9,11},{10,... | collective-permute-start | bytes 835592 | tf_op jit(solution)/shard_map/ppermute | solution.py:556
  17.3 9.8 %collective-permute-start.4 = (bf16[416,256]{1,0:T(8,128)(2,1)S(1)}, bf16[416,256]{1,0:T(8,128)(2,1)S(1)}, u32[]{:S(2)}, u32[]{:S(2)}) collective-permute-start(bf16[416,256]{1,0:T(8,128)(2,1)S(1)} %get-tuple-element.79), channel_id=1, source_target_pairs={{0,6},{1,7},{2,4},{3,5},{4,2},{5,3},{6,0},{7,1},{8,14},{9,15},{10,... | collective-permute-start | bytes 638984 | tf_op jit(solution)/shard_map/ppermute | solution.py:556
  17.6 10.4 %collective-permute-start.7 = (bf16[544,256]{1,0:T(8,128)(2,1)S(1)}, bf16[544,256]{1,0:T(8,128)(2,1)S(1)}, u32[]{:S(2)}, u32[]{:S(2)}) collective-permute-start(bf16[544,256]{1,0:T(8,128)(2,1)S(1)} %get-tuple-element.77.refs_0_), channel_id=1, source_target_pairs={{0,1},{1,0},{2,3},{3,2},{4,5},{5,4},{6,7},{7,6},{8,9},{9,8},{10,11... | collective-permute-start | bytes 835592 | tf_op jit(solution)/shard_map/ppermute | solution.py:556
  27.3 1.6 %collective-permute-start.8 = (bf16[544,256]{1,0:T(8,128)(2,1)S(1)}, bf16[544,256]{1,0:T(8,128)(2,1)S(1)}, u32[]{:S(2)}, u32[]{:S(2)}) collective-permute-start(bf16[544,256]{1,0:T(8,128)(2,1)S(1)} %shard_map.112.refs_1_), channel_id=1, source_target_pairs={{0,1},{1,0},{2,3},{3,2},{4,5},{5,4},{6,7},{7,6},{8,9},{9,8},{10,11... | collective-permute-start | bytes 835592 | tf_op jit(solution)/shard_map/ppermute | solution.py:556
  27.4 1.9 %collective-permute-start.9 = (bf16[544,256]{1,0:T(8,128)(2,1)S(1)}, bf16[544,256]{1,0:T(8,128)(2,1)S(1)}, u32[]{:S(2)}, u32[]{:S(2)}) collective-permute-start(bf16[544,256]{1,0:T(8,128)(2,1)S(1)} %collective-permute-done.5.refs_2_), channel_id=1, source_target_pairs={{0,1},{1,0},{2,3},{3,2},{4,5},{5,4},{6,7},{7,6},{8,9},{9,8},{10,11... | collective-permute-start | bytes 835592 | tf_op jit(solution)/shard_map/ppermute | solution.py:556
  27.9 1.8 %collective-permute-start.10 = (bf16[544,256]{1,0:T(8,128)(2,1)S(1)}, bf16[544,256]{1,0:T(8,128)(2,1)S(1)}, u32[]{:S(2)}, u32[]{:S(2)}) collective-permute-start(bf16[544,256]{1,0:T(8,128)(2,1)S(1)} %collective-permute-done.6.refs_3_), channel_id=1, source_target_pairs={{0,1},{1,0},{2,3},{3,2},{4,5},{5,4},{6,7},{7,6},{8,9},{9,8},{10,11... | collective-permute-start | bytes 835592 | tf_op jit(solution)/shard_map/ppermute | solution.py:556
  33.4 30.7 %all-to-all-start = ((bf16[32,64,256]{2,1,0:T(8,128)(2,1)}), bf16[32,64,256]{2,1,0:T(8,128)(2,1)S(1)}, u32[]{:S(2)}, u32[]{:S(2)}) async-start(bf16[32,64,256]{2,1,0:T(8,128)(2,1)} %bitcast.2), calls=%async_computation | async-start | bytes 2097152 | tf_op jit(solution)/shard_map/all_to_all | solution.py:638
  37.9 2.0 %collective-permute-start.11 = (bf16[1024,256]{1,0:T(8,128)(2,1)S(1)}, bf16[1024,256]{1,0:T(8,128)(2,1)S(1)}, u32[]{:S(2)}, u32[]{:S(2)}) collective-permute-start(bf16[1024,256]{1,0:T(8,128)(2,1)S(1)} %get-tuple-element.86.own_ref), channel_id=1, source_target_pairs={{0,1},{1,0},{2,3},{3,2},{4,5},{5,4},{6,7},{7,6},{8,9},{9,8},{10,11... | collective-permute-start | bytes 1572872 | tf_op jit(solution)/shard_map/ppermute | solution.py:556
  39.9 9.7 %collective-permute-start.12 = (bf16[128,256]{1,0:T(8,128)(2,1)S(1)}, bf16[128,256]{1,0:T(8,128)(2,1)S(1)}, u32[]{:S(2)}, u32[]{:S(2)}) collective-permute-start(bf16[128,256]{1,0:T(8,128)(2,1)S(1)} %get-tuple-element.88), channel_id=1, source_target_pairs={{0,2},{1,3},{2,0},{3,1},{4,6},{5,7},{6,4},{7,5},{8,10},{9,11},{10,... | collective-permute-start | bytes 196616 | tf_op jit(solution)/shard_map/ppermute | solution.py:556
  41.8 8.0 %collective-permute-start.13 = (bf16[128,256]{1,0:T(8,128)(2,1)S(1)}, bf16[128,256]{1,0:T(8,128)(2,1)S(1)}, u32[]{:S(2)}, u32[]{:S(2)}) collective-permute-start(bf16[128,256]{1,0:T(8,128)(2,1)S(1)} %get-tuple-element.89), channel_id=1, source_target_pairs={{0,4},{1,5},{2,6},{3,7},{4,0},{5,1},{6,2},{7,3},{8,12},{9,13},{10,... | collective-permute-start | bytes 196616 | tf_op jit(solution)/shard_map/ppermute | solution.py:556
  43.2 12.4 %collective-permute-start.14 = (bf16[128,256]{1,0:T(8,128)(2,1)S(1)}, bf16[128,256]{1,0:T(8,128)(2,1)S(1)}, u32[]{:S(2)}, u32[]{:S(2)}) collective-permute-start(bf16[128,256]{1,0:T(8,128)(2,1)S(1)} %get-tuple-element.90), channel_id=1, source_target_pairs={{0,6},{1,7},{2,4},{3,5},{4,2},{5,3},{6,0},{7,1},{8,14},{9,15},{10,... | collective-permute-start | bytes 196616 | tf_op jit(solution)/shard_map/ppermute | solution.py:556
  43.5 13.7 %collective-permute-start.15 = (bf16[128,256]{1,0:T(8,128)(2,1)S(1)}, bf16[128,256]{1,0:T(8,128)(2,1)S(1)}, u32[]{:S(2)}, u32[]{:S(2)}) collective-permute-start(bf16[128,256]{1,0:T(8,128)(2,1)S(1)} %get-tuple-element.91), channel_id=1, source_target_pairs={{0,8},{1,9},{2,10},{3,11},{4,12},{5,13},{6,14},{7,15},{8,0},{9,1},... | collective-permute-start | bytes 196616 | tf_op jit(solution)/shard_map/ppermute | solution.py:556
  45.2 13.4 %collective-permute-start.16 = (bf16[128,256]{1,0:T(8,128)(2,1)S(1)}, bf16[128,256]{1,0:T(8,128)(2,1)S(1)}, u32[]{:S(2)}, u32[]{:S(2)}) collective-permute-start(bf16[128,256]{1,0:T(8,128)(2,1)S(1)} %get-tuple-element.92), channel_id=1, source_target_pairs={{0,10},{1,11},{2,8},{3,9},{4,14},{5,15},{6,12},{7,13},{8,2},{9,3},... | collective-permute-start | bytes 196616 | tf_op jit(solution)/shard_map/ppermute | solution.py:556
  49.6 11.2 %collective-permute-start.17 = (bf16[128,256]{1,0:T(8,128)(2,1)S(1)}, bf16[128,256]{1,0:T(8,128)(2,1)S(1)}, u32[]{:S(2)}, u32[]{:S(2)}) collective-permute-start(bf16[128,256]{1,0:T(8,128)(2,1)S(1)} %get-tuple-element.93), channel_id=1, source_target_pairs={{0,12},{1,13},{2,14},{3,15},{4,8},{5,9},{6,10},{7,11},{8,4},{9,5},... | collective-permute-start | bytes 196616 | tf_op jit(solution)/shard_map/ppermute | solution.py:556
  49.8 14.1 %collective-permute-start.18 = (bf16[128,256]{1,0:T(8,128)(2,1)S(1)}, bf16[128,256]{1,0:T(8,128)(2,1)S(1)}, u32[]{:S(2)}, u32[]{:S(2)}) collective-permute-start(bf16[128,256]{1,0:T(8,128)(2,1)S(1)} %get-tuple-element.94), channel_id=1, source_target_pairs={{0,14},{1,15},{2,12},{3,13},{4,10},{5,11},{6,8},{7,9},{8,6},{9,7},... | collective-permute-start | bytes 196616 | tf_op jit(solution)/shard_map/ppermute | solution.py:556
